TPU v7x, 32 devices: a whole 2x2x4 slice. The times are simulated.
32 devices in a mesh: grp: 8 (over y, x, core), dp: 4 (over z).
Axes of the slice: x: 2, y: 2, z: 4, core: 2. Of those that a mesh axis runs over, the one named last changes fastest.
Arguments:
- vis_features: bfloat16 [2048, 3200], P(('grp', 'dp')), may hold values from -6 to 6
- vis_gain: float32 [3200], replicated, may hold values from 0.1 to 1.9
- proj_weight: bfloat16 [3200, 8192], P(None, 'dp'), may hold values from -0.109375 to 0.109375
- proj_bias: float32 [8192], P('dp'), may hold values from -3 to 3
- text_embed: bfloat16 [2048, 8192], P('grp', 'dp'), may hold values from -6 to 6
- out_gain: float32 [8192], P('dp'), may hold values from 0.1 to 1.9
- image_counts: int32 [32], P(('grp', 'dp')), may hold values from 1 to 4, as said below
- owner_block: int32 [128], P(('grp', 'dp')), may hold values from 0 to 7, as said below
- offsets: int32 [128], P(('grp', 'dp')), may hold values from 0 to 240, as said below
Outputs:
- hidden: bfloat16 [2048, 8192], P('grp', 'dp')
Inputs may be any that keep to these rules, and one draw needn't show every extreme that they name: The live images of a device are its first image_counts slots; some device holds 4 in every draw. `owner_block`: among the image slots of one index of grp (live or not), at most 2 name the same owner, and in every such block some owner is named by exactly 2. `offsets`: the image slots that name one owner (live or not) cover disjoint runs of 16 positions inside its 256 positions.
All inputs are finite; a program needn't handle non-finite values.
Results may differ from a plain program's by a relative error of at most 0.0043.
Values may be sent and summed in bfloat16 or wider, within the bound.
No kernel may reach another device: no remote copies, remote signals or barrier semaphores. Data moves between devices by JAX's collectives and lax.ppermute only.
A program may use at most 64 MiB of HBM per device.

v0:
```python
import jax
import jax.numpy as jnp
from jax import lax
from jax.sharding import PartitionSpec as P

D = 8192


def on_device(
    vis_features,
    vis_gain,
    proj_weight,
    proj_bias,
    text_embed,
    out_gain,
    image_counts,
    owner_block,
    offsets,
):
    groups = lax.axis_size("grp")
    slots_device = owner_block.shape[0]
    per_image = vis_features.shape[0] // slots_device
    columns = proj_weight.shape[1]
    seq_len = text_embed.shape[0]
    capacity = seq_len // (groups * per_image)
    features_f = vis_features.astype(jnp.float32)
    normed = (
        features_f
        * lax.rsqrt(jnp.mean(features_f * features_f, axis=-1, keepdims=True) + 1e-06)
        * vis_gain
    ).astype(jnp.bfloat16)
    slot_local = jnp.arange(slots_device, dtype=jnp.int32)
    live_offsets = jnp.where(slot_local < image_counts[0], offsets, -1)
    block_owner, block_offsets = (
        lax.all_gather(owner_block, "dp", axis=0, tiled=True),
        lax.all_gather(live_offsets, "dp", axis=0, tiled=True),
    )
    projected = (
        jnp.dot(
            lax.all_gather(normed, "dp", axis=0, tiled=True),
            proj_weight,
            preferred_element_type=jnp.float32,
        )
        + proj_bias
    ).astype(jnp.bfloat16)
    block_slots = block_owner.shape[0]
    earlier = jnp.arange(block_slots)[:, None] > jnp.arange(block_slots)[None, :]
    same_owner = block_owner[:, None] == block_owner[None, :]
    rank_in = jnp.sum(same_owner & earlier, axis=1)
    bucket = block_owner * capacity + rank_in
    selector = jnp.arange(groups * capacity, dtype=jnp.int32)[:, None] == bucket[None, :]
    flat_rows = projected.reshape(block_slots, per_image * columns)
    bucketed = jnp.dot(
        selector.astype(jnp.bfloat16), flat_rows, preferred_element_type=jnp.float32
    ).astype(jnp.bfloat16)
    bucketed = bucketed.reshape(groups, capacity * per_image * columns)
    bucket_offsets = jnp.max(jnp.where(selector, block_offsets[None, :], -1), axis=1).reshape(
        groups, capacity
    )
    arrived, arrived_offsets = (
        lax.all_to_all(bucketed, "grp", split_axis=0, concat_axis=0, tiled=True),
        lax.all_to_all(bucket_offsets, "grp", split_axis=0, concat_axis=0, tiled=True),
    )
    received = arrived.reshape(groups * capacity * per_image, columns)
    starts = arrived_offsets.reshape(groups * capacity)
    target = jnp.where(
        starts[:, None] >= 0,
        starts[:, None] + jnp.arange(per_image, dtype=jnp.int32)[None, :],
        seq_len,
    )
    target = target.reshape(-1).astype(jnp.int32)
    merged = text_embed.at[target].set(received, mode="drop")
    local_squares = jnp.sum(jnp.square(merged.astype(jnp.float32)), axis=1)
    row_total = lax.psum(local_squares, "dp")
    inverse_rms = lax.rsqrt(row_total / D + 1e-05)
    hidden = merged.astype(jnp.float32) * inverse_rms[:, None] * out_gain
    return hidden.astype(jnp.bfloat16)


def solution(mesh):
    return jax.shard_map(
        on_device,
        mesh=mesh,
        in_specs=(
            P(("grp", "dp"), None),
            P(),
            P(None, "dp"),
            P("dp"),
            P("grp", "dp"),
            P("dp"),
            P(("grp", "dp")),
            P(("grp", "dp")),
            P(("grp", "dp")),
        ),
        out_specs=P("grp", "dp"),
        check_vma=False,
    )
```

profile of v0, /device:TPU:0, one launch (start us, length us, event | category | flops | bytes accessed | tf_op | source)
XLA Modules:
  0.0 120.6 jit_solution(5611415358622579225)
XLA Ops:
  6.5 0.0 copy-start.7
  6.5 0.0 copy-start.1
  6.5 0.0 copy-start.2
  6.5 0.0 copy-start.5
  6.5 0.0 copy-start.6
  6.5 0.0 copy-start.4
  6.6 0.0 all-gather.2.cloned.1.call-start
  6.6 0.9 copy-done.1
  7.6 0.2 fusion.4
  7.7 0.0 copy-done.2
  7.8 0.9 fusion.6
  8.7 0.0 all-gather.2.cloned.1.call-update
  9.3 0.0 copy-done.7
  9.4 0.7 dynamic-slice
  10.7 0.0 copy-done.6
  10.7 0.2 dynamic-update-slice
  11.0 0.0 copy-done.4
  11.0 0.1 fusion.9
  11.1 9.9 %all-reduce.2 = (s32[16]{0:T(128)S(1)}, s32[16]{0:T(128)S(1)}) all-reduce(s32[16]{0:T(128)S(1)} %fusion.9, s32[16]{0:T(128)S(1)} %dynamic-update-slice), channel_id=1, replica_groups=mesh['grp'=8,'dp'=4] {'dp'}, use_global_device_ids=true, to_apply=%add.1 | all-reduce | flops 32 | bytes 256
  21.0 0.2 convert_reduce_fusion
  21.2 0.1 select_reduce_fusion
  21.3 0.7 all_to_all.12
  21.9 3.7 %all-to-all-start = ((s32[8,1,2]{2,1,0:T(1,128)}), s32[8,1,2]{2,1,0:T(1,128)S(1)}, u32[]{:S(2)}, u32[]{:S(2)}) async-start(s32[8,1,2]{2,1,0:T(1,128)} %bitcast.2), calls=%async_computation | async-start | bytes 8192 | tf_op jit(solution)/shard_map/all_to_all | solution.py:62
  25.7 24.2 %all-gather.2.cloned.1.call-done = bf16[256,3200]{1,0:T(8,128)(2,1)} async-done(((bf16[64,3200]{1,0:T(8,128)(2,1)}), bf16[256,3200]{1,0:T(8,128)(2,1)}) %all-gather.2.cloned.1.call-update) | async-done | bytes 1638416 | tf_op jit(solution)/shard_map/all_gather | solution.py:40
  49.9 0.0 copy-done.5
  49.9 8.9 %fusion = bf16[256,2048]{1,0:T(8,128)(2,1)S(1)} fusion(bf16[256,3200]{1,0:T(8,128)(2,1)} %all-gather.2.cloned.1.call-done, bf16[3200,2048]{1,0:T(8,128)(2,1)} %param.11, f32[2048]{0:T(1024)S(1)} %copy-done.5), kind=kOutput, calls=%fused_computation.5 | convolution fusion | flops 3356491776 | bytes 15802368 | tf_op jit(solution)/shard_map/dot_general | solution.py:39
  58.8 0.5 reshape.84
  59.3 0.4 convolution_convert_fusion
  59.7 1.6 %all_to_all.16 = bf16[8,1,65536]{2,1,0:T(2,128)(2,1)S(1)} reshape(bf16[16,32768]{1,0:T(8,128)(2,1)S(1)} %convolution_convert_fusion) | data formatting | bytes 2097152 | tf_op jit(solution)/shard_map/all_to_all | solution.py:61
  61.3 0.5 broadcast.69
  61.9 7.0 %reduce.5 = bf16[8,65536]{1,0:T(8,128)(2,1)S(1)} reduce(bf16[8,1,65536]{2,1,0:T(2,128)(2,1)S(1)} %all_to_all.16, bf16[]{:T(256)} %broadcast.69), dimensions={1}, to_apply=%all_to_all.16.reduce_sub_computation | reduce | bytes 2097154 | tf_op jit(solution)/shard_map/all_to_all | solution.py:61
  68.9 1.9 %reshape.114 = bf16[8,2,32768]{2,1,0:T(2,128)(2,1)} reshape(bf16[8,65536]{1,0:T(8,128)(2,1)S(1)} %reduce.5) | data formatting | bytes 2097152
  70.8 0.0 all-to-all-done
  70.8 3.7 %all-to-all-start.1 = ((bf16[8,2,32768]{2,1,0:T(2,128)(2,1)}), bf16[8,2,32768]{2,1,0:T(2,128)(2,1)S(1)}, u32[]{:S(2)}, u32[]{:S(2)}) async-start(bf16[8,2,32768]{2,1,0:T(2,128)(2,1)} %reshape.114), calls=%async_computation.1 | async-start | bytes 2097152 | tf_op jit(solution)/shard_map/all_to_all | solution.py:61
  74.5 0.6 broadcast.68
  75.1 0.7 reduce.4
  75.8 0.1 broadcast_in_dim_reshape.4
  75.9 0.1 add_select_fusion
  76.0 0.1 select_n.36
  76.1 13.8 %all-to-all-done.1 = bf16[8,2,32768]{2,1,0:T(2,128)(2,1)S(1)} async-done(((bf16[8,2,32768]{2,1,0:T(2,128)(2,1)}), bf16[8,2,32768]{2,1,0:T(2,128)(2,1)S(1)}, u32[]{:S(2)}, u32[]{:S(2)}) %all-to-all-start.1) | async-done | bytes 1048608 | tf_op jit(solution)/shard_map/all_to_all | solution.py:61
  89.8 1.0 reshape.115
  90.9 0.0 copy-start
  90.9 7.4 %reduce.1 = bf16[8,65536]{1,0:T(8,128)(2,1)} reduce(bf16[8,1,65536]{2,1,0:T(2,128)(2,1)S(1)} %reshape.115, bf16[]{:T(256)} %constant.41), dimensions={1}, to_apply=%all_to_all.15.reduce_sub_computation | reduce | bytes 2097154 | tf_op jit(solution)/shard_map/all_to_all | solution.py:61
  98.2 1.7 %reshape.90 = bf16[256,2048]{1,0:T(8,128)(2,1)S(1)} reshape(bf16[8,65536]{1,0:T(8,128)(2,1)} %reduce.1) | data formatting | bytes 2097152 | tf_op jit(solution)/shard_map/reshape | solution.py:64
  99.9 0.0 copy-done
  100.0 0.0 copy-start.3
  100.0 2.6 %scatter_fusion = bf16[256,2048]{1,0:T(8,128)(2,1)S(1)} fusion(bf16[256,2048]{1,0:T(8,128)(2,1)S(1)} %copy-done, s32[256]{0:T(256)S(1)} %bitcast.9, bf16[256,2048]{1,0:T(8,128)(2,1)S(1)} %reshape.90), kind=kCustom, calls=%fused_computation | custom fusion | bytes 3146752 | tf_op jit(solution)/shard_map/scatter | solution.py:72
  102.6 0.3 fusion.1
  102.9 9.6 %psum.7 = f32[256]{0:T(256)S(1)} all-reduce(f32[256]{0:T(256)S(1)} %fusion.1), channel_id=1, replica_groups=mesh['grp'=8,'dp'=4] {'dp'}, use_global_device_ids=true, to_apply=%region_5.6 | all-reduce | flops 256 | bytes 2048 | tf_op jit(solution)/shard_map/psum | solution.py:74
  112.5 0.0 copy-done.3
  112.5 1.3 %fusion.3 = bf16[256,2048]{1,0:T(8,128)(2,1)} fusion(bf16[256,2048]{1,0:T(8,128)(2,1)S(1)} %scatter_fusion, f32[2048]{0:T(1024)S(1)} %copy-done.3, f32[256]{0:T(256)S(1)} %add_rsqrt_fusion), kind=kLoop, calls=%fused_computation.8 | loop fusion | flops 2097152 | bytes 2106368 | tf_op jit(solution)/shard_map/convert_element_type | solution.py:77
  (7 shorter events, 0.0 us)
Async XLA Ops:
  6.5 2.8 %copy-start.7 = (u32[32]{0:T(128)S(1)}, u32[32]{0:T(128)}, u32[]{:S(2)}) copy-start(u32[32]{0:T(128)} %constant.30) | copy-start | bytes 388
  6.5 1.0 copy-start.1
  6.5 1.2 %copy-start.2 = (f32[3200]{0:T(1024)S(1)}, f32[3200]{0:T(1024)}, u32[]{:S(2)}) copy-start(f32[3200]{0:T(1024)} %param.10) | copy-start | bytes 38404
  6.5 43.3 %copy-start.5 = (f32[2048]{0:T(1024)S(1)}, f32[2048]{0:T(1024)}, u32[]{:S(2)}) copy-start(f32[2048]{0:T(1024)} %param.12) | copy-start | bytes 24580
  6.5 4.2 %copy-start.6 = (s32[4]{0:T(128)S(1)}, s32[4]{0:T(128)}, u32[]{:S(2)}) copy-start(s32[4]{0:T(128)} %param.16) | copy-start | bytes 52
  6.5 4.4 %copy-start.4 = (s32[4]{0:T(128)S(1)}, s32[4]{0:T(128)}, u32[]{:S(2)}) copy-start(s32[4]{0:T(128)} %param.17) | copy-start | bytes 52
  6.6 43.3 %all-gather.2.cloned.1.call-start = ((), (), s32[]{:S(2)}) async-start(), calls=%async_computation.2 | async-start | bytes 2048000 | tf_op jit(solution)/shard_map/all_gather | solution.py:40
  21.9 48.8 %all-to-all-start = ((s32[8,1,2]{2,1,0:T(1,128)}), s32[8,1,2]{2,1,0:T(1,128)S(1)}, u32[]{:S(2)}, u32[]{:S(2)}) async-start(s32[8,1,2]{2,1,0:T(1,128)} %bitcast.2), calls=%async_computation | async-start | bytes 8192 | tf_op jit(solution)/shard_map/all_to_all | solution.py:62
  70.8 19.1 %all-to-all-start.1 = ((bf16[8,2,32768]{2,1,0:T(2,128)(2,1)}), bf16[8,2,32768]{2,1,0:T(2,128)(2,1)S(1)}, u32[]{:S(2)}, u32[]{:S(2)}) async-start(bf16[8,2,32768]{2,1,0:T(2,128)(2,1)} %reshape.114), calls=%async_computation.1 | async-start | bytes 2097152 | tf_op jit(solution)/shard_map/all_to_all | solution.py:61
  90.9 9.1 %copy-start = (bf16[256,2048]{1,0:T(8,128)(2,1)S(1)}, bf16[256,2048]{1,0:T(8,128)(2,1)}, u32[]{:S(2)}) copy-start(bf16[256,2048]{1,0:T(8,128)(2,1)} %param.13) | copy-start | bytes 3145732
  100.0 12.5 %copy-start.3 = (f32[2048]{0:T(1024)S(1)}, f32[2048]{0:T(1024)}, u32[]{:S(2)}) copy-start(f32[2048]{0:T(1024)} %param.14) | copy-start | bytes 24580
Sparse Core Ops, SparseCore 0:
  9.0 40.8 all-gather.1
where the time goes:
time: 121 us
  waiting for transfers between devices  38 us (31%)
  blocking collectives  19.5 us (16%)
  other arithmetic  18.3 us (15%)
  between operations  14.9 us (12%)
  local copies, waits for them, and re-layouts  13.2 us (11%)
  matrix products  9.33 us (8%)
  starting transfers between devices  7.5 us (6%)
    all_gather x1, waiting for transfers between devices, on_device(): lax.all_gather(normed, 'dp', axis=0, tiled=True)  24.2 us
    all_to_all x2, other arithmetic, on_device(): lax.all_to_all(bucketed, 'grp', split_axis=0, concat_axis=0, tiled=True)  14.4 us
    all_to_all x1, waiting for transfers between devices, on_device(): lax.all_to_all(bucketed, 'grp', split_axis=0, concat_axis=0, tiled=True)  13.8 us
    unnamed x1, blocking collectives  9.89 us
    psum x1, blocking collectives, on_device(): row_total = lax.psum(local_squares, 'dp')  9.61 us
    dot_general x1, matrix products, on_device(): jnp.dot(lax.all_gather(normed, 'dp', axis=0, tiled=True), proj_weight, pr...  8.91 us
    unnamed x22, local copies, waits for them, and re-layouts  4.78 us
    all_to_all x1, starting transfers between devices, on_device(): lax.all_to_all(bucketed, 'grp', split_axis=0, concat_axis=0, tiled=True)  3.74 us
  transfers between devices with their start and end apart: 3, of which 2 were waited for; matrix products, arithmetic and copies ran while one was open for 18% of the time, Pallas kernels for 0%

commit v1 on v0

--- a/solution.py
+++ b/solution.py
@@ -1,23 +1,306 @@
+import functools
+
 import jax
 import jax.numpy as jnp
 from jax import lax
+from jax.experimental import pallas as pl
+from jax.experimental.pallas import tpu as pltpu
 from jax.sharding import PartitionSpec as P
 
-D = 8192
-
-
-def on_device(
-    vis_features,
-    vis_gain,
-    proj_weight,
-    proj_bias,
-    text_embed,
-    out_gain,
-    image_counts,
-    owner_block,
-    offsets,
+EPS_VIS = 1e-06
+EPS_OUT = 1e-05
+TILE = (8, 128)
+F32 = jnp.float32
+BF16 = jnp.bfloat16
+VMEM = pl.BlockSpec(memory_space=pltpu.VMEM)
+SMEM = pl.BlockSpec(memory_space=pltpu.SMEM)
+ANY = pl.BlockSpec(memory_space=pl.ANY)
+
+
+def lanes():
+    return lax.broadcasted_iota(jnp.int32, TILE, 1)
+
+
+def norm_kernel(slots, half, vis, gain, owners, offsets, counts, rows_a, rows_b, info):
+    x = vis[...].astype(F32)
+    y = x * lax.rsqrt(jnp.mean(x * x, axis=-1, keepdims=True) + EPS_VIS) * gain[...]
+    y = y.reshape(slots, 2, half, y.shape[-1])
+    rows_a[...] = y[:, 0].reshape(rows_a.shape).astype(BF16)
+    rows_b[...] = y[:, 1].reshape(rows_b.shape).astype(BF16)
+    lane = lanes()
+    tile = jnp.zeros(TILE, jnp.int32)
+    for i in range(slots):
+        tile = jnp.where(lane == i, owners[i], tile)
+        tile = jnp.where(lane == slots + i, jnp.where(i < counts[0], offsets[i], -1), tile)
+    for q in range(info.shape[0] // TILE[0]):
+        info[q * TILE[0] : (q + 1) * TILE[0], :] = tile
+
+
+def text_kernel(groups, dp, slots, cap, info, text, squares, seat, start):
+    me, row = lax.axis_index("grp"), lax.axis_index("dp")
+    lane = lanes()
+    tile = jnp.zeros(TILE, F32)
+    for c in range(text.shape[0] // 16):
+        x = text[c * 16 : (c + 1) * 16, :].astype(F32)
+        sums = jnp.sum(x * x, axis=1, keepdims=True)
+        tile = jnp.where(lane == 2 * c, sums[:8], tile)
+        tile = jnp.where(lane == 2 * c + 1, sums[8:], tile)
+    squares[...] = tile
+    for o in range(groups):
+        start[groups * cap + o] = 0
+
+    def one(image, carry):
+        device = image // slots
+        owner = info[me * dp + device, image % slots]
+        rank = start[groups * cap + owner]
+        start[groups * cap + owner] = rank + 1
+        seat[(device ^ row) * slots + image % slots] = (owner ^ me) * cap + rank
+        return carry
+
+    lax.fori_loop(0, dp * slots, one, 0)
+
+    def other(source, carry):
+        def step(image, rank):
+            device = source * dp + image // slots
+            mine = info[device, image % slots] == me
+            place = (source ^ me) * cap + rank
+
+            @pl.when(mine)
+            def _():
+                start[place] = info[device, slots + image % slots]
+
+            return rank + mine.astype(jnp.int32)
+
+        lax.fori_loop(0, dp * slots, step, jnp.int32(0))
+        return carry
+
+    lax.fori_loop(0, groups, other, 0)
+
+
+def project_kernel(
+    groups, cap, half, second, steps, seat, own, a1, b1, a2, b2, a3, weight, bias, *rest
+):
+    if second:
+        before, text_squares, *rest = rest
+    outs, (squares, x, placed, partial, sem) = rest[:groups], rest[groups:]
+    n = pl.program_id(0)
+    row = lax.axis_index("dp")
+    rows = own.shape[0]
+    images = placed.shape[0] // half
+
+    @pl.when(n == 0)
+    def _():
+        middle = jnp.logical_or(row == 1, row == 2)
+        copies = [pltpu.make_async_copy(own, x.at[0:rows], sem), pltpu.make_async_copy(a1, x.at[rows : 2 * rows], sem)]
+        for copy in copies:
+            copy.start()
+
+        @pl.when(middle)
+        def _():
+            pltpu.make_async_copy(b2, x.at[2 * rows : 3 * rows], sem).start()
+            pltpu.make_async_copy(b1, x.at[3 * rows : 4 * rows], sem).start()
+
+        @pl.when(jnp.logical_not(middle))
+        def _():
+            pltpu.make_async_copy(a2, x.at[2 * rows : 3 * rows], sem).start()
+            pltpu.make_async_copy(a3, x.at[3 * rows : 4 * rows], sem).start()
+
+        for _ in range(4):
+            copies[0].wait()
+        partial[...] = jnp.zeros_like(partial)
+
+    y = jnp.dot(x[...], weight[...], preferred_element_type=F32) + bias[...]
+    for i in range(images):
+        at = pl.multiple_of(seat[i] * half, half)
+        placed[pl.ds(at, half), :] = y[i * half : (i + 1) * half, :]
+    for k in range(groups):
+        part = slice(k * cap * half, (k + 1) * cap * half)
+        rounded = placed[part, :].astype(BF16)
+        outs[k][...] = rounded
+        wide = rounded.astype(F32)
+        wide = wide * wide
+        total = partial[part, :]
+        for c in range(wide.shape[1] // 128):
+            total = total + wide[:, c * 128 : (c + 1) * 128]
+        partial[part, :] = total
+
+    @pl.when(n == steps - 1)
+    def _():
+        lane = lanes()
+        me = lax.axis_index("grp")
+        for k in range(groups):
+            owner = me ^ k
+            if second:
+                tile = before[k * 8 : (k + 1) * 8, :]
+            else:
+                tile = jnp.zeros(TILE, F32)
+            for r in range(cap):
+                at = (k * cap + r) * half
+                sums = jnp.sum(partial[at : at + half, :], axis=1, keepdims=True)
+                tile = jnp.where(lane == (cap if second else 0) + r, sums, tile)
+            if not second:
+                squares[k * 8 : (k + 1) * 8, :] = tile
+            else:
+                if k == 0:
+                    text = pltpu.roll(text_squares[...], 2 * cap, 1)
+                    tile = jnp.where(lane < 2 * cap, tile, text)
+                copies = squares.shape[0] // (8 * groups)
+                for q in range(copies):
+                    at = pl.multiple_of((owner * copies + q) * 8, 8)
+                    squares[pl.ds(at, 8), :] = tile
+
+
+def place_kernel(groups, dp, cap, half, width, start, squares, gain, text, *rest):
+    first, second, (out, scale) = rest[:groups], rest[groups : 2 * groups], rest[2 * groups :]
+
+    @pl.when(pl.program_id(0) == 0)
+    def _():
+        me = lax.axis_index("grp")
+        for k in range(groups):
+            base = (me ^ k) * (dp * 8)
+            total = squares[pl.ds(pl.multiple_of(base, 8), 8), :]
+            for d in range(1, dp):
+                total = total + squares[pl.ds(pl.multiple_of(base + d * 8, 8), 8), :]
+            scale[k * 8 : (k + 1) * 8, :] = lax.rsqrt(total / width + EPS_OUT)
+
+    g = gain[...]
+    base = scale[0:8, :]
+    for c in range(text.shape[0] // 16):
+        at = 2 * cap + 2 * c
+        inverse = jnp.concatenate([base[:, at : at + 1], base[:, at + 1 : at + 2]], axis=0)
+        x = text[c * 16 : (c + 1) * 16, :].astype(F32)
+        out[c * 16 : (c + 1) * 16, :] = (x * inverse * g).astype(BF16)
+    for k in range(groups):
+        tile = scale[k * 8 : (k + 1) * 8, :]
+        for r in range(cap):
+            at = start[k * cap + r]
+
+            @pl.when(at >= 0)
+            def _():
+                part = slice(r * half, (r + 1) * half)
+                a = first[k][...].astype(F32)[part] * tile[:, r : r + 1]
+                b = second[k][...].astype(F32)[part] * tile[:, cap + r : cap + r + 1]
+                rows = (jnp.concatenate([a, b], axis=0) * g).astype(BF16)
+                out[pl.ds(pl.multiple_of(at, 2 * half), 2 * half), :] = rows
+
+
+def project(groups, cap, half, seat, pieces, weight, bias, before=None, text_squares=None, devices=1):
+    depth, columns = weight.shape
+    block = 256
+    steps = columns // block
+    second = before is not None
+    rows = pieces[0].shape[0]
+    whole = lambda a: pl.BlockSpec(a.shape, lambda n: (0,) * a.ndim)
+    extra = (before, text_squares) if second else ()
+    shape = (devices * 8, 128) if second else (groups * 8, 128)
+    return pl.pallas_call(
+        functools.partial(project_kernel, groups, cap, half, second, steps),
+        grid=(steps,),
+        in_specs=[SMEM]
+        + [ANY] * len(pieces)
+        + [pl.BlockSpec((depth, block), lambda n: (0, n)), pl.BlockSpec((1, block), lambda n: (0, n))]
+        + [whole(a) for a in extra],
+        out_specs=[pl.BlockSpec((cap * half, block), lambda n: (0, n))] * groups + [pl.BlockSpec(shape, lambda n: (0, 0))],
+        out_shape=[jax.ShapeDtypeStruct((cap * half, columns), BF16)] * groups + [jax.ShapeDtypeStruct(shape, F32)],
+        scratch_shapes=[
+            pltpu.VMEM((4 * rows, depth), BF16),
+            pltpu.VMEM((4 * rows, block), F32),
+            pltpu.VMEM((4 * rows, 128), F32),
+            pltpu.SemaphoreType.DMA,
+        ],
+        compiler_params=pltpu.CompilerParams(vmem_limit_bytes=32 << 20),
+        cost_estimate=pl.CostEstimate(
+            flops=8 * rows * depth * columns, bytes_accessed=2 * depth * columns, transcendentals=0
+        ),
+        name="project",
+    )(seat, *pieces, weight, bias, *extra)
+
+
+def exchange(x):
+    pairs = [(0, 1), (1, 0), (2, 3), (3, 2)]
+    return lax.ppermute(x, "dp", pairs)
+
+
+def inner(x):
+    return lax.ppermute(x, "dp", [(1, 2), (2, 1), (0, 0), (3, 3)])
+
+
+def route(groups, parts):
+    sent = [
+        lax.ppermute(parts[k], "grp", [(i, i ^ k) for i in range(groups)]) for k in range(1, groups)
+    ]
+    return [parts[0]] + sent
+
+
+def fast(vis, vis_gain, weight, bias, text, out_gain, counts, owners, offsets):
+    groups, dp = lax.axis_size("grp"), lax.axis_size("dp")
+    devices = groups * dp
+    slots = owners.shape[0]
+    per_image = vis.shape[0] // slots
+    half = per_image // 2
+    seq_len, columns = text.shape
+    cap = seq_len // (groups * per_image)
+    rows = slots * half
+    rows_a, rows_b, info = pl.pallas_call(
+        functools.partial(norm_kernel, slots, half),
+        in_specs=[VMEM, VMEM, SMEM, SMEM, SMEM],
+        out_specs=[VMEM] * 3,
+        out_shape=[jax.ShapeDtypeStruct((rows, vis.shape[1]), BF16)] * 2
+        + [jax.ShapeDtypeStruct((devices * 8, 128), jnp.int32)],
+        name="norm",
+    )(vis, vis_gain[None, :], owners, offsets, counts)
+
+    a1, a1_b = exchange(rows_a), exchange(rows_b)
+    b1, b1_b = inner(rows_a), inner(rows_b)
+    b2, b2_b = inner(a1), inner(a1_b)
+    a2, a2_b = exchange(b1), exchange(b1_b)
+    a3, a3_b = exchange(b2), exchange(b2_b)
+    known = lax.all_to_all(info, ("grp", "dp"), 0, 0, tiled=True)
+    known = known.reshape(devices, 8, 128)[:, 0, : 2 * slots]
+    text_squares, seat, start = pl.pallas_call(
+        functools.partial(text_kernel, groups, dp, slots, cap),
+        in_specs=[SMEM, VMEM],
+        out_specs=[VMEM, SMEM, SMEM],
+        out_shape=[
+            jax.ShapeDtypeStruct(TILE, F32),
+            jax.ShapeDtypeStruct((dp * slots,), jnp.int32),
+            jax.ShapeDtypeStruct((groups * cap + groups,), jnp.int32),
+        ],
+        name="tables",
+    )(known, text)
+    bias = bias[None, :]
+    *parts_a, squares_a = project(groups, cap, half, seat, (rows_a, a1, b1, a2, b2, a3), weight, bias)
+    first = route(groups, parts_a)
+    *parts_b, squares = project(
+        groups, cap, half, seat, (rows_b, a1_b, b1_b, a2_b, b2_b, a3_b), weight, bias, squares_a, text_squares, devices
+    )
+    squares = lax.all_to_all(squares, ("grp", "dp"), 0, 0, tiled=True)
+    second = route(groups, parts_b)
+    block = 1024
+    spec = pl.BlockSpec((cap * half, block), lambda n: (0, n))
+    return pl.pallas_call(
+        functools.partial(place_kernel, groups, dp, cap, half, columns * dp),
+        grid=(columns // block,),
+        in_specs=[
+            SMEM,
+            pl.BlockSpec((devices * 8, 128), lambda n: (0, 0)),
+            pl.BlockSpec((1, block), lambda n: (0, n)),
+            pl.BlockSpec((seq_len, block), lambda n: (0, n)),
+        ]
+        + [spec] * (2 * groups),
+        out_specs=pl.BlockSpec((seq_len, block), lambda n: (0, n)),
+        out_shape=jax.ShapeDtypeStruct(text.shape, BF16),
+        scratch_shapes=[pltpu.VMEM((groups * 8, 128), F32)],
+        compiler_params=pltpu.CompilerParams(vmem_limit_bytes=24 << 20),
+        name="place",
+    )(start, squares, out_gain[None, :], text, *first, *second)
+
+
+def general(
+    vis_features, vis_gain, proj_weight, proj_bias, text_embed, out_gain, image_counts, owner_block, offsets
 ):
     groups = lax.axis_size("grp")
+    width = proj_weight.shape[1] * lax.axis_size("dp")
     slots_device = owner_block.shape[0]
     per_image = vis_features.shape[0] // slots_device
     columns = proj_weight.shape[1]
@@ -26,7 +309,7 @@
     features_f = vis_features.astype(jnp.float32)
     normed = (
         features_f
-        * lax.rsqrt(jnp.mean(features_f * features_f, axis=-1, keepdims=True) + 1e-06)
+        * lax.rsqrt(jnp.mean(features_f * features_f, axis=-1, keepdims=True) + EPS_VIS)
         * vis_gain
     ).astype(jnp.bfloat16)
     slot_local = jnp.arange(slots_device, dtype=jnp.int32)
@@ -72,9 +355,20 @@
     merged = text_embed.at[target].set(received, mode="drop")
     local_squares = jnp.sum(jnp.square(merged.astype(jnp.float32)), axis=1)
     row_total = lax.psum(local_squares, "dp")
-    inverse_rms = lax.rsqrt(row_total / D + 1e-05)
+    inverse_rms = lax.rsqrt(row_total / width + EPS_OUT)
     hidden = merged.astype(jnp.float32) * inverse_rms[:, None] * out_gain
     return hidden.astype(jnp.bfloat16)
+
+
+def on_device(vis, vis_gain, weight, bias, text, out_gain, counts, owners, offsets):
+    groups, dp = lax.axis_size("grp"), lax.axis_size("dp")
+    per_image = vis.shape[0] // owners.shape[0]
+    cap = text.shape[0] // (groups * per_image)
+    full = dp * owners.shape[0] == groups * cap and groups * cap * per_image == text.shape[0]
+    fits = dp == 4 and groups & (groups - 1) == 0 and per_image == 16 and cap == 2 and text.shape[0] <= 512
+    fits = fits and owners.shape[0] % 4 == 0 and weight.shape[1] % 1024 == 0
+    form = fast if full and fits else general
+    return form(vis, vis_gain, weight, bias, text, out_gain, counts, owners, offsets)
 
 
 def solution(mesh):

time: 121 us -> 96.6 us (0.80)
  starting transfers between devices: 7.5 us -> 48.1 us
  waiting for transfers between devices: 38 us -> 9.63 us
  Pallas kernels: 0 us -> 25 us
  blocking collectives: 19.5 us -> 0 us
  other arithmetic: 18.3 us -> 0 us
  between operations: 14.9 us -> 0.86 us
  matrix products: 9.33 us -> 0 us
    ppermute x0 -> x24, starting transfers between devices: none -> 36.9 us  [the longest x6 16.7 us: exchange(): return lax.ppermute(x, 'dp', pairs)]
    pallas_call x0 -> x5, Pallas kernels: none -> 25 us  [the longest x2 15.5 us: project(): pl.pallas_call(functools.partial(project_kernel, groups, cap, half, secon...]
    all_gather x1 -> x0, waiting for transfers between devices: 24.2 us -> none  [on_device(): lax.all_gather(normed, 'dp', axis=0, tiled=True)]
    all_to_all x3 -> x0, other arithmetic: 15.1 us -> none  [the longest x2 14.4 us: on_device(): lax.all_to_all(bucketed, 'grp', split_axis=0, concat_axis=0, tiled=True)]
    all_to_all x2, waiting for transfers between devices: 13.8 us -> 0.01 us  [the longest x1 0.01 us: fast(): known = lax.all_to_all(info, ('grp', 'dp'), 0, 0, tiled=True)]
    unnamed x1 -> x0, blocking collectives: 9.89 us -> none
    ppermute x0 -> x24, waiting for transfers between devices: none -> 9.63 us  [the longest x14 5.14 us: route(): lax.ppermute(parts[k], 'grp', [(i, i ^ k) for i in range(groups)])]
    psum x1 -> x0, blocking collectives: 9.61 us -> none  [on_device(): row_total = lax.psum(local_squares, 'dp')]
  transfers between devices with their start and end apart: 3 -> 26, of which waited for: 2 -> 5; matrix products, arithmetic and copies ran while one was open for 18% -> 1% of each run, Pallas kernels for 0% -> 13%
where the time goes in v1:
time: 96.6 us; the launch traced here: 95.6 us
  starting transfers between devices  48.1 us (50%)
  Pallas kernels  25 us (26%)
  local copies, waits for them, and re-layouts  12.1 us (13%)
  waiting for transfers between devices  9.63 us (10%)
    ppermute x6, starting transfers between devices, exchange(): return lax.ppermute(x, 'dp', pairs)  16.7 us
    ppermute x14, starting transfers between devices, route(): lax.ppermute(parts[k], 'grp', [(i, i ^ k) for i in range(groups)])  15.7 us
    pallas_call x2, Pallas kernels, project(): pl.pallas_call(functools.partial(project_kernel, groups, cap, half, secon...  15.5 us
    unnamed x40, local copies, waits for them, and re-layouts  10.1 us
    all_to_all x1, starting transfers between devices, fast(): known = lax.all_to_all(info, ('grp', 'dp'), 0, 0, tiled=True)  7.13 us
    ppermute x14, waiting for transfers between devices, route(): lax.ppermute(parts[k], 'grp', [(i, i ^ k) for i in range(groups)])  5.14 us
    pallas_call x1, Pallas kernels, fast(): pl.pallas_call(functools.partial(text_kernel, groups, dp, slots, cap), in...  4.67 us
    ppermute x4, starting transfers between devices, inner(): return lax.ppermute(x, 'dp', [(1, 2), (2, 1), (0, 0), (3, 3)])  4.49 us
  transfers between devices with their start and end apart: 26, of which 5 were waited for; matrix products, arithmetic and copies ran while one was open for 1% of the time, Pallas kernels for 13%

profile of v1, /device:TPU:0, one launch (start us, length us, event | category | flops | bytes accessed | tf_op | source)
XLA Modules:
  0.0 95.6 jit_solution(4923944154708672265)
XLA Ops:
  0.0 1.3 %broadcast_in_dim.9.gain = f32[1,3200]{1,0:T(1,128)} reshape(f32[3200]{0:T(1024)} %param.10) | data formatting | bytes 25600 | tf_op jit(solution)/shard_map/broadcast_in_dim | solution.py:251
  2.0 2.0 %norm.1 = (bf16[32,3200]{1,0:T(8,128)(2,1)}, bf16[32,3200]{1,0:T(8,128)(2,1)}, s32[256,128]{1,0:T(8,128)}) custom-call(bf16[64,3200]{1,0:T(8,128)(2,1)} %vis.1, f32[1,3200]{1,0:T(1,128)} %broadcast_in_dim.9.gain, s32[4]{0:T(128)} %owners.1, s32[4]{0:T(128)} %offsets.1, s32[1]{0:T(128)S(6)} %copy.13.counts), custom_call_target="tpu_custom_call" | custom-call | tf_op jit(solution)/shard_map/norm/pallas_call | solution.py:244
  3.9 3.0 %collective-permute-start.5 = (bf16[32,3200]{1,0:T(8,128)(2,1)}, bf16[32,3200]{1,0:T(8,128)(2,1)S(1)}, u32[]{:S(2)}, u32[]{:S(2)}) collective-permute-start(bf16[32,3200]{1,0:T(8,128)(2,1)} %get-tuple-element.33.own), channel_id=1, source_target_pairs={{0,1},{1,0},{2,3},{3,2},{4,5},{5,4},{6,7},{7,6},{8,9},{9,8},{10,11... | collective-permute-start | bytes 614408 | tf_op jit(solution)/shard_map/ppermute | solution.py:221
  7.0 0.1 collective-permute-start
  7.0 1.6 %collective-permute-start.6 = (bf16[32,3200]{1,0:T(8,128)(2,1)}, bf16[32,3200]{1,0:T(8,128)(2,1)S(1)}, u32[]{:S(2)}, u32[]{:S(2)}) collective-permute-start(bf16[32,3200]{1,0:T(8,128)(2,1)} %get-tuple-element.33.own), channel_id=1, source_target_pairs={{1,2},{2,1},{0,0},{3,3},{5,6},{6,5},{4,4},{7,7},{9,10},{10,9},{8,8... | collective-permute-start | bytes 614408 | tf_op jit(solution)/shard_map/ppermute | solution.py:225
  8.6 4.5 %collective-permute-done.5.a1 = bf16[32,3200]{1,0:T(8,128)(2,1)S(1)} collective-permute-done((bf16[32,3200]{1,0:T(8,128)(2,1)}, bf16[32,3200]{1,0:T(8,128)(2,1)S(1)}, u32[]{:S(2)}, u32[]{:S(2)}) %collective-permute-start.5) | collective-permute-done | bytes 204832 | tf_op jit(solution)/shard_map/ppermute | solution.py:221
  13.1 0.7 collective-permute-start.8
  13.7 7.1 %all-to-all-start = ((s32[32,8,128]{2,1,0:T(8,128)}), s32[32,8,128]{2,1,0:T(8,128)S(1)}, u32[]{:S(2)}, u32[]{:S(2)}) async-start(s32[32,8,128]{2,1,0:T(8,128)} %bitcast.12), calls=%async_computation | async-start | bytes 262144 | tf_op jit(solution)/shard_map/all_to_all | solution.py:258
  20.9 1.6 %collective-permute-start.1 = (bf16[32,3200]{1,0:T(8,128)(2,1)}, bf16[32,3200]{1,0:T(8,128)(2,1)S(1)}, u32[]{:S(2)}, u32[]{:S(2)}) collective-permute-start(bf16[32,3200]{1,0:T(8,128)(2,1)} %get-tuple-element.32.own), channel_id=1, source_target_pairs={{1,2},{2,1},{0,0},{3,3},{5,6},{6,5},{4,4},{7,7},{9,10},{10,9},{8,8... | collective-permute-start | bytes 614408 | tf_op jit(solution)/shard_map/ppermute | solution.py:225
  22.5 0.0 collective-permute-done.a1
  22.5 0.7 collective-permute-start.3
  23.1 0.0 collective-permute-done.6.b1
  23.1 5.4 %collective-permute-start.7 = (bf16[32,3200]{1,0:T(8,128)(2,1)S(1)}, bf16[32,3200]{1,0:T(8,128)(2,1)S(1)}, u32[]{:S(2)}, u32[]{:S(2)}) collective-permute-start(bf16[32,3200]{1,0:T(8,128)(2,1)S(1)} %collective-permute-done.6.b1), channel_id=1, source_target_pairs={{0,1},{1,0},{2,3},{3,2},{4,5},{5,4},{6,7},{7,6},{8,9},{9,8},{10,11... | collective-permute-start | bytes 614408 | tf_op jit(solution)/shard_map/ppermute | solution.py:221
  28.6 0.0 collective-permute-done.8.b2
  28.6 0.1 collective-permute-start.9
  28.7 0.0 collective-permute-done.1.b1
  28.7 4.0 %collective-permute-start.2 = (bf16[32,3200]{1,0:T(8,128)(2,1)S(1)}, bf16[32,3200]{1,0:T(8,128)(2,1)S(1)}, u32[]{:S(2)}, u32[]{:S(2)}) collective-permute-start(bf16[32,3200]{1,0:T(8,128)(2,1)S(1)} %collective-permute-done.1.b1), channel_id=1, source_target_pairs={{0,1},{1,0},{2,3},{3,2},{4,5},{5,4},{6,7},{7,6},{8,9},{9,8},{10,11... | collective-permute-start | bytes 614408 | tf_op jit(solution)/shard_map/ppermute | solution.py:221
  32.7 0.0 collective-permute-done.3.b2
  32.7 4.1 %collective-permute-start.4 = (bf16[32,3200]{1,0:T(8,128)(2,1)S(1)}, bf16[32,3200]{1,0:T(8,128)(2,1)S(1)}, u32[]{:S(2)}, u32[]{:S(2)}) collective-permute-start(bf16[32,3200]{1,0:T(8,128)(2,1)S(1)} %collective-permute-done.3.b2), channel_id=1, source_target_pairs={{0,1},{1,0},{2,3},{3,2},{4,5},{5,4},{6,7},{7,6},{8,9},{9,8},{10,11... | collective-permute-start | bytes 614408 | tf_op jit(solution)/shard_map/ppermute | solution.py:221
  36.8 0.0 all-to-all-done
  36.8 0.6 slice.4
  37.4 4.7 %tables.1 = (f32[8,128]{1,0:T(8,128)}, s32[16]{0:T(128)}, s32[24]{0:T(128)}) custom-call(s32[32,8]{1,0:T(8,128)} %bitcast.13, bf16[256,2048]{1,0:T(8,128)(2,1)} %text.3), custom_call_target="tpu_custom_call" | custom-call | tf_op jit(solution)/shard_map/tables/pallas_call | solution.py:260
  42.1 0.0 collective-permute-done.7.a2
  42.1 0.0 collective-permute-done.9.a3
  42.1 0.0 copy-start
  42.1 4.7 %copy-done = bf16[3200,2048]{1,0:T(8,128)(2,1)S(1)} copy-done((bf16[3200,2048]{1,0:T(8,128)(2,1)S(1)}, bf16[3200,2048]{1,0:T(8,128)(2,1)}, u32[]{:S(2)}) %copy-start) | copy-done | bytes 13107224
  46.8 0.9 copy-done.4
  47.8 0.7 copy-done.5
  48.5 0.6 copy-done.8
  49.1 7.4 %project.2 = (bf16[16,2048]{1,0:T(8,128)(2,1)S(1)}, bf16[16,2048]{1,0:T(8,128)(2,1)S(1)}, bf16[16,2048]{1,0:T(8,128)(2,1)S(1)}, bf16[16,2048]{1,0:T(8,128)(2,1)S...) custom-call(s32[16]{0:T(128)S(1)} %copy-done.8, ...), custom_call_target="tpu_custom_call" | custom-call | flops 1677721600 | bytes 13107200 | tf_op jit(solution)/shard_map/project/pallas_call | solution.py:196
  56.5 0.6 copy-done.10
  57.1 0.6 copy-done.12
  57.8 0.6 copy-done.14
  58.4 0.6 copy-done.16
  59.0 0.6 copy-done.18
  59.6 0.0 collective-permute-done.2.a2
  59.7 0.0 collective-permute-done.4.a3
  59.7 8.1 %project.3 = (bf16[16,2048]{1,0:T(8,128)(2,1)S(1)}, bf16[16,2048]{1,0:T(8,128)(2,1)S(1)}, bf16[16,2048]{1,0:T(8,128)(2,1)S(1)}, bf16[16,2048]{1,0:T(8,128)(2,1)S...) custom-call(s32[16]{0:T(128)S(1)} %copy-done.8, ...), custom_call_target="tpu_custom_call" | custom-call | flops 1677721600 | bytes 13107200 | tf_op jit(solution)/shard_map/project/pallas_call | solution.py:196
  67.8 4.0 %all-to-all-start.1 = ((f32[32,8,128]{2,1,0:T(8,128)}), f32[32,8,128]{2,1,0:T(8,128)S(1)}, u32[]{:S(2)}, u32[]{:S(2)}) async-start(f32[32,8,128]{2,1,0:T(8,128)} %bitcast.3), calls=%async_computation.1 | async-start | bytes 262144 | tf_op jit(solution)/shard_map/all_to_all | solution.py:277
  71.8 0.3 collective-permute-start.17
  72.1 1.7 %collective-permute-start.18 = (bf16[16,2048]{1,0:T(8,128)(2,1)S(1)}, bf16[16,2048]{1,0:T(8,128)(2,1)S(1)}, u32[]{:S(2)}, u32[]{:S(2)}) collective-permute-start(bf16[16,2048]{1,0:T(8,128)(2,1)S(1)} %get-tuple-element.47), channel_id=1, source_target_pairs={{0,8},{4,12},{8,0},{12,4},{16,24},{20,28},{24,16},{28,20},{1,9},{5... | collective-permute-start | bytes 196616 | tf_op jit(solution)/shard_map/ppermute | solution.py:230
  73.8 0.0 collective-permute-start.19
  73.8 1.7 %collective-permute-start.20 = (bf16[16,2048]{1,0:T(8,128)(2,1)S(1)}, bf16[16,2048]{1,0:T(8,128)(2,1)S(1)}, u32[]{:S(2)}, u32[]{:S(2)}) collective-permute-start(bf16[16,2048]{1,0:T(8,128)(2,1)S(1)} %get-tuple-element.49), channel_id=1, source_target_pairs={{0,16},{4,20},{8,24},{12,28},{16,0},{20,4},{24,8},{28,12},{1,17},{... | collective-permute-start | bytes 196616 | tf_op jit(solution)/shard_map/ppermute | solution.py:230
  75.5 0.1 collective-permute-start.21
  75.6 0.0 collective-permute-done.17.rest_9_
  75.6 2.6 %collective-permute-start.22 = (bf16[16,2048]{1,0:T(8,128)(2,1)S(1)}, bf16[16,2048]{1,0:T(8,128)(2,1)S(1)}, u32[]{:S(2)}, u32[]{:S(2)}) collective-permute-start(bf16[16,2048]{1,0:T(8,128)(2,1)S(1)} %get-tuple-element.51), channel_id=1, source_target_pairs={{0,24},{4,28},{8,16},{12,20},{16,8},{20,12},{24,0},{28,4},{1,25},{... | collective-permute-start | bytes 196616 | tf_op jit(solution)/shard_map/ppermute | solution.py:230
  78.2 0.0 collective-permute-done.18.rest_10_
  78.2 0.6 collective-permute-start.23
  78.8 0.0 collective-permute-done.19.rest_11_
  78.8 1.2 %collective-permute-start.10 = (bf16[16,2048]{1,0:T(8,128)(2,1)S(1)}, bf16[16,2048]{1,0:T(8,128)(2,1)S(1)}, u32[]{:S(2)}, u32[]{:S(2)}) collective-permute-start(bf16[16,2048]{1,0:T(8,128)(2,1)S(1)} %copy-done.19), channel_id=1, source_target_pairs={{0,4},{4,0},{8,12},{12,8},{16,20},{20,16},{24,28},{28,24},{1,5},{5... | collective-permute-start | bytes 196616 | tf_op jit(solution)/shard_map/ppermute | solution.py:230
  80.1 0.0 collective-permute-done.20.rest_12_
  80.1 0.8 collective-permute-start.11
  80.8 1.3 %collective-permute-done.21.rest_13_ = bf16[16,2048]{1,0:T(8,128)(2,1)S(1)} collective-permute-done((bf16[16,2048]{1,0:T(8,128)(2,1)S(1)}, bf16[16,2048]{1,0:T(8,128)(2,1)S(1)}, u32[]{:S(2)}, u32[]{:S(2)}) %collective-permute-start.21) | collective-permute-done | bytes 65568 | tf_op jit(solution)/shard_map/ppermute | solution.py:230
  82.2 2.3 %collective-permute-start.12 = (bf16[16,2048]{1,0:T(8,128)(2,1)S(1)}, bf16[16,2048]{1,0:T(8,128)(2,1)S(1)}, u32[]{:S(2)}, u32[]{:S(2)}) collective-permute-start(bf16[16,2048]{1,0:T(8,128)(2,1)S(1)} %copy-done.15), channel_id=1, source_target_pairs={{0,12},{4,8},{8,4},{12,0},{16,28},{20,24},{24,20},{28,16},{1,13},{... | collective-permute-start | bytes 196616 | tf_op jit(solution)/shard_map/ppermute | solution.py:230
  84.5 0.0 collective-permute-done.22.rest_14_
  84.5 1.2 %collective-permute-start.13 = (bf16[16,2048]{1,0:T(8,128)(2,1)S(1)}, bf16[16,2048]{1,0:T(8,128)(2,1)S(1)}, u32[]{:S(2)}, u32[]{:S(2)}) collective-permute-start(bf16[16,2048]{1,0:T(8,128)(2,1)S(1)} %copy-done.13), channel_id=1, source_target_pairs={{0,16},{4,20},{8,24},{12,28},{16,0},{20,4},{24,8},{28,12},{1,17},{... | collective-permute-start | bytes 196616 | tf_op jit(solution)/shard_map/ppermute | solution.py:230
  85.7 0.2 collective-permute-start.14
  85.9 0.0 collective-permute-done.10.rest_1_
  85.9 1.1 %collective-permute-start.15 = (bf16[16,2048]{1,0:T(8,128)(2,1)S(1)}, bf16[16,2048]{1,0:T(8,128)(2,1)S(1)}, u32[]{:S(2)}, u32[]{:S(2)}) collective-permute-start(bf16[16,2048]{1,0:T(8,128)(2,1)S(1)} %get-tuple-element.43), channel_id=1, source_target_pairs={{0,24},{4,28},{8,16},{12,20},{16,8},{20,12},{24,0},{28,4},{1,25},{... | collective-permute-start | bytes 196616 | tf_op jit(solution)/shard_map/ppermute | solution.py:230
  87.0 1.9 %collective-permute-start.16 = (bf16[16,2048]{1,0:T(8,128)(2,1)S(1)}, bf16[16,2048]{1,0:T(8,128)(2,1)S(1)}, u32[]{:S(2)}, u32[]{:S(2)}) collective-permute-start(bf16[16,2048]{1,0:T(8,128)(2,1)S(1)} %get-tuple-element.44), channel_id=1, source_target_pairs={{0,28},{4,24},{8,20},{12,16},{16,12},{20,8},{24,4},{28,0},{1,29},{... | collective-permute-start | bytes 196616 | tf_op jit(solution)/shard_map/ppermute | solution.py:230
  88.9 1.1 %collective-permute-done.14.rest_5_ = bf16[16,2048]{1,0:T(8,128)(2,1)S(1)} collective-permute-done((bf16[16,2048]{1,0:T(8,128)(2,1)S(1)}, bf16[16,2048]{1,0:T(8,128)(2,1)S(1)}, u32[]{:S(2)}, u32[]{:S(2)}) %collective-permute-start.14) | collective-permute-done | bytes 65568 | tf_op jit(solution)/shard_map/ppermute | solution.py:230
  90.1 1.8 %collective-permute-done.15.rest_6_ = bf16[16,2048]{1,0:T(8,128)(2,1)S(1)} collective-permute-done((bf16[16,2048]{1,0:T(8,128)(2,1)S(1)}, bf16[16,2048]{1,0:T(8,128)(2,1)S(1)}, u32[]{:S(2)}, u32[]{:S(2)}) %collective-permute-start.15) | collective-permute-done | bytes 65568 | tf_op jit(solution)/shard_map/ppermute | solution.py:230
  91.8 0.9 collective-permute-done.16.rest_7_
  92.7 2.9 %place.1 = bf16[256,2048]{1,0:T(8,128)(2,1)} custom-call(s32[24]{0:T(128)S(1)} %copy-done.9, f32[256,128]{1,0:T(8,128)S(1)} %bitcast.8, f32[1,2048]{1,0:T(1,128)S(1)} %bitcast.11, bf16[256,2048]{1,0:T(8,128)(2,1)S(1)} %copy-done.2, bf16[16,2048]{1,0:T(8,128)(2,1)S(1)} %get-tuple-element.37.rest_0_, bf16[16,2048]{1,0:T(8,128)(2,1)S(1)} %collective-permute-done.10.rest_1_, ...), custom_call_target="tpu_custom_call" | custom-call | tf_op jit(solution)/shard_map/place/pallas_call | solution.py:281
  (35 shorter events, 0.1 us)
Async XLA Ops:
  3.9 55.7 %copy-start.3 = (bf16[32,3200]{1,0:T(8,128)(2,1)S(1)}, bf16[32,3200]{1,0:T(8,128)(2,1)}, u32[]{:S(2)}) copy-start(bf16[32,3200]{1,0:T(8,128)(2,1)} %get-tuple-element.32.own) | copy-start | bytes 614404
  3.9 9.1 %collective-permute-start.5 = (bf16[32,3200]{1,0:T(8,128)(2,1)}, bf16[32,3200]{1,0:T(8,128)(2,1)S(1)}, u32[]{:S(2)}, u32[]{:S(2)}) collective-permute-start(bf16[32,3200]{1,0:T(8,128)(2,1)} %get-tuple-element.33.own), channel_id=1, source_target_pairs={{0,1},{1,0},{2,3},{3,2},{4,5},{5,4},{6,7},{7,6},{8,9},{9,8},{10,11... | collective-permute-start | bytes 614408 | tf_op jit(solution)/shard_map/ppermute | solution.py:221
  7.0 15.5 %collective-permute-start = (bf16[32,3200]{1,0:T(8,128)(2,1)}, bf16[32,3200]{1,0:T(8,128)(2,1)S(1)}, u32[]{:S(2)}, u32[]{:S(2)}) collective-permute-start(bf16[32,3200]{1,0:T(8,128)(2,1)} %get-tuple-element.32.own), channel_id=1, source_target_pairs={{0,1},{1,0},{2,3},{3,2},{4,5},{5,4},{6,7},{7,6},{8,9},{9,8},{10,11... | collective-permute-start | bytes 614408 | tf_op jit(solution)/shard_map/ppermute | solution.py:221
  7.0 16.1 %collective-permute-start.6 = (bf16[32,3200]{1,0:T(8,128)(2,1)}, bf16[32,3200]{1,0:T(8,128)(2,1)S(1)}, u32[]{:S(2)}, u32[]{:S(2)}) collective-permute-start(bf16[32,3200]{1,0:T(8,128)(2,1)} %get-tuple-element.33.own), channel_id=1, source_target_pairs={{1,2},{2,1},{0,0},{3,3},{5,6},{6,5},{4,4},{7,7},{9,10},{10,9},{8,8... | collective-permute-start | bytes 614408 | tf_op jit(solution)/shard_map/ppermute | solution.py:225
  13.1 15.5 %collective-permute-start.8 = (bf16[32,3200]{1,0:T(8,128)(2,1)S(1)}, bf16[32,3200]{1,0:T(8,128)(2,1)S(1)}, u32[]{:S(2)}, u32[]{:S(2)}) collective-permute-start(bf16[32,3200]{1,0:T(8,128)(2,1)S(1)} %collective-permute-done.5.a1), channel_id=1, source_target_pairs={{1,2},{2,1},{0,0},{3,3},{5,6},{6,5},{4,4},{7,7},{9,10},{10,9},{8,8... | collective-permute-start | bytes 614408 | tf_op jit(solution)/shard_map/ppermute | solution.py:225
  13.7 23.1 %all-to-all-start = ((s32[32,8,128]{2,1,0:T(8,128)}), s32[32,8,128]{2,1,0:T(8,128)S(1)}, u32[]{:S(2)}, u32[]{:S(2)}) async-start(s32[32,8,128]{2,1,0:T(8,128)} %bitcast.12), calls=%async_computation | async-start | bytes 262144 | tf_op jit(solution)/shard_map/all_to_all | solution.py:258
  20.9 7.8 %collective-permute-start.1 = (bf16[32,3200]{1,0:T(8,128)(2,1)}, bf16[32,3200]{1,0:T(8,128)(2,1)S(1)}, u32[]{:S(2)}, u32[]{:S(2)}) collective-permute-start(bf16[32,3200]{1,0:T(8,128)(2,1)} %get-tuple-element.32.own), channel_id=1, source_target_pairs={{1,2},{2,1},{0,0},{3,3},{5,6},{6,5},{4,4},{7,7},{9,10},{10,9},{8,8... | collective-permute-start | bytes 614408 | tf_op jit(solution)/shard_map/ppermute | solution.py:225
  22.5 10.2 %collective-permute-start.3 = (bf16[32,3200]{1,0:T(8,128)(2,1)S(1)}, bf16[32,3200]{1,0:T(8,128)(2,1)S(1)}, u32[]{:S(2)}, u32[]{:S(2)}) collective-permute-start(bf16[32,3200]{1,0:T(8,128)(2,1)S(1)} %collective-permute-done.a1), channel_id=1, source_target_pairs={{1,2},{2,1},{0,0},{3,3},{5,6},{6,5},{4,4},{7,7},{9,10},{10,9},{8,8... | collective-permute-start | bytes 614408 | tf_op jit(solution)/shard_map/ppermute | solution.py:225
  23.1 18.9 %collective-permute-start.7 = (bf16[32,3200]{1,0:T(8,128)(2,1)S(1)}, bf16[32,3200]{1,0:T(8,128)(2,1)S(1)}, u32[]{:S(2)}, u32[]{:S(2)}) collective-permute-start(bf16[32,3200]{1,0:T(8,128)(2,1)S(1)} %collective-permute-done.6.b1), channel_id=1, source_target_pairs={{0,1},{1,0},{2,3},{3,2},{4,5},{5,4},{6,7},{7,6},{8,9},{9,8},{10,11... | collective-permute-start | bytes 614408 | tf_op jit(solution)/shard_map/ppermute | solution.py:221
  28.6 13.5 %collective-permute-start.9 = (bf16[32,3200]{1,0:T(8,128)(2,1)S(1)}, bf16[32,3200]{1,0:T(8,128)(2,1)S(1)}, u32[]{:S(2)}, u32[]{:S(2)}) collective-permute-start(bf16[32,3200]{1,0:T(8,128)(2,1)S(1)} %collective-permute-done.8.b2), channel_id=1, source_target_pairs={{0,1},{1,0},{2,3},{3,2},{4,5},{5,4},{6,7},{7,6},{8,9},{9,8},{10,11... | collective-permute-start | bytes 614408 | tf_op jit(solution)/shard_map/ppermute | solution.py:221
  28.7 30.9 %collective-permute-start.2 = (bf16[32,3200]{1,0:T(8,128)(2,1)S(1)}, bf16[32,3200]{1,0:T(8,128)(2,1)S(1)}, u32[]{:S(2)}, u32[]{:S(2)}) collective-permute-start(bf16[32,3200]{1,0:T(8,128)(2,1)S(1)} %collective-permute-done.1.b1), channel_id=1, source_target_pairs={{0,1},{1,0},{2,3},{3,2},{4,5},{5,4},{6,7},{7,6},{8,9},{9,8},{10,11... | collective-permute-start | bytes 614408 | tf_op jit(solution)/shard_map/ppermute | solution.py:221
  32.7 27.0 %collective-permute-start.4 = (bf16[32,3200]{1,0:T(8,128)(2,1)S(1)}, bf16[32,3200]{1,0:T(8,128)(2,1)S(1)}, u32[]{:S(2)}, u32[]{:S(2)}) collective-permute-start(bf16[32,3200]{1,0:T(8,128)(2,1)S(1)} %collective-permute-done.3.b2), channel_id=1, source_target_pairs={{0,1},{1,0},{2,3},{3,2},{4,5},{5,4},{6,7},{7,6},{8,9},{9,8},{10,11... | collective-permute-start | bytes 614408 | tf_op jit(solution)/shard_map/ppermute | solution.py:221
  42.1 4.7 %copy-start = (bf16[3200,2048]{1,0:T(8,128)(2,1)S(1)}, bf16[3200,2048]{1,0:T(8,128)(2,1)}, u32[]{:S(2)}) copy-start(bf16[3200,2048]{1,0:T(8,128)(2,1)} %weight.3) | copy-start | bytes 39321604
  46.8 0.9 copy-start.4
  47.8 0.7 copy-start.5
  48.5 0.6 copy-start.8
  49.1 10.6 %copy-start.1 = (bf16[3200,2048]{1,0:T(8,128)(2,1)S(1)}, bf16[3200,2048]{1,0:T(8,128)(2,1)}, u32[]{:S(2)}) copy-start(bf16[3200,2048]{1,0:T(8,128)(2,1)} %weight.3) | copy-start | bytes 39321604
  49.1 10.6 %copy-start.7 = (f32[8,128]{1,0:T(8,128)S(1)}, f32[8,128]{1,0:T(8,128)}, u32[]{:S(2)}) copy-start(f32[8,128]{1,0:T(8,128)} %get-tuple-element.35.rest_1_) | copy-start | bytes 12292
  49.1 43.6 %copy-start.2 = (bf16[256,2048]{1,0:T(8,128)(2,1)S(1)}, bf16[256,2048]{1,0:T(8,128)(2,1)}, u32[]{:S(2)}) copy-start(bf16[256,2048]{1,0:T(8,128)(2,1)} %text.3) | copy-start | bytes 3145732
  49.1 43.6 %copy-start.6 = (f32[2048]{0:T(1024)S(1)}, f32[2048]{0:T(1024)}, u32[]{:S(2)}) copy-start(f32[2048]{0:T(1024)} %param.14) | copy-start | bytes 24580
  49.1 43.6 %copy-start.9 = (s32[24]{0:T(128)S(1)}, s32[24]{0:T(128)}, u32[]{:S(2)}) copy-start(s32[24]{0:T(128)} %get-tuple-element.30.start) | copy-start | bytes 292
  56.5 0.6 copy-start.10
  57.1 0.6 copy-start.12
  57.8 0.6 copy-start.14
  58.4 0.6 copy-start.16
  59.0 0.6 copy-start.18
  59.6 19.2 %copy-start.19 = (bf16[16,2048]{1,0:T(8,128)(2,1)S(1)}, bf16[16,2048]{1,0:T(8,128)(2,1)}, u32[]{:S(2)}) copy-start(bf16[16,2048]{1,0:T(8,128)(2,1)} %copy-done.18) | copy-start | bytes 196612
  59.6 20.4 %copy-start.17 = (bf16[16,2048]{1,0:T(8,128)(2,1)S(1)}, bf16[16,2048]{1,0:T(8,128)(2,1)}, u32[]{:S(2)}) copy-start(bf16[16,2048]{1,0:T(8,128)(2,1)} %copy-done.16) | copy-start | bytes 196612
  59.6 22.5 %copy-start.15 = (bf16[16,2048]{1,0:T(8,128)(2,1)S(1)}, bf16[16,2048]{1,0:T(8,128)(2,1)}, u32[]{:S(2)}) copy-start(bf16[16,2048]{1,0:T(8,128)(2,1)} %copy-done.14) | copy-start | bytes 196612
  59.6 24.9 %copy-start.13 = (bf16[16,2048]{1,0:T(8,128)(2,1)S(1)}, bf16[16,2048]{1,0:T(8,128)(2,1)}, u32[]{:S(2)}) copy-start(bf16[16,2048]{1,0:T(8,128)(2,1)} %copy-done.12) | copy-start | bytes 196612
  59.6 26.1 %copy-start.11 = (bf16[16,2048]{1,0:T(8,128)(2,1)S(1)}, bf16[16,2048]{1,0:T(8,128)(2,1)}, u32[]{:S(2)}) copy-start(bf16[16,2048]{1,0:T(8,128)(2,1)} %copy-done.10) | copy-start | bytes 196612
  67.8 24.9 %all-to-all-start.1 = ((f32[32,8,128]{2,1,0:T(8,128)}), f32[32,8,128]{2,1,0:T(8,128)S(1)}, u32[]{:S(2)}, u32[]{:S(2)}) async-start(f32[32,8,128]{2,1,0:T(8,128)} %bitcast.3), calls=%async_computation.1 | async-start | bytes 262144 | tf_op jit(solution)/shard_map/all_to_all | solution.py:277
  71.8 3.8 %collective-permute-start.17 = (bf16[16,2048]{1,0:T(8,128)(2,1)S(1)}, bf16[16,2048]{1,0:T(8,128)(2,1)S(1)}, u32[]{:S(2)}, u32[]{:S(2)}) collective-permute-start(bf16[16,2048]{1,0:T(8,128)(2,1)S(1)} %get-tuple-element.46), channel_id=1, source_target_pairs={{0,4},{4,0},{8,12},{12,8},{16,20},{20,16},{24,28},{28,24},{1,5},{5... | collective-permute-start | bytes 196616 | tf_op jit(solution)/shard_map/ppermute | solution.py:230
  72.1 6.1 %collective-permute-start.18 = (bf16[16,2048]{1,0:T(8,128)(2,1)S(1)}, bf16[16,2048]{1,0:T(8,128)(2,1)S(1)}, u32[]{:S(2)}, u32[]{:S(2)}) collective-permute-start(bf16[16,2048]{1,0:T(8,128)(2,1)S(1)} %get-tuple-element.47), channel_id=1, source_target_pairs={{0,8},{4,12},{8,0},{12,4},{16,24},{20,28},{24,16},{28,20},{1,9},{5... | collective-permute-start | bytes 196616 | tf_op jit(solution)/shard_map/ppermute | solution.py:230
  73.8 5.0 %collective-permute-start.19 = (bf16[16,2048]{1,0:T(8,128)(2,1)S(1)}, bf16[16,2048]{1,0:T(8,128)(2,1)S(1)}, u32[]{:S(2)}, u32[]{:S(2)}) collective-permute-start(bf16[16,2048]{1,0:T(8,128)(2,1)S(1)} %get-tuple-element.48), channel_id=1, source_target_pairs={{0,12},{4,8},{8,4},{12,0},{16,28},{20,24},{24,20},{28,16},{1,13},{... | collective-permute-start | bytes 196616 | tf_op jit(solution)/shard_map/ppermute | solution.py:230
  73.8 6.2 %collective-permute-start.20 = (bf16[16,2048]{1,0:T(8,128)(2,1)S(1)}, bf16[16,2048]{1,0:T(8,128)(2,1)S(1)}, u32[]{:S(2)}, u32[]{:S(2)}) collective-permute-start(bf16[16,2048]{1,0:T(8,128)(2,1)S(1)} %get-tuple-element.49), channel_id=1, source_target_pairs={{0,16},{4,20},{8,24},{12,28},{16,0},{20,4},{24,8},{28,12},{1,17},{... | collective-permute-start | bytes 196616 | tf_op jit(solution)/shard_map/ppermute | solution.py:230
  75.5 6.6 %collective-permute-start.21 = (bf16[16,2048]{1,0:T(8,128)(2,1)S(1)}, bf16[16,2048]{1,0:T(8,128)(2,1)S(1)}, u32[]{:S(2)}, u32[]{:S(2)}) collective-permute-start(bf16[16,2048]{1,0:T(8,128)(2,1)S(1)} %get-tuple-element.50), channel_id=1, source_target_pairs={{0,20},{4,16},{8,28},{12,24},{16,4},{20,0},{24,12},{28,8},{1,21},{... | collective-permute-start | bytes 196616 | tf_op jit(solution)/shard_map/ppermute | solution.py:230
  75.6 8.9 %collective-permute-start.22 = (bf16[16,2048]{1,0:T(8,128)(2,1)S(1)}, bf16[16,2048]{1,0:T(8,128)(2,1)S(1)}, u32[]{:S(2)}, u32[]{:S(2)}) collective-permute-start(bf16[16,2048]{1,0:T(8,128)(2,1)S(1)} %get-tuple-element.51), channel_id=1, source_target_pairs={{0,24},{4,28},{8,16},{12,20},{16,8},{20,12},{24,0},{28,4},{1,25},{... | collective-permute-start | bytes 196616 | tf_op jit(solution)/shard_map/ppermute | solution.py:230
  78.2 7.5 %collective-permute-start.23 = (bf16[16,2048]{1,0:T(8,128)(2,1)S(1)}, bf16[16,2048]{1,0:T(8,128)(2,1)S(1)}, u32[]{:S(2)}, u32[]{:S(2)}) collective-permute-start(bf16[16,2048]{1,0:T(8,128)(2,1)S(1)} %get-tuple-element.52), channel_id=1, source_target_pairs={{0,28},{4,24},{8,20},{12,16},{16,12},{20,8},{24,4},{28,0},{1,29},{... | collective-permute-start | bytes 196616 | tf_op jit(solution)/shard_map/ppermute | solution.py:230
  78.8 7.1 %collective-permute-start.10 = (bf16[16,2048]{1,0:T(8,128)(2,1)S(1)}, bf16[16,2048]{1,0:T(8,128)(2,1)S(1)}, u32[]{:S(2)}, u32[]{:S(2)}) collective-permute-start(bf16[16,2048]{1,0:T(8,128)(2,1)S(1)} %copy-done.19), channel_id=1, source_target_pairs={{0,4},{4,0},{8,12},{12,8},{16,20},{20,16},{24,28},{28,24},{1,5},{5... | collective-permute-start | bytes 196616 | tf_op jit(solution)/shard_map/ppermute | solution.py:230
  80.1 6.9 %collective-permute-start.11 = (bf16[16,2048]{1,0:T(8,128)(2,1)S(1)}, bf16[16,2048]{1,0:T(8,128)(2,1)S(1)}, u32[]{:S(2)}, u32[]{:S(2)}) collective-permute-start(bf16[16,2048]{1,0:T(8,128)(2,1)S(1)} %copy-done.17), channel_id=1, source_target_pairs={{0,8},{4,12},{8,0},{12,4},{16,24},{20,28},{24,16},{28,20},{1,9},{5... | collective-permute-start | bytes 196616 | tf_op jit(solution)/shard_map/ppermute | solution.py:230
  82.2 6.8 %collective-permute-start.12 = (bf16[16,2048]{1,0:T(8,128)(2,1)S(1)}, bf16[16,2048]{1,0:T(8,128)(2,1)S(1)}, u32[]{:S(2)}, u32[]{:S(2)}) collective-permute-start(bf16[16,2048]{1,0:T(8,128)(2,1)S(1)} %copy-done.15), channel_id=1, source_target_pairs={{0,12},{4,8},{8,4},{12,0},{16,28},{20,24},{24,20},{28,16},{1,13},{... | collective-permute-start | bytes 196616 | tf_op jit(solution)/shard_map/ppermute | solution.py:230
  84.5 4.4 %collective-permute-start.13 = (bf16[16,2048]{1,0:T(8,128)(2,1)S(1)}, bf16[16,2048]{1,0:T(8,128)(2,1)S(1)}, u32[]{:S(2)}, u32[]{:S(2)}) collective-permute-start(bf16[16,2048]{1,0:T(8,128)(2,1)S(1)} %copy-done.13), channel_id=1, source_target_pairs={{0,16},{4,20},{8,24},{12,28},{16,0},{20,4},{24,8},{28,12},{1,17},{... | collective-permute-start | bytes 196616 | tf_op jit(solution)/shard_map/ppermute | solution.py:230
  85.7 4.3 %collective-permute-start.14 = (bf16[16,2048]{1,0:T(8,128)(2,1)S(1)}, bf16[16,2048]{1,0:T(8,128)(2,1)S(1)}, u32[]{:S(2)}, u32[]{:S(2)}) collective-permute-start(bf16[16,2048]{1,0:T(8,128)(2,1)S(1)} %copy-done.11), channel_id=1, source_target_pairs={{0,20},{4,16},{8,28},{12,24},{16,4},{20,0},{24,12},{28,8},{1,21},{... | collective-permute-start | bytes 196616 | tf_op jit(solution)/shard_map/ppermute | solution.py:230
  85.9 5.9 %collective-permute-start.15 = (bf16[16,2048]{1,0:T(8,128)(2,1)S(1)}, bf16[16,2048]{1,0:T(8,128)(2,1)S(1)}, u32[]{:S(2)}, u32[]{:S(2)}) collective-permute-start(bf16[16,2048]{1,0:T(8,128)(2,1)S(1)} %get-tuple-element.43), channel_id=1, source_target_pairs={{0,24},{4,28},{8,16},{12,20},{16,8},{20,12},{24,0},{28,4},{1,25},{... | collective-permute-start | bytes 196616 | tf_op jit(solution)/shard_map/ppermute | solution.py:230
  87.0 5.7 %collective-permute-start.16 = (bf16[16,2048]{1,0:T(8,128)(2,1)S(1)}, bf16[16,2048]{1,0:T(8,128)(2,1)S(1)}, u32[]{:S(2)}, u32[]{:S(2)}) collective-permute-start(bf16[16,2048]{1,0:T(8,128)(2,1)S(1)} %get-tuple-element.44), channel_id=1, source_target_pairs={{0,28},{4,24},{8,20},{12,16},{16,12},{20,8},{24,4},{28,0},{1,29},{... | collective-permute-start | bytes 196616 | tf_op jit(solution)/shard_map/ppermute | solution.py:230

commit v2 on v0

--- a/solution.py
+++ b/solution.py
@@ -1,23 +1,270 @@
+import functools
+
 import jax
 import jax.numpy as jnp
 from jax import lax
+from jax.experimental import pallas as pl
+from jax.experimental.pallas import tpu as pltpu
 from jax.sharding import PartitionSpec as P
 
-D = 8192
-
-
-def on_device(
-    vis_features,
-    vis_gain,
-    proj_weight,
-    proj_bias,
-    text_embed,
-    out_gain,
-    image_counts,
-    owner_block,
-    offsets,
+EPS_VIS = 1e-06
+EPS_OUT = 1e-05
+TILE = (8, 128)
+F32 = jnp.float32
+BF16 = jnp.bfloat16
+VMEM = pl.BlockSpec(memory_space=pltpu.VMEM)
+SMEM = pl.BlockSpec(memory_space=pltpu.SMEM)
+ANY = pl.BlockSpec(memory_space=pl.ANY)
+LIMIT = 16 << 20
+
+
+def lanes():
+    return lax.broadcasted_iota(jnp.int32, TILE, 1)
+
+
+def tables_kernel(slots, size, text, owners, offsets, counts, squares, info):
+    lane = lanes()
+    tile = jnp.zeros(TILE, F32)
+    for c in range(text.shape[0] // 16):
+        x = text[c * 16 : (c + 1) * 16, :].astype(F32)
+        sums = jnp.sum(x * x, axis=1, keepdims=True)
+        tile = jnp.where(lane == 2 * c, sums[:8], tile)
+        tile = jnp.where(lane == 2 * c + 1, sums[8:], tile)
+    squares[...] = tile
+    row = lax.axis_index("dp")
+    lane = lax.broadcasted_iota(jnp.int32, (size, 128), 1)
+    for i in range(slots):
+        code = jnp.where(i < counts[0], offsets[i] // size + 1, 0)
+        known = jnp.where(lane == 0, owners[i], jnp.where(lane == 1, row * slots + i, jnp.where(lane == 2, code, 0)))
+        info[i * size : (i + 1) * size, :] = known.astype(F32).astype(BF16)
+
+
+def hold_kernel(weight, tile, out):
+    del weight
+    out[...] = tile[...]
+
+
+def normed(rows, gain):
+    x = rows.astype(F32)
+    scale = lax.rsqrt(jnp.mean(x * x, axis=-1, keepdims=True) + EPS_VIS)
+    return (x * scale * gain).astype(BF16)
+
+
+def norm_kernel(own, outer, inner, ends, gain, rows):
+    row = lax.axis_index("dp")
+    middle = jnp.logical_or(row == 1, row == 2)
+    g = gain[...].reshape(1, own.shape[1])
+    count = own.shape[0]
+    rows[0:count] = normed(own[...], g)
+    rows[count : 2 * count] = normed(outer[...], g)
+    rows[2 * count : 3 * count] = normed(jnp.where(middle, inner[...], ends[...]), g)
+
+
+def pass_kernel(own, inner, sent):
+    row = lax.axis_index("dp")
+    sent[...] = jnp.where(jnp.logical_or(row == 1, row == 2), inner[...], own[...])
+
+
+def project_kernel(groups, cap, size, i0, i1, i2, i3, rows, last, gain, weight, bias, text_squares, *rest):
+    *outs, tiles, x = rest
+    me = lax.axis_index("grp")
+    depth, columns = weight.shape
+    known = jnp.concatenate([i0[...], i1[...], i2[...], i3[...]], axis=0)
+    total = known.shape[0]
+    down = known.astype(F32)
+    across = down.T
+    owner_down, slot_down = down[:, 0:1], down[:, 1:2]
+    owner, slot = across[0:1, :], across[1:2, :]
+    earlier = jnp.logical_and(owner_down == owner, slot_down < slot)
+    rank = jnp.sum(earlier.astype(F32), axis=0, keepdims=True).astype(jnp.int32) // size
+    place = owner.astype(jnp.int32) ^ me
+    position = lax.broadcasted_iota(jnp.int32, (1, total), 1) % size
+    seat = (place * cap + rank) * size + position
+    order = (lax.broadcasted_iota(jnp.int32, (total, total), 0) == seat).astype(BF16)
+    codes = jnp.dot(order, known, preferred_element_type=F32)[:, 2:3]
+    every = jnp.concatenate([rows[...], normed(last[...], gain[...].reshape(1, depth))], axis=0)
+    x[...] = jnp.dot(order, every, preferred_element_type=F32).astype(BF16)
+    block = 256
+    partial = jnp.zeros((total, 128), F32)
+    for n in range(columns // block):
+        at = slice(n * block, (n + 1) * block)
+        y = jnp.dot(x[...], weight[:, at], preferred_element_type=F32) + bias[:, at]
+        y = y.astype(BF16)
+        for k in range(groups):
+            outs[k][:, at] = y[k * cap * size : (k + 1) * cap * size]
+        wide = y.astype(F32)
+        wide = wide * wide
+        for c in range(block // 128):
+            partial = partial + wide[:, c * 128 : (c + 1) * 128]
+    lane = lanes()
+    sums = jnp.sum(partial, axis=1, keepdims=True)
+    copies = tiles.shape[0] // (8 * groups)
+    for k in range(groups):
+        tile = jnp.zeros(TILE, F32)
+        for r in range(cap):
+            at = (k * cap + r) * size
+            tile = jnp.where(lane == 2 * r, sums[at : at + 8], tile)
+            tile = jnp.where(lane == 2 * r + 1, sums[at + 8 : at + 16], tile)
+            tile = jnp.where(lane == 2 * cap + r, codes[at : at + 8], tile)
+        if k == 0:
+            tile = jnp.where(lane < 3 * cap, tile, pltpu.roll(text_squares[...], 3 * cap, 1))
+        for q in range(copies):
+            tiles[pl.ds(pl.multiple_of(((me ^ k) * copies + q) * 8, 8), 8), :] = tile
+
+
+def place_kernel(groups, dp, cap, size, width, squares, gain, text, *rest):
+    arrived, (out, rows) = rest[:groups], rest[groups:]
+    me = lax.axis_index("grp")
+    seq_len = text.shape[0]
+    total = groups * cap * size
+    g = gain[...]
+    codes = []
+    for k in range(groups):
+        base = (me ^ k) * (dp * 8)
+        tile = squares[pl.ds(pl.multiple_of(base, 8), 8), :]
+        code = tile
+        for d in range(1, dp):
+            tile = tile + squares[pl.ds(pl.multiple_of(base + d * 8, 8), 8), :]
+        scale = lax.rsqrt(tile / width + EPS_OUT)
+        if k == 0:
+            own = scale
+        for r in range(cap):
+            inverse = jnp.concatenate([scale[:, 2 * r : 2 * r + 1], scale[:, 2 * r + 1 : 2 * r + 2]], axis=0)
+            part = slice(r * size, (r + 1) * size)
+            at = (k * cap + r) * size
+            rows[at : at + size, :] = (arrived[k][part, :].astype(F32) * inverse * g).astype(BF16)
+            codes += [jnp.broadcast_to(code[:, 2 * cap + r : 2 * cap + r + 1], TILE)] * 2
+    code = jnp.concatenate(codes, axis=0).T[0:1, :].astype(jnp.int32)
+    position = lax.broadcasted_iota(jnp.int32, (1, total), 1) % size
+    target = jnp.where(code > 0, (code - 1) * size + position, -1)
+    order = (lax.broadcasted_iota(jnp.int32, (seq_len, total), 0) == target).astype(F32)
+    covered = jnp.sum(order, axis=1, keepdims=True)
+    moved = jnp.dot(order.astype(BF16), rows[...], preferred_element_type=F32)
+    for c in range(seq_len // 16):
+        at = 3 * cap + 2 * c
+        inverse = jnp.concatenate([own[:, at : at + 1], own[:, at + 1 : at + 2]], axis=0)
+        part = slice(c * 16, (c + 1) * 16)
+        x = text[part, :].astype(F32) * inverse * g
+        out[part, :] = jnp.where(covered[part] > 0, moved[part], x).astype(BF16)
+
+
+def outer(x):
+    return lax.ppermute(x, "dp", [(0, 1), (1, 0), (2, 3), (3, 2)])
+
+
+def inner(x):
+    return lax.ppermute(x, "dp", [(1, 2), (2, 1), (0, 0), (3, 3)])
+
+
+def ends(x):
+    return lax.ppermute(x, "dp", [(0, 3), (3, 0), (1, 1), (2, 2)])
+
+
+def mirror(x):
+    return lax.ppermute(x, "dp", [(0, 3), (1, 2), (2, 1), (3, 0)])
+
+
+def second(x):
+    return lax.ppermute(x, "dp", [(0, 2), (1, 3), (2, 0), (3, 1)])
+
+
+def far(x):
+    return lax.ppermute(x, "dp", [(0, 2), (1, 0), (2, 3), (3, 1)])
+
+
+def route(parts):
+    groups = len(parts)
+    near = [k for k in range(1, groups) if k & (k - 1) == 0]
+    order = near[:0:-1] + [k for k in range(groups - 1, 0, -1) if k not in near] + near[:1]
+    arrived = {k: lax.ppermute(parts[k], "grp", [(i, i ^ k) for i in range(groups)]) for k in order}
+    return [parts[0]] + [arrived[k] for k in range(1, groups)]
+
+
+def fast(vis, vis_gain, weight, bias, text, out_gain, counts, owners, offsets):
+    groups, dp = lax.axis_size("grp"), lax.axis_size("dp")
+    devices = groups * dp
+    slots = owners.shape[0]
+    size = vis.shape[0] // slots
+    seq_len, columns = text.shape
+    cap = seq_len // (groups * size)
+    depth = vis.shape[1]
+    small = pltpu.CompilerParams(vmem_limit_bytes=LIMIT)
+    count = slots * size
+
+    x_outer, x_inner = outer(vis), inner(vis)
+    text_squares, info = pl.pallas_call(
+        functools.partial(tables_kernel, slots, size),
+        in_specs=[VMEM, SMEM, SMEM, SMEM],
+        out_specs=[VMEM] * 2,
+        out_shape=[jax.ShapeDtypeStruct(TILE, F32), jax.ShapeDtypeStruct((count, 128), BF16)],
+        compiler_params=small,
+        name="tables",
+    )(text, owners, offsets, counts)
+    late, text_squares = lax.optimization_barrier((vis, text_squares))
+    x_ends = ends(late)
+    x_inner, x_outer, late = lax.optimization_barrier((x_inner, x_outer, late))
+    sent = pl.pallas_call(
+        pass_kernel,
+        in_specs=[VMEM] * 2,
+        out_specs=VMEM,
+        out_shape=jax.ShapeDtypeStruct(vis.shape, BF16),
+        compiler_params=small,
+        name="pass",
+    )(late, x_inner)
+    x_far = far(sent)
+    sent, text_squares = lax.optimization_barrier((sent, text_squares))
+    weight = pltpu.with_memory_space_constraint(weight, pltpu.VMEM)
+    text_squares = pl.pallas_call(
+        hold_kernel,
+        in_specs=[ANY, VMEM],
+        out_specs=VMEM,
+        out_shape=jax.ShapeDtypeStruct(TILE, F32),
+        compiler_params=small,
+        cost_estimate=pl.CostEstimate(flops=0, bytes_accessed=2 * weight.size, transcendentals=0),
+        name="hold",
+    )(weight, text_squares)
+    x_outer, text_squares = lax.optimization_barrier((x_outer, text_squares))
+    known = (info, outer(info), mirror(info), second(info))
+    rows = pl.pallas_call(
+        norm_kernel,
+        in_specs=[VMEM] * 5,
+        out_specs=VMEM,
+        out_shape=jax.ShapeDtypeStruct((3 * count, depth), BF16),
+        compiler_params=small,
+        cost_estimate=pl.CostEstimate(flops=0, bytes_accessed=2 * weight.size, transcendentals=0),
+        name="norm",
+    )(vis, x_outer, x_inner, x_ends, vis_gain)
+    *parts, squares = pl.pallas_call(
+        functools.partial(project_kernel, groups, cap, size),
+        in_specs=[VMEM] * 10,
+        out_specs=[VMEM] * (groups + 1),
+        out_shape=[jax.ShapeDtypeStruct((cap * size, columns), BF16)] * groups
+        + [jax.ShapeDtypeStruct((devices * 8, 128), F32)],
+        scratch_shapes=[pltpu.VMEM((dp * slots * size, depth), BF16)],
+        compiler_params=small,
+        cost_estimate=pl.CostEstimate(
+            flops=2 * dp * slots * size * depth * columns, bytes_accessed=2 * depth * columns, transcendentals=0
+        ),
+        name="project",
+    )(*known, rows, x_far, vis_gain, weight, bias[None, :], text_squares)
+    squares = lax.all_to_all(squares, ("grp", "dp"), 0, 0, tiled=True)
+    arrived = route(parts)
+    return pl.pallas_call(
+        functools.partial(place_kernel, groups, dp, cap, size, columns * dp),
+        in_specs=[VMEM] * (3 + groups),
+        out_specs=VMEM,
+        out_shape=jax.ShapeDtypeStruct(text.shape, BF16),
+        scratch_shapes=[pltpu.VMEM((groups * cap * size, columns), BF16)],
+        compiler_params=small,
+        name="place",
+    )(squares, out_gain[None, :], text, *arrived)
+
+
+def general(
+    vis_features, vis_gain, proj_weight, proj_bias, text_embed, out_gain, image_counts, owner_block, offsets
 ):
     groups = lax.axis_size("grp")
+    width = proj_weight.shape[1] * lax.axis_size("dp")
     slots_device = owner_block.shape[0]
     per_image = vis_features.shape[0] // slots_device
     columns = proj_weight.shape[1]
@@ -26,7 +273,7 @@
     features_f = vis_features.astype(jnp.float32)
     normed = (
         features_f
-        * lax.rsqrt(jnp.mean(features_f * features_f, axis=-1, keepdims=True) + 1e-06)
+        * lax.rsqrt(jnp.mean(features_f * features_f, axis=-1, keepdims=True) + EPS_VIS)
         * vis_gain
     ).astype(jnp.bfloat16)
     slot_local = jnp.arange(slots_device, dtype=jnp.int32)
@@ -72,9 +319,20 @@
     merged = text_embed.at[target].set(received, mode="drop")
     local_squares = jnp.sum(jnp.square(merged.astype(jnp.float32)), axis=1)
     row_total = lax.psum(local_squares, "dp")
-    inverse_rms = lax.rsqrt(row_total / D + 1e-05)
+    inverse_rms = lax.rsqrt(row_total / width + EPS_OUT)
     hidden = merged.astype(jnp.float32) * inverse_rms[:, None] * out_gain
     return hidden.astype(jnp.bfloat16)
+
+
+def on_device(vis, vis_gain, weight, bias, text, out_gain, counts, owners, offsets):
+    groups, dp = lax.axis_size("grp"), lax.axis_size("dp")
+    per_image = vis.shape[0] // owners.shape[0]
+    cap = text.shape[0] // (groups * per_image)
+    full = dp * owners.shape[0] == groups * cap and groups * cap * per_image == text.shape[0]
+    fits = dp == 4 and groups & (groups - 1) == 0 and per_image == 16 and cap == 2 and text.shape[0] <= 512
+    fits = fits and owners.shape[0] % 4 == 0 and weight.shape[1] % 1024 == 0
+    form = fast if full and fits else general
+    return form(vis, vis_gain, weight, bias, text, out_gain, counts, owners, offsets)
 
 
 def solution(mesh):

time: 121 us -> 65.6 us (0.54)
  blocking collectives: 19.5 us -> 0 us
  starting transfers between devices: 7.5 us -> 26.5 us
  other arithmetic: 18.3 us -> 0 us
  waiting for transfers between devices: 38 us -> 21.1 us
  between operations: 14.9 us -> 0.75 us
  matrix products: 9.33 us -> 0 us
  Pallas kernels: 0 us -> 8.53 us
  local copies, waits for them, and re-layouts: 13.2 us -> 8.28 us
    all_gather x1 -> x0, waiting for transfers between devices: 24.2 us -> none  [on_device(): lax.all_gather(normed, 'dp', axis=0, tiled=True)]
    ppermute x0 -> x14, starting transfers between devices: none -> 21.6 us  [the longest x7 6.4 us: route(): lax.ppermute(parts[k], 'grp', [(i, i ^ k) for i in range(groups)])]
    ppermute x0 -> x14, waiting for transfers between devices: none -> 21.1 us  [the longest x7 10.8 us: route(): lax.ppermute(parts[k], 'grp', [(i, i ^ k) for i in range(groups)])]
    all_to_all x3 -> x0, other arithmetic: 15.1 us -> none  [the longest x2 14.4 us: on_device(): lax.all_to_all(bucketed, 'grp', split_axis=0, concat_axis=0, tiled=True)]
    all_to_all x2 -> x1, waiting for transfers between devices: 13.8 us -> 0.01 us  [fast(): squares = lax.all_to_all(squares, ('grp', 'dp'), 0, 0, tiled=True)]
    unnamed x1 -> x0, blocking collectives: 9.89 us -> none
    psum x1 -> x0, blocking collectives: 9.61 us -> none  [on_device(): row_total = lax.psum(local_squares, 'dp')]
    dot_general x2 -> x0, matrix products: 9.33 us -> none  [the longest x1 8.91 us: on_device(): jnp.dot(lax.all_gather(normed, 'dp', axis=0, tiled=True), proj_weight, pr...]
  transfers between devices with their start and end apart: 3 -> 15, of which waited for: 2 -> 8; matrix products, arithmetic and copies ran while one was open for 18% -> 0% of each run, Pallas kernels for 0% -> 2%
where the time goes in v2:
time: 65.6 us; the launch traced here: 65.2 us
  starting transfers between devices  26.5 us (40%)
  waiting for transfers between devices  21.1 us (32%)
  Pallas kernels  8.53 us (13%)
  local copies, waits for them, and re-layouts  8.28 us (13%)
  between operations  0.75 us (1%)
    ppermute x7, waiting for transfers between devices, route(): lax.ppermute(parts[k], 'grp', [(i, i ^ k) for i in range(groups)])  10.8 us
    ppermute x2, waiting for transfers between devices, outer(): return lax.ppermute(x, 'dp', [(0, 1), (1, 0), (2, 3), (3, 2)])  9.39 us
    unnamed x22, local copies, waits for them, and re-layouts  8.28 us
    ppermute x7, starting transfers between devices, route(): lax.ppermute(parts[k], 'grp', [(i, i ^ k) for i in range(groups)])  6.4 us
    ppermute x2, starting transfers between devices, outer(): return lax.ppermute(x, 'dp', [(0, 1), (1, 0), (2, 3), (3, 2)])  5.98 us
    pallas_call x1, Pallas kernels, fast(): pl.pallas_call(functools.partial(project_kernel, groups, cap, size), in_s...  5.2 us
    all_to_all x1, starting transfers between devices, fast(): squares = lax.all_to_all(squares, ('grp', 'dp'), 0, 0, tiled=True)  4.95 us
    ppermute x1, starting transfers between devices, ends(): return lax.ppermute(x, 'dp', [(0, 3), (3, 0), (1, 1), (2, 2)])  3.25 us
  transfers between devices with their start and end apart: 15, of which 8 were waited for; matrix products, arithmetic and copies ran while one was open for 0% of the time, Pallas kernels for 2%

profile of v2, /device:TPU:0, one launch (start us, length us, event | category | flops | bytes accessed | tf_op | source)
XLA Modules:
  0.0 65.2 jit_solution(17771005493882803038)
XLA Ops:
  0.0 1.6 %collective-permute-start.3 = (bf16[64,3200]{1,0:T(8,128)(2,1)}, bf16[64,3200]{1,0:T(8,128)(2,1)S(1)}, u32[]{:S(2)}, u32[]{:S(2)}) collective-permute-start(bf16[64,3200]{1,0:T(8,128)(2,1)} %own.2), channel_id=1, source_target_pairs={{1,2},{2,1},{0,0},{3,3},{5,6},{6,5},{4,4},{7,7},{9,10},{10,9},{8,8... | collective-permute-start | bytes 1228808 | tf_op jit(solution)/shard_map/ppermute | solution.py:156
  1.7 4.9 %collective-permute-start.4 = (bf16[64,3200]{1,0:T(8,128)(2,1)}, bf16[64,3200]{1,0:T(8,128)(2,1)S(1)}, u32[]{:S(2)}, u32[]{:S(2)}) collective-permute-start(bf16[64,3200]{1,0:T(8,128)(2,1)} %own.2), channel_id=1, source_target_pairs={{0,1},{1,0},{2,3},{3,2},{4,5},{5,4},{6,7},{7,6},{8,9},{9,8},{10,11... | collective-permute-start | bytes 1228808 | tf_op jit(solution)/shard_map/ppermute | solution.py:152
  7.2 0.0 copy-start.2
  7.2 1.2 %copy-done.2 = bf16[256,2048]{1,0:T(8,128)(2,1)S(1)} copy-done((bf16[256,2048]{1,0:T(8,128)(2,1)S(1)}, bf16[256,2048]{1,0:T(8,128)(2,1)}, u32[]{:S(2)}) %copy-start.2) | copy-done | bytes 1048600
  8.5 0.0 copy-start.9
  8.5 0.7 %copy-done.9 = s32[4]{0:T(128)S(1)} copy-done((s32[4]{0:T(128)S(1)}, s32[4]{0:T(128)}, u32[]{:S(2)}) %copy-start.9) | copy-done | bytes 40
  9.1 0.0 copy-start.10
  9.1 0.7 %copy-done.10 = s32[4]{0:T(128)S(1)} copy-done((s32[4]{0:T(128)S(1)}, s32[4]{0:T(128)}, u32[]{:S(2)}) %copy-start.10) | copy-done | bytes 40
  9.8 0.0 copy-start.5
  9.8 0.0 copy-start.6
  9.8 0.0 copy-start.7
  9.8 0.8 %tables.1 = (f32[8,128]{1,0:T(8,128)S(1)}, bf16[64,128]{1,0:T(8,128)(2,1)S(1)}) custom-call(bf16[256,2048]{1,0:T(8,128)(2,1)S(1)} %copy-done.2, s32[4]{0:T(128)S(1)} %copy-done.9, s32[4]{0:T(128)S(1)} %copy-done.10, s32[1]{0:T(128)S(6)} %copy.10.counts), custom_call_target="tpu_custom_call" | custom-call | tf_op jit(solution)/shard_map/tables/pallas_call | solution.py:195
  10.6 3.2 %collective-permute-start.5 = (bf16[64,3200]{1,0:T(8,128)(2,1)}, bf16[64,3200]{1,0:T(8,128)(2,1)S(1)}, u32[]{:S(2)}, u32[]{:S(2)}) collective-permute-start(bf16[64,3200]{1,0:T(8,128)(2,1)} %own.2), channel_id=1, source_target_pairs={{0,3},{3,0},{1,1},{2,2},{4,7},{7,4},{5,5},{6,6},{8,11},{11,8},{9,9... | collective-permute-start | bytes 1228808 | tf_op jit(solution)/shard_map/ppermute | solution.py:160
  13.9 0.0 collective-permute-done.3.inner
  13.9 2.9 %collective-permute-done.4.outer = bf16[64,3200]{1,0:T(8,128)(2,1)S(1)} collective-permute-done((bf16[64,3200]{1,0:T(8,128)(2,1)}, bf16[64,3200]{1,0:T(8,128)(2,1)S(1)}, u32[]{:S(2)}, u32[]{:S(2)}) %collective-permute-start.4) | collective-permute-done | bytes 409632 | tf_op jit(solution)/shard_map/ppermute | solution.py:152
  16.8 0.0 copy-start.4
  16.8 1.0 %copy-done.4 = bf16[64,3200]{1,0:T(8,128)(2,1)S(1)} copy-done((bf16[64,3200]{1,0:T(8,128)(2,1)S(1)}, bf16[64,3200]{1,0:T(8,128)(2,1)}, u32[]{:S(2)}) %copy-start.4) | copy-done | bytes 409624
  17.8 0.1 pass.1
  17.9 1.5 %collective-permute-start.6 = (bf16[64,3200]{1,0:T(8,128)(2,1)S(1)}, bf16[64,3200]{1,0:T(8,128)(2,1)S(1)}, u32[]{:S(2)}, u32[]{:S(2)}) collective-permute-start(bf16[64,3200]{1,0:T(8,128)(2,1)S(1)} %pass.1), channel_id=1, source_target_pairs={{0,2},{1,0},{2,3},{3,1},{4,6},{5,4},{6,7},{7,5},{8,10},{9,8},{10,1... | collective-permute-start | bytes 1228808 | tf_op jit(solution)/shard_map/ppermute | solution.py:172
  19.3 1.1 %collective-permute-start = (bf16[64,128]{1,0:T(8,128)(2,1)S(1)}, bf16[64,128]{1,0:T(8,128)(2,1)S(1)}, u32[]{:S(2)}, u32[]{:S(2)}) collective-permute-start(bf16[64,128]{1,0:T(8,128)(2,1)S(1)} %get-tuple-element.24.i0), channel_id=1, source_target_pairs={{0,1},{1,0},{2,3},{3,2},{4,5},{5,4},{6,7},{7,6},{8,9},{9,8},{10,11... | collective-permute-start | bytes 49160 | tf_op jit(solution)/shard_map/ppermute | solution.py:152
  20.4 2.3 %collective-permute-start.1 = (bf16[64,128]{1,0:T(8,128)(2,1)S(1)}, bf16[64,128]{1,0:T(8,128)(2,1)S(1)}, u32[]{:S(2)}, u32[]{:S(2)}) collective-permute-start(bf16[64,128]{1,0:T(8,128)(2,1)S(1)} %get-tuple-element.24.i0), channel_id=1, source_target_pairs={{0,3},{1,2},{2,1},{3,0},{4,7},{5,6},{6,5},{7,4},{8,11},{9,10},{10,... | collective-permute-start | bytes 49160 | tf_op jit(solution)/shard_map/ppermute | solution.py:164
  22.6 0.6 collective-permute-start.2
  23.2 0.0 copy-start
  23.2 4.7 %copy-done = bf16[3200,2048]{1,0:T(8,128)(2,1)S(1)} copy-done((bf16[3200,2048]{1,0:T(8,128)(2,1)S(1)}, bf16[3200,2048]{1,0:T(8,128)(2,1)}, u32[]{:S(2)}) %copy-start) | copy-done | bytes 13107224
  27.9 0.0 copy-start.1
  27.9 0.0 copy-start.3
  27.9 0.0 copy-start.8
  27.9 0.0 collective-permute-done.5.ends
  28.0 0.0 copy-done.5
  28.0 0.0 copy-done.6
  28.0 0.7 %norm.1.rows = bf16[192,3200]{1,0:T(8,128)(2,1)S(1)} custom-call(bf16[64,3200]{1,0:T(8,128)(2,1)S(1)} %copy-done.5, bf16[64,3200]{1,0:T(8,128)(2,1)S(1)} %collective-permute-done.4.outer, bf16[64,3200]{1,0:T(8,128)(2,1)S(1)} %collective-permute-done.3.inner, bf16[64,3200]{1,0:T(8,128)(2,1)S(1)} %collective-permute-done.5.ends, f32[3200]{0:T(1024)S(1)} %copy-done.6), custom_call_target="tpu_custom_call" | custom-call | bytes 13107200 | tf_op jit(solution)/shard_map/norm/pallas_call | solution.py:228
  28.7 6.5 %collective-permute-done.i1 = bf16[64,128]{1,0:T(8,128)(2,1)S(1)} collective-permute-done((bf16[64,128]{1,0:T(8,128)(2,1)S(1)}, bf16[64,128]{1,0:T(8,128)(2,1)S(1)}, u32[]{:S(2)}, u32[]{:S(2)}) %collective-permute-start) | collective-permute-done | bytes 16416 | tf_op jit(solution)/shard_map/ppermute | solution.py:152
  35.1 0.4 collective-permute-done.1.i2
  35.6 0.5 collective-permute-done.2.i3
  36.0 0.0 collective-permute-done.6.last
  36.0 0.0 copy-done.7
  36.0 0.0 copy-done.1
  36.0 5.2 %project.1 = (bf16[32,2048]{1,0:T(8,128)(2,1)S(1)}, bf16[32,2048]{1,0:T(8,128)(2,1)S(1)}, bf16[32,2048]{1,0:T(8,128)(2,1)S(1)}, bf16[32,2048]{1,0:T(8,128)(2,1)S...) custom-call(bf16[64,128]{1,0:T(8,128)(2,1)S(1)} %get-tuple-element.2, ...), custom_call_target="tpu_custom_call" | custom-call | flops 3355443200 | bytes 13107200 | tf_op jit(solution)/shard_map/project/pallas_call | solution.py:237
  41.2 1.5 %collective-permute-start.10 = (bf16[32,2048]{1,0:T(8,128)(2,1)S(1)}, bf16[32,2048]{1,0:T(8,128)(2,1)S(1)}, u32[]{:S(2)}, u32[]{:S(2)}) collective-permute-start(bf16[32,2048]{1,0:T(8,128)(2,1)S(1)} %get-tuple-element.39), channel_id=1, source_target_pairs={{0,16},{4,20},{8,24},{12,28},{16,0},{20,4},{24,8},{28,12},{1,17},{... | collective-permute-start | bytes 393224 | tf_op jit(solution)/shard_map/ppermute | solution.py:179
  42.8 0.0 collective-permute-start.11
  42.8 5.0 %all-to-all-start = ((f32[32,8,128]{2,1,0:T(8,128)}), f32[32,8,128]{2,1,0:T(8,128)S(1)}, u32[]{:S(2)}, u32[]{:S(2)}) async-start(f32[32,8,128]{2,1,0:T(8,128)} %bitcast.1), calls=%async_computation | async-start | bytes 262144 | tf_op jit(solution)/shard_map/all_to_all | solution.py:250
  47.7 2.7 %collective-permute-start.12 = (bf16[32,2048]{1,0:T(8,128)(2,1)S(1)}, bf16[32,2048]{1,0:T(8,128)(2,1)S(1)}, u32[]{:S(2)}, u32[]{:S(2)}) collective-permute-start(bf16[32,2048]{1,0:T(8,128)(2,1)S(1)} %get-tuple-element.41), channel_id=1, source_target_pairs={{0,24},{4,28},{8,16},{12,20},{16,8},{20,12},{24,0},{28,4},{1,25},{... | collective-permute-start | bytes 393224 | tf_op jit(solution)/shard_map/ppermute | solution.py:179
  50.5 0.0 collective-permute-start.13
  50.5 0.4 collective-permute-start.7
  50.8 0.0 collective-permute-done.10.rest_4_
  50.8 1.8 %collective-permute-start.8 = (bf16[32,2048]{1,0:T(8,128)(2,1)S(1)}, bf16[32,2048]{1,0:T(8,128)(2,1)S(1)}, u32[]{:S(2)}, u32[]{:S(2)}) collective-permute-start(bf16[32,2048]{1,0:T(8,128)(2,1)S(1)} %get-tuple-element.37), channel_id=1, source_target_pairs={{0,8},{4,12},{8,0},{12,4},{16,24},{20,28},{24,16},{28,20},{1,9},{5... | collective-permute-start | bytes 393224 | tf_op jit(solution)/shard_map/ppermute | solution.py:179
  52.6 0.0 collective-permute-done.11.rest_5_
  52.6 0.0 collective-permute-start.9
  52.6 3.5 %collective-permute-done.12.rest_6_ = bf16[32,2048]{1,0:T(8,128)(2,1)S(1)} collective-permute-done((bf16[32,2048]{1,0:T(8,128)(2,1)S(1)}, bf16[32,2048]{1,0:T(8,128)(2,1)S(1)}, u32[]{:S(2)}, u32[]{:S(2)}) %collective-permute-start.12) | collective-permute-done | bytes 131104 | tf_op jit(solution)/shard_map/ppermute | solution.py:179
  56.1 1.9 %collective-permute-done.13.rest_7_ = bf16[32,2048]{1,0:T(8,128)(2,1)S(1)} collective-permute-done((bf16[32,2048]{1,0:T(8,128)(2,1)S(1)}, bf16[32,2048]{1,0:T(8,128)(2,1)S(1)}, u32[]{:S(2)}, u32[]{:S(2)}) %collective-permute-start.13) | collective-permute-done | bytes 131104 | tf_op jit(solution)/shard_map/ppermute | solution.py:179
  58.0 0.0 collective-permute-done.7.rest_1_
  58.0 3.6 %collective-permute-done.8.rest_2_ = bf16[32,2048]{1,0:T(8,128)(2,1)S(1)} collective-permute-done((bf16[32,2048]{1,0:T(8,128)(2,1)S(1)}, bf16[32,2048]{1,0:T(8,128)(2,1)S(1)}, u32[]{:S(2)}, u32[]{:S(2)}) %collective-permute-start.8) | collective-permute-done | bytes 131104 | tf_op jit(solution)/shard_map/ppermute | solution.py:179
  61.6 1.8 %collective-permute-done.9.rest_3_ = bf16[32,2048]{1,0:T(8,128)(2,1)S(1)} collective-permute-done((bf16[32,2048]{1,0:T(8,128)(2,1)S(1)}, bf16[32,2048]{1,0:T(8,128)(2,1)S(1)}, u32[]{:S(2)}, u32[]{:S(2)}) %collective-permute-start.9) | collective-permute-done | bytes 131104 | tf_op jit(solution)/shard_map/ppermute | solution.py:179
  63.4 0.0 all-to-all-done
  63.4 0.0 copy-done.3
  63.4 0.0 copy-done.8
  63.4 1.8 %place.1 = bf16[256,2048]{1,0:T(8,128)(2,1)} custom-call(f32[256,128]{1,0:T(8,128)S(1)} %bitcast.4, f32[1,2048]{1,0:T(1,128)S(1)} %bitcast.6, bf16[256,2048]{1,0:T(8,128)(2,1)S(1)} %copy-done.3, bf16[32,2048]{1,0:T(8,128)(2,1)S(1)} %get-tuple-element.35.rest_0_, bf16[32,2048]{1,0:T(8,128)(2,1)S(1)} %collective-permute-done.7.rest_1_, ...), custom_call_target="tpu_custom_call" | custom-call | tf_op jit(solution)/shard_map/place/pallas_call | solution.py:252
  (1 shorter events, 0.0 us)
Async XLA Ops:
  0.0 13.9 %collective-permute-start.3 = (bf16[64,3200]{1,0:T(8,128)(2,1)}, bf16[64,3200]{1,0:T(8,128)(2,1)S(1)}, u32[]{:S(2)}, u32[]{:S(2)}) collective-permute-start(bf16[64,3200]{1,0:T(8,128)(2,1)} %own.2), channel_id=1, source_target_pairs={{1,2},{2,1},{0,0},{3,3},{5,6},{6,5},{4,4},{7,7},{9,10},{10,9},{8,8... | collective-permute-start | bytes 1228808 | tf_op jit(solution)/shard_map/ppermute | solution.py:156
  1.7 15.1 %collective-permute-start.4 = (bf16[64,3200]{1,0:T(8,128)(2,1)}, bf16[64,3200]{1,0:T(8,128)(2,1)S(1)}, u32[]{:S(2)}, u32[]{:S(2)}) collective-permute-start(bf16[64,3200]{1,0:T(8,128)(2,1)} %own.2), channel_id=1, source_target_pairs={{0,1},{1,0},{2,3},{3,2},{4,5},{5,4},{6,7},{7,6},{8,9},{9,8},{10,11... | collective-permute-start | bytes 1228808 | tf_op jit(solution)/shard_map/ppermute | solution.py:152
  7.2 1.2 %copy-start.2 = (bf16[256,2048]{1,0:T(8,128)(2,1)S(1)}, bf16[256,2048]{1,0:T(8,128)(2,1)}, u32[]{:S(2)}) copy-start(bf16[256,2048]{1,0:T(8,128)(2,1)} %text.3) | copy-start | bytes 3145732
  8.5 0.7 %copy-start.9 = (s32[4]{0:T(128)S(1)}, s32[4]{0:T(128)}, u32[]{:S(2)}) copy-start(s32[4]{0:T(128)} %owners.1) | copy-start | bytes 52
  9.1 0.7 %copy-start.10 = (s32[4]{0:T(128)S(1)}, s32[4]{0:T(128)}, u32[]{:S(2)}) copy-start(s32[4]{0:T(128)} %offsets.1) | copy-start | bytes 52
  9.8 18.2 %copy-start.5 = (bf16[64,3200]{1,0:T(8,128)(2,1)S(1)}, bf16[64,3200]{1,0:T(8,128)(2,1)}, u32[]{:S(2)}) copy-start(bf16[64,3200]{1,0:T(8,128)(2,1)} %own.2) | copy-start | bytes 1228804
  9.8 18.2 %copy-start.6 = (f32[3200]{0:T(1024)S(1)}, f32[3200]{0:T(1024)}, u32[]{:S(2)}) copy-start(f32[3200]{0:T(1024)} %gain.3) | copy-start | bytes 38404
  9.8 26.3 %copy-start.7 = (f32[2048]{0:T(1024)S(1)}, f32[2048]{0:T(1024)}, u32[]{:S(2)}) copy-start(f32[2048]{0:T(1024)} %param.12) | copy-start | bytes 24580
  10.6 17.4 %collective-permute-start.5 = (bf16[64,3200]{1,0:T(8,128)(2,1)}, bf16[64,3200]{1,0:T(8,128)(2,1)S(1)}, u32[]{:S(2)}, u32[]{:S(2)}) collective-permute-start(bf16[64,3200]{1,0:T(8,128)(2,1)} %own.2), channel_id=1, source_target_pairs={{0,3},{3,0},{1,1},{2,2},{4,7},{7,4},{5,5},{6,6},{8,11},{11,8},{9,9... | collective-permute-start | bytes 1228808 | tf_op jit(solution)/shard_map/ppermute | solution.py:160
  16.8 1.0 %copy-start.4 = (bf16[64,3200]{1,0:T(8,128)(2,1)S(1)}, bf16[64,3200]{1,0:T(8,128)(2,1)}, u32[]{:S(2)}) copy-start(bf16[64,3200]{1,0:T(8,128)(2,1)} %own.2) | copy-start | bytes 1228804
  17.9 18.2 %collective-permute-start.6 = (bf16[64,3200]{1,0:T(8,128)(2,1)S(1)}, bf16[64,3200]{1,0:T(8,128)(2,1)S(1)}, u32[]{:S(2)}, u32[]{:S(2)}) collective-permute-start(bf16[64,3200]{1,0:T(8,128)(2,1)S(1)} %pass.1), channel_id=1, source_target_pairs={{0,2},{1,0},{2,3},{3,1},{4,6},{5,4},{6,7},{7,5},{8,10},{9,8},{10,1... | collective-permute-start | bytes 1228808 | tf_op jit(solution)/shard_map/ppermute | solution.py:172
  19.3 15.8 %collective-permute-start = (bf16[64,128]{1,0:T(8,128)(2,1)S(1)}, bf16[64,128]{1,0:T(8,128)(2,1)S(1)}, u32[]{:S(2)}, u32[]{:S(2)}) collective-permute-start(bf16[64,128]{1,0:T(8,128)(2,1)S(1)} %get-tuple-element.24.i0), channel_id=1, source_target_pairs={{0,1},{1,0},{2,3},{3,2},{4,5},{5,4},{6,7},{7,6},{8,9},{9,8},{10,11... | collective-permute-start | bytes 49160 | tf_op jit(solution)/shard_map/ppermute | solution.py:152
  20.4 15.2 %collective-permute-start.1 = (bf16[64,128]{1,0:T(8,128)(2,1)S(1)}, bf16[64,128]{1,0:T(8,128)(2,1)S(1)}, u32[]{:S(2)}, u32[]{:S(2)}) collective-permute-start(bf16[64,128]{1,0:T(8,128)(2,1)S(1)} %get-tuple-element.24.i0), channel_id=1, source_target_pairs={{0,3},{1,2},{2,1},{3,0},{4,7},{5,6},{6,5},{7,4},{8,11},{9,10},{10,... | collective-permute-start | bytes 49160 | tf_op jit(solution)/shard_map/ppermute | solution.py:164
  22.6 13.4 %collective-permute-start.2 = (bf16[64,128]{1,0:T(8,128)(2,1)S(1)}, bf16[64,128]{1,0:T(8,128)(2,1)S(1)}, u32[]{:S(2)}, u32[]{:S(2)}) collective-permute-start(bf16[64,128]{1,0:T(8,128)(2,1)S(1)} %get-tuple-element.24.i0), channel_id=1, source_target_pairs={{0,2},{1,3},{2,0},{3,1},{4,6},{5,7},{6,4},{7,5},{8,10},{9,11},{10,... | collective-permute-start | bytes 49160 | tf_op jit(solution)/shard_map/ppermute | solution.py:168
  23.2 4.7 %copy-start = (bf16[3200,2048]{1,0:T(8,128)(2,1)S(1)}, bf16[3200,2048]{1,0:T(8,128)(2,1)}, u32[]{:S(2)}) copy-start(bf16[3200,2048]{1,0:T(8,128)(2,1)} %weight.3) | copy-start | bytes 39321604
  27.9 8.1 %copy-start.1 = (bf16[3200,2048]{1,0:T(8,128)(2,1)S(1)}, bf16[3200,2048]{1,0:T(8,128)(2,1)}, u32[]{:S(2)}) copy-start(bf16[3200,2048]{1,0:T(8,128)(2,1)} %weight.3) | copy-start | bytes 39321604
  27.9 35.5 %copy-start.3 = (bf16[256,2048]{1,0:T(8,128)(2,1)S(1)}, bf16[256,2048]{1,0:T(8,128)(2,1)}, u32[]{:S(2)}) copy-start(bf16[256,2048]{1,0:T(8,128)(2,1)} %text.3) | copy-start | bytes 3145732
  27.9 35.5 %copy-start.8 = (f32[2048]{0:T(1024)S(1)}, f32[2048]{0:T(1024)}, u32[]{:S(2)}) copy-start(f32[2048]{0:T(1024)} %param.14) | copy-start | bytes 24580
  41.2 9.6 %collective-permute-start.10 = (bf16[32,2048]{1,0:T(8,128)(2,1)S(1)}, bf16[32,2048]{1,0:T(8,128)(2,1)S(1)}, u32[]{:S(2)}, u32[]{:S(2)}) collective-permute-start(bf16[32,2048]{1,0:T(8,128)(2,1)S(1)} %get-tuple-element.39), channel_id=1, source_target_pairs={{0,16},{4,20},{8,24},{12,28},{16,0},{20,4},{24,8},{28,12},{1,17},{... | collective-permute-start | bytes 393224 | tf_op jit(solution)/shard_map/ppermute | solution.py:179
  42.8 9.8 %collective-permute-start.11 = (bf16[32,2048]{1,0:T(8,128)(2,1)S(1)}, bf16[32,2048]{1,0:T(8,128)(2,1)S(1)}, u32[]{:S(2)}, u32[]{:S(2)}) collective-permute-start(bf16[32,2048]{1,0:T(8,128)(2,1)S(1)} %get-tuple-element.40), channel_id=1, source_target_pairs={{0,20},{4,16},{8,28},{12,24},{16,4},{20,0},{24,12},{28,8},{1,21},{... | collective-permute-start | bytes 393224 | tf_op jit(solution)/shard_map/ppermute | solution.py:179
  42.8 20.6 %all-to-all-start = ((f32[32,8,128]{2,1,0:T(8,128)}), f32[32,8,128]{2,1,0:T(8,128)S(1)}, u32[]{:S(2)}, u32[]{:S(2)}) async-start(f32[32,8,128]{2,1,0:T(8,128)} %bitcast.1), calls=%async_computation | async-start | bytes 262144 | tf_op jit(solution)/shard_map/all_to_all | solution.py:250
  47.7 8.4 %collective-permute-start.12 = (bf16[32,2048]{1,0:T(8,128)(2,1)S(1)}, bf16[32,2048]{1,0:T(8,128)(2,1)S(1)}, u32[]{:S(2)}, u32[]{:S(2)}) collective-permute-start(bf16[32,2048]{1,0:T(8,128)(2,1)S(1)} %get-tuple-element.41), channel_id=1, source_target_pairs={{0,24},{4,28},{8,16},{12,20},{16,8},{20,12},{24,0},{28,4},{1,25},{... | collective-permute-start | bytes 393224 | tf_op jit(solution)/shard_map/ppermute | solution.py:179
  50.5 7.6 %collective-permute-start.13 = (bf16[32,2048]{1,0:T(8,128)(2,1)S(1)}, bf16[32,2048]{1,0:T(8,128)(2,1)S(1)}, u32[]{:S(2)}, u32[]{:S(2)}) collective-permute-start(bf16[32,2048]{1,0:T(8,128)(2,1)S(1)} %get-tuple-element.42), channel_id=1, source_target_pairs={{0,28},{4,24},{8,20},{12,16},{16,12},{20,8},{24,4},{28,0},{1,29},{... | collective-permute-start | bytes 393224 | tf_op jit(solution)/shard_map/ppermute | solution.py:179
  50.5 7.6 %collective-permute-start.7 = (bf16[32,2048]{1,0:T(8,128)(2,1)S(1)}, bf16[32,2048]{1,0:T(8,128)(2,1)S(1)}, u32[]{:S(2)}, u32[]{:S(2)}) collective-permute-start(bf16[32,2048]{1,0:T(8,128)(2,1)S(1)} %get-tuple-element.36), channel_id=1, source_target_pairs={{0,4},{4,0},{8,12},{12,8},{16,20},{20,16},{24,28},{28,24},{1,5},{5... | collective-permute-start | bytes 393224 | tf_op jit(solution)/shard_map/ppermute | solution.py:179
  50.8 10.8 %collective-permute-start.8 = (bf16[32,2048]{1,0:T(8,128)(2,1)S(1)}, bf16[32,2048]{1,0:T(8,128)(2,1)S(1)}, u32[]{:S(2)}, u32[]{:S(2)}) collective-permute-start(bf16[32,2048]{1,0:T(8,128)(2,1)S(1)} %get-tuple-element.37), channel_id=1, source_target_pairs={{0,8},{4,12},{8,0},{12,4},{16,24},{20,28},{24,16},{28,20},{1,9},{5... | collective-permute-start | bytes 393224 | tf_op jit(solution)/shard_map/ppermute | solution.py:179
  52.6 10.8 %collective-permute-start.9 = (bf16[32,2048]{1,0:T(8,128)(2,1)S(1)}, bf16[32,2048]{1,0:T(8,128)(2,1)S(1)}, u32[]{:S(2)}, u32[]{:S(2)}) collective-permute-start(bf16[32,2048]{1,0:T(8,128)(2,1)S(1)} %get-tuple-element.38), channel_id=1, source_target_pairs={{0,12},{4,8},{8,4},{12,0},{16,28},{20,24},{24,20},{28,16},{1,13},{... | collective-permute-start | bytes 393224 | tf_op jit(solution)/shard_map/ppermute | solution.py:179

commit v3 on v2

--- a/solution.py
+++ b/solution.py
@@ -22,7 +22,7 @@
     return lax.broadcasted_iota(jnp.int32, TILE, 1)
 
 
-def tables_kernel(slots, size, text, owners, offsets, counts, squares, info):
+def tables_kernel(slots, size, text, vis, owners, offsets, counts, squares, info, own):
     lane = lanes()
     tile = jnp.zeros(TILE, F32)
     for c in range(text.shape[0] // 16):
@@ -37,6 +37,12 @@
         code = jnp.where(i < counts[0], offsets[i] // size + 1, 0)
         known = jnp.where(lane == 0, owners[i], jnp.where(lane == 1, row * slots + i, jnp.where(lane == 2, code, 0)))
         info[i * size : (i + 1) * size, :] = known.astype(F32).astype(BF16)
+    own[...] = vis[...]
+
+
+def pass_kernel(own, inner, sent):
+    row = lax.axis_index("dp")
+    sent[...] = jnp.where(jnp.logical_or(row == 1, row == 2), inner[...], own[...])
 
 
 def hold_kernel(weight, tile, out):
@@ -50,23 +56,23 @@
     return (x * scale * gain).astype(BF16)
 
 
-def norm_kernel(own, outer, inner, ends, gain, rows):
+def early_kernel(own, outer, inner, ends, gain, weight, bias, y, x):
     row = lax.axis_index("dp")
     middle = jnp.logical_or(row == 1, row == 2)
-    g = gain[...].reshape(1, own.shape[1])
+    depth, columns = weight.shape
     count = own.shape[0]
-    rows[0:count] = normed(own[...], g)
-    rows[count : 2 * count] = normed(outer[...], g)
-    rows[2 * count : 3 * count] = normed(jnp.where(middle, inner[...], ends[...]), g)
-
-
-def pass_kernel(own, inner, sent):
-    row = lax.axis_index("dp")
-    sent[...] = jnp.where(jnp.logical_or(row == 1, row == 2), inner[...], own[...])
-
-
-def project_kernel(groups, cap, size, i0, i1, i2, i3, rows, last, gain, weight, bias, text_squares, *rest):
-    *outs, tiles, x = rest
+    g = gain[...].reshape(1, depth)
+    x[0:count] = normed(own[...], g)
+    x[count : 2 * count] = normed(outer[...], g)
+    x[2 * count : 3 * count] = normed(jnp.where(middle, inner[...], ends[...]), g)
+    block = 256
+    for n in range(columns // block):
+        at = slice(n * block, (n + 1) * block)
+        y[:, at] = (jnp.dot(x[...], weight[:, at], preferred_element_type=F32) + bias[:, at]).astype(BF16)
+
+
+def project_kernel(groups, cap, size, i0, i1, i2, i3, last, gain, weight, bias, early, text_squares, *rest):
+    *parts, tiles, y, z, codes = rest
     me = lax.axis_index("grp")
     depth, columns = weight.shape
     known = jnp.concatenate([i0[...], i1[...], i2[...], i3[...]], axis=0)
@@ -80,72 +86,116 @@
     place = owner.astype(jnp.int32) ^ me
     position = lax.broadcasted_iota(jnp.int32, (1, total), 1) % size
     seat = (place * cap + rank) * size + position
-    order = (lax.broadcasted_iota(jnp.int32, (total, total), 0) == seat).astype(BF16)
-    codes = jnp.dot(order, known, preferred_element_type=F32)[:, 2:3]
-    every = jnp.concatenate([rows[...], normed(last[...], gain[...].reshape(1, depth))], axis=0)
-    x[...] = jnp.dot(order, every, preferred_element_type=F32).astype(BF16)
+    first = position == 0
+    image = lax.broadcasted_iota(jnp.int32, (1, total), 1) // size
+    seats = [
+        pl.multiple_of(jnp.sum(jnp.where(jnp.logical_and(first, image == i), seat, 0)), size)
+        for i in range(total // size)
+    ]
+    x = normed(last[...], gain[...].reshape(1, depth))
+    count = last.shape[0]
+    for i in range((total - count) // size):
+        y[pl.ds(seats[i], size), :] = early[i * size : (i + 1) * size]
     block = 256
-    partial = jnp.zeros((total, 128), F32)
     for n in range(columns // block):
         at = slice(n * block, (n + 1) * block)
-        y = jnp.dot(x[...], weight[:, at], preferred_element_type=F32) + bias[:, at]
-        y = y.astype(BF16)
-        for k in range(groups):
-            outs[k][:, at] = y[k * cap * size : (k + 1) * cap * size]
-        wide = y.astype(F32)
-        wide = wide * wide
-        for c in range(block // 128):
-            partial = partial + wide[:, c * 128 : (c + 1) * 128]
+        z[:, at] = (jnp.dot(x, weight[:, at], preferred_element_type=F32) + bias[:, at]).astype(BF16)
+    for i in range(count // size):
+        y[pl.ds(seats[(total - count) // size + i], size), :] = z[i * size : (i + 1) * size]
+    for i in range(total // size):
+        codes[pl.ds(seats[i], size), :] = down[i * size : (i + 1) * size]
+    rows = total // len(parts)
+    for m, part in enumerate(parts):
+        part[...] = y[m * rows : (m + 1) * rows]
     lane = lanes()
-    sums = jnp.sum(partial, axis=1, keepdims=True)
     copies = tiles.shape[0] // (8 * groups)
     for k in range(groups):
         tile = jnp.zeros(TILE, F32)
         for r in range(cap):
             at = (k * cap + r) * size
-            tile = jnp.where(lane == 2 * r, sums[at : at + 8], tile)
-            tile = jnp.where(lane == 2 * r + 1, sums[at + 8 : at + 16], tile)
-            tile = jnp.where(lane == 2 * cap + r, codes[at : at + 8], tile)
+            wide = y[at : at + size, :].astype(F32)
+            sums = jnp.sum(wide * wide, axis=1, keepdims=True)
+            tile = jnp.where(lane == 2 * r, sums[:8], jnp.where(lane == 2 * r + 1, sums[8:], tile))
+            tile = jnp.where(lane == 2 * cap + r, codes[at : at + 8, 2:3], tile)
         if k == 0:
             tile = jnp.where(lane < 3 * cap, tile, pltpu.roll(text_squares[...], 3 * cap, 1))
         for q in range(copies):
             tiles[pl.ds(pl.multiple_of(((me ^ k) * copies + q) * 8, 8), 8), :] = tile
 
 
-def place_kernel(groups, dp, cap, size, width, squares, gain, text, *rest):
-    arrived, (out, rows) = rest[:groups], rest[groups:]
+def scale_kernel(groups, dp, cap, width, squares, scales):
     me = lax.axis_index("grp")
-    seq_len = text.shape[0]
-    total = groups * cap * size
-    g = gain[...]
-    codes = []
+    lane = lanes()
+    is_code = jnp.logical_and(lane >= 2 * cap, lane < 3 * cap)
     for k in range(groups):
         base = (me ^ k) * (dp * 8)
         tile = squares[pl.ds(pl.multiple_of(base, 8), 8), :]
         code = tile
         for d in range(1, dp):
             tile = tile + squares[pl.ds(pl.multiple_of(base + d * 8, 8), 8), :]
-        scale = lax.rsqrt(tile / width + EPS_OUT)
-        if k == 0:
-            own = scale
-        for r in range(cap):
-            inverse = jnp.concatenate([scale[:, 2 * r : 2 * r + 1], scale[:, 2 * r + 1 : 2 * r + 2]], axis=0)
-            part = slice(r * size, (r + 1) * size)
-            at = (k * cap + r) * size
-            rows[at : at + size, :] = (arrived[k][part, :].astype(F32) * inverse * g).astype(BF16)
-            codes += [jnp.broadcast_to(code[:, 2 * cap + r : 2 * cap + r + 1], TILE)] * 2
+        scales[k * 8 : (k + 1) * 8, :] = jnp.where(is_code, code, lax.rsqrt(tile / width + EPS_OUT))
+
+
+def pack_kernel(*refs):
+    *parts, out = refs
+    rows = parts[0].shape[0] // 2
+    for n, part in enumerate(parts):
+        out[n * rows : (n + 1) * rows, :] = part[rows:, :]
+
+
+def scaled(cap, size, k, rows, scales, gain):
+    scale = scales[k * 8 : (k + 1) * 8, :]
+    out = []
+    for r in range(cap):
+        inverse = jnp.concatenate([scale[:, 2 * r : 2 * r + 1], scale[:, 2 * r + 1 : 2 * r + 2]], axis=0)
+        out.append((rows[r * size : (r + 1) * size, :].astype(F32) * inverse * gain).astype(BF16))
+    return out
+
+
+def moves(seq_len, cap, size, senders, scales):
+    lane = 2 * cap
+    codes = [
+        jnp.broadcast_to(scales[k * 8 : (k + 1) * 8, lane + r : lane + r + 1], TILE)
+        for k in senders
+        for r in range(cap)
+        for _ in range(size // 8)
+    ]
     code = jnp.concatenate(codes, axis=0).T[0:1, :].astype(jnp.int32)
-    position = lax.broadcasted_iota(jnp.int32, (1, total), 1) % size
+    position = lax.broadcasted_iota(jnp.int32, code.shape, 1) % size
     target = jnp.where(code > 0, (code - 1) * size + position, -1)
-    order = (lax.broadcasted_iota(jnp.int32, (seq_len, total), 0) == target).astype(F32)
-    covered = jnp.sum(order, axis=1, keepdims=True)
+    return (lax.broadcasted_iota(jnp.int32, (seq_len, code.shape[1]), 0) == target).astype(F32)
+
+
+def base_kernel(groups, cap, size, scales, gain, text, *rest):
+    *even, base, order_odd, rows = rest
+    seq_len = text.shape[0]
+    g = gain[...]
+    order = moves(seq_len, cap, size, range(0, groups, 2), scales)
+    odd = moves(seq_len, cap, size, range(1, groups, 2), scales)
+    order_odd[...] = odd.astype(BF16)
+    covered = jnp.sum(order + odd, axis=1, keepdims=True)
+    for n, part in enumerate(even):
+        for r, x in enumerate(scaled(cap, size, 2 * n, part, scales, g)):
+            at = (n * cap + r) * size
+            rows[at : at + size, :] = x
     moved = jnp.dot(order.astype(BF16), rows[...], preferred_element_type=F32)
+    own = scales[0:8, :]
     for c in range(seq_len // 16):
         at = 3 * cap + 2 * c
         inverse = jnp.concatenate([own[:, at : at + 1], own[:, at + 1 : at + 2]], axis=0)
         part = slice(c * 16, (c + 1) * 16)
         x = text[part, :].astype(F32) * inverse * g
-        out[part, :] = jnp.where(covered[part] > 0, moved[part], x).astype(BF16)
+        base[part, :] = jnp.where(covered[part] > 0, moved[part], x).astype(BF16)
+
+
+def place_kernel(groups, cap, size, scales, gain, odd, base, order, out, rows):
+    g = gain[...]
+    for n, k in enumerate(range(1, groups, 2)):
+        at = n * cap * size
+        for r, x in enumerate(scaled(cap, size, k, odd[at : at + cap * size], scales, g)):
+            rows[at + r * size : at + (r + 1) * size, :] = x
+    moved = jnp.dot(order[...], rows[...], preferred_element_type=F32)
+    out[...] = (base[...].astype(F32) + moved).astype(BF16)
 
 
 def outer(x):
@@ -172,12 +222,8 @@
     return lax.ppermute(x, "dp", [(0, 2), (1, 0), (2, 3), (3, 1)])
 
 
-def route(parts):
-    groups = len(parts)
-    near = [k for k in range(1, groups) if k & (k - 1) == 0]
-    order = near[:0:-1] + [k for k in range(groups - 1, 0, -1) if k not in near] + near[:1]
-    arrived = {k: lax.ppermute(parts[k], "grp", [(i, i ^ k) for i in range(groups)]) for k in order}
-    return [parts[0]] + [arrived[k] for k in range(1, groups)]
+def across(x, k):
+    return lax.ppermute(x, "grp", [(i, i ^ k) for i in range(lax.axis_size("grp"))])
 
 
 def fast(vis, vis_gain, weight, bias, text, out_gain, counts, owners, offsets):
@@ -190,19 +236,30 @@
     depth = vis.shape[1]
     small = pltpu.CompilerParams(vmem_limit_bytes=LIMIT)
     count = slots * size
-
-    x_outer, x_inner = outer(vis), inner(vis)
-    text_squares, info = pl.pallas_call(
+    tile = jax.ShapeDtypeStruct(TILE, F32)
+    bias = bias[None, :]
+
+    x_inner, x_outer = inner(vis), outer(vis)
+    text_squares, info, own = pl.pallas_call(
         functools.partial(tables_kernel, slots, size),
-        in_specs=[VMEM, SMEM, SMEM, SMEM],
-        out_specs=[VMEM] * 2,
-        out_shape=[jax.ShapeDtypeStruct(TILE, F32), jax.ShapeDtypeStruct((count, 128), BF16)],
+        in_specs=[VMEM, VMEM, SMEM, SMEM, SMEM],
+        out_specs=[VMEM] * 3,
+        out_shape=[tile, jax.ShapeDtypeStruct((count, 128), BF16), jax.ShapeDtypeStruct(vis.shape, BF16)],
         compiler_params=small,
         name="tables",
-    )(text, owners, offsets, counts)
-    late, text_squares = lax.optimization_barrier((vis, text_squares))
-    x_ends = ends(late)
-    x_inner, x_outer, late = lax.optimization_barrier((x_inner, x_outer, late))
+    )(text, vis, owners, offsets, counts)
+    x_ends = ends(own)
+    weight = pltpu.with_memory_space_constraint(weight, pltpu.VMEM)
+    text_squares = pl.pallas_call(
+        hold_kernel,
+        in_specs=[ANY, VMEM],
+        out_specs=VMEM,
+        out_shape=tile,
+        compiler_params=small,
+        cost_estimate=pl.CostEstimate(flops=0, bytes_accessed=2 * weight.size, transcendentals=0),
+        name="hold",
+    )(weight, text_squares)
+    x_inner, text_squares = lax.optimization_barrier((x_inner, text_squares))
     sent = pl.pallas_call(
         pass_kernel,
         in_specs=[VMEM] * 2,
@@ -210,54 +267,79 @@
         out_shape=jax.ShapeDtypeStruct(vis.shape, BF16),
         compiler_params=small,
         name="pass",
-    )(late, x_inner)
+    )(own, x_inner)
+    sent, x_outer = lax.optimization_barrier((sent, x_outer))
     x_far = far(sent)
-    sent, text_squares = lax.optimization_barrier((sent, text_squares))
-    weight = pltpu.with_memory_space_constraint(weight, pltpu.VMEM)
-    text_squares = pl.pallas_call(
-        hold_kernel,
-        in_specs=[ANY, VMEM],
+    known = (info, outer(info), mirror(info), second(info))
+    cost = pl.CostEstimate(
+        flops=2 * 3 * count * depth * columns, bytes_accessed=2 * weight.size, transcendentals=0
+    )
+    early = pl.pallas_call(
+        early_kernel,
+        in_specs=[VMEM] * 7,
         out_specs=VMEM,
-        out_shape=jax.ShapeDtypeStruct(TILE, F32),
-        compiler_params=small,
-        cost_estimate=pl.CostEstimate(flops=0, bytes_accessed=2 * weight.size, transcendentals=0),
-        name="hold",
-    )(weight, text_squares)
-    x_outer, text_squares = lax.optimization_barrier((x_outer, text_squares))
-    known = (info, outer(info), mirror(info), second(info))
-    rows = pl.pallas_call(
-        norm_kernel,
-        in_specs=[VMEM] * 5,
-        out_specs=VMEM,
-        out_shape=jax.ShapeDtypeStruct((3 * count, depth), BF16),
-        compiler_params=small,
-        cost_estimate=pl.CostEstimate(flops=0, bytes_accessed=2 * weight.size, transcendentals=0),
-        name="norm",
-    )(vis, x_outer, x_inner, x_ends, vis_gain)
+        out_shape=jax.ShapeDtypeStruct((3 * count, columns), BF16),
+        scratch_shapes=[pltpu.VMEM((3 * count, depth), BF16)],
+        compiler_params=small,
+        cost_estimate=cost,
+        name="early",
+    )(own, x_outer, x_inner, x_ends, vis_gain, weight, bias)
+    pairs = groups // 2
     *parts, squares = pl.pallas_call(
         functools.partial(project_kernel, groups, cap, size),
         in_specs=[VMEM] * 10,
-        out_specs=[VMEM] * (groups + 1),
-        out_shape=[jax.ShapeDtypeStruct((cap * size, columns), BF16)] * groups
+        out_specs=[VMEM] * (pairs + 1),
+        out_shape=[jax.ShapeDtypeStruct((2 * cap * size, columns), BF16)] * pairs
         + [jax.ShapeDtypeStruct((devices * 8, 128), F32)],
-        scratch_shapes=[pltpu.VMEM((dp * slots * size, depth), BF16)],
-        compiler_params=small,
-        cost_estimate=pl.CostEstimate(
-            flops=2 * dp * slots * size * depth * columns, bytes_accessed=2 * depth * columns, transcendentals=0
-        ),
+        scratch_shapes=[
+            pltpu.VMEM((dp * count, columns), BF16),
+            pltpu.VMEM((count, columns), BF16),
+            pltpu.VMEM((dp * count, 128), F32),
+        ],
+        compiler_params=small,
+        cost_estimate=cost,
         name="project",
-    )(*known, rows, x_far, vis_gain, weight, bias[None, :], text_squares)
+    )(*known, x_far, vis_gain, weight, bias, early, text_squares)
     squares = lax.all_to_all(squares, ("grp", "dp"), 0, 0, tiled=True)
-    arrived = route(parts)
+    scales = pl.pallas_call(
+        functools.partial(scale_kernel, groups, dp, cap, columns * dp),
+        in_specs=[VMEM],
+        out_specs=VMEM,
+        out_shape=jax.ShapeDtypeStruct((groups * 8, 128), F32),
+        compiler_params=small,
+        cost_estimate=pl.CostEstimate(flops=0, bytes_accessed=4 * weight.size, transcendentals=0),
+        name="scale",
+    )(squares)
+    even = [parts[0]] + [across(parts[j], 2 * j) for j in range(1, pairs)]
+    *even, scales = lax.optimization_barrier((*even, scales))
+    arrived = jax.ShapeDtypeStruct((pairs * cap * size, columns), BF16)
+    odd = pl.pallas_call(
+        pack_kernel, in_specs=[VMEM] * pairs, out_specs=VMEM, out_shape=arrived, compiler_params=small, name="pack"
+    )(*even)
+    odd = across(odd, 1)
+    gain = out_gain[None, :]
+    base, order = pl.pallas_call(
+        functools.partial(base_kernel, groups, cap, size),
+        in_specs=[VMEM] * (3 + pairs),
+        out_specs=[VMEM] * 2,
+        out_shape=[
+            jax.ShapeDtypeStruct(text.shape, BF16),
+            jax.ShapeDtypeStruct((seq_len, pairs * cap * size), BF16),
+        ],
+        scratch_shapes=[pltpu.VMEM(arrived.shape, BF16)],
+        compiler_params=small,
+        cost_estimate=pl.CostEstimate(flops=0, bytes_accessed=2 * weight.size, transcendentals=0),
+        name="base",
+    )(scales, gain, text, *even)
     return pl.pallas_call(
-        functools.partial(place_kernel, groups, dp, cap, size, columns * dp),
-        in_specs=[VMEM] * (3 + groups),
+        functools.partial(place_kernel, groups, cap, size),
+        in_specs=[VMEM] * 5,
         out_specs=VMEM,
         out_shape=jax.ShapeDtypeStruct(text.shape, BF16),
-        scratch_shapes=[pltpu.VMEM((groups * cap * size, columns), BF16)],
+        scratch_shapes=[pltpu.VMEM(arrived.shape, BF16)],
         compiler_params=small,
         name="place",
-    )(squares, out_gain[None, :], text, *arrived)
+    )(scales, gain, odd, base, order)
 
 
 def general(

time: 65.6 us -> 59.5 us (0.907)
  blocking collectives: 0 us -> 13 us
  waiting for transfers between devices: 21.1 us -> 9.69 us
  starting transfers between devices: 26.5 us -> 18 us
  Pallas kernels: 8.53 us -> 9.44 us
    all_to_all x0 -> x1, blocking collectives: none -> 13 us  [fast(): squares = lax.all_to_all(squares, ('grp', 'dp'), 0, 0, tiled=True)]
    ppermute x7 -> x4, waiting for transfers between devices: 10.8 us -> 1.08 us  [across(): lax.ppermute(x, 'grp', [(i, i ^ k) for i in range(lax.axis_size('grp'))])]
    ppermute x2, waiting for transfers between devices: 9.39 us -> 4.15 us  [outer(): return lax.ppermute(x, 'dp', [(0, 1), (1, 0), (2, 3), (3, 2)])]
    all_to_all x1 -> x0, starting transfers between devices: 4.95 us -> none  [fast(): squares = lax.all_to_all(squares, ('grp', 'dp'), 0, 0, tiled=True)]
    ppermute x1, waiting for transfers between devices: 0.01 us -> 3.58 us  [ends(): return lax.ppermute(x, 'dp', [(0, 3), (3, 0), (1, 1), (2, 2)])]
    pallas_call x2 -> x5, Pallas kernels: 2.45 us -> 5.67 us  [the longest x1 3.26 us: fast(): pl.pallas_call(early_kernel, in_specs=[VMEM] * 7, out_specs=VMEM, out_sha...]
    ppermute x7 -> x4, starting transfers between devices: 6.4 us -> 3.65 us  [across(): lax.ppermute(x, 'grp', [(i, i ^ k) for i in range(lax.axis_size('grp'))])]
    pallas_call x1, Pallas kernels: 5.2 us -> 2.9 us  [fast(): pl.pallas_call(functools.partial(project_kernel, groups, cap, size), in_s...]
  transfers between devices with their start and end apart: 15 -> 11, of which waited for: 8 -> 5; matrix products, arithmetic and copies ran while one was open for 0% -> 0% of each run, Pallas kernels for 2% -> 8%
where the time goes in v3:
time: 59.5 us; the launch traced here: 59.2 us
  starting transfers between devices  18 us (30%)
  blocking collectives  13 us (22%)
  waiting for transfers between devices  9.69 us (16%)
  Pallas kernels  9.44 us (16%)
  local copies, waits for them, and re-layouts  8.27 us (14%)
  between operations  0.79 us (1%)
    all_to_all x1, blocking collectives, fast(): squares = lax.all_to_all(squares, ('grp', 'dp'), 0, 0, tiled=True)  13 us
    unnamed x20, local copies, waits for them, and re-layouts  8.27 us
    ppermute x2, starting transfers between devices, outer(): return lax.ppermute(x, 'dp', [(0, 1), (1, 0), (2, 3), (3, 2)])  6.93 us
    ppermute x2, waiting for transfers between devices, outer(): return lax.ppermute(x, 'dp', [(0, 1), (1, 0), (2, 3), (3, 2)])  4.15 us
    ppermute x4, starting transfers between devices, across(): lax.ppermute(x, 'grp', [(i, i ^ k) for i in range(lax.axis_size('grp'))])  3.65 us
    ppermute x1, waiting for transfers between devices, ends(): return lax.ppermute(x, 'dp', [(0, 3), (3, 0), (1, 1), (2, 2)])  3.58 us
    pallas_call x1, Pallas kernels, fast(): pl.pallas_call(early_kernel, in_specs=[VMEM] * 7, out_specs=VMEM, out_sha...  3.26 us
    ppermute x1, starting transfers between devices, ends(): return lax.ppermute(x, 'dp', [(0, 3), (3, 0), (1, 1), (2, 2)])  3.24 us
  transfers between devices with their start and end apart: 11, of which 5 were waited for; matrix products, arithmetic and copies ran while one was open for 0% of the time, Pallas kernels for 8%

profile of v3, /device:TPU:0, one launch (start us, length us, event | category | flops | bytes accessed | tf_op | source)
XLA Modules:
  0.0 59.2 jit_solution(14381249763914876914)
XLA Ops:
  0.0 1.6 %collective-permute-start.3 = (bf16[64,3200]{1,0:T(8,128)(2,1)}, bf16[64,3200]{1,0:T(8,128)(2,1)S(1)}, u32[]{:S(2)}, u32[]{:S(2)}) collective-permute-start(bf16[64,3200]{1,0:T(8,128)(2,1)} %vis.1), channel_id=1, source_target_pairs={{1,2},{2,1},{0,0},{3,3},{5,6},{6,5},{4,4},{7,7},{9,10},{10,9},{8,8... | collective-permute-start | bytes 1228808 | tf_op jit(solution)/shard_map/ppermute | solution.py:206
  1.6 4.9 %collective-permute-start.4 = (bf16[64,3200]{1,0:T(8,128)(2,1)}, bf16[64,3200]{1,0:T(8,128)(2,1)S(1)}, u32[]{:S(2)}, u32[]{:S(2)}) collective-permute-start(bf16[64,3200]{1,0:T(8,128)(2,1)} %vis.1), channel_id=1, source_target_pairs={{0,1},{1,0},{2,3},{3,2},{4,5},{5,4},{6,7},{7,6},{8,9},{9,8},{10,11... | collective-permute-start | bytes 1228808 | tf_op jit(solution)/shard_map/ppermute | solution.py:202
  7.2 0.0 copy-start.2
  7.2 1.2 %copy-done.2 = bf16[256,2048]{1,0:T(8,128)(2,1)S(1)} copy-done((bf16[256,2048]{1,0:T(8,128)(2,1)S(1)}, bf16[256,2048]{1,0:T(8,128)(2,1)}, u32[]{:S(2)}) %copy-start.2) | copy-done | bytes 1048600
  8.4 0.0 copy-start.4
  8.5 1.0 %copy-done.4 = bf16[64,3200]{1,0:T(8,128)(2,1)S(1)} copy-done((bf16[64,3200]{1,0:T(8,128)(2,1)S(1)}, bf16[64,3200]{1,0:T(8,128)(2,1)}, u32[]{:S(2)}) %copy-start.4) | copy-done | bytes 409624
  9.5 0.0 copy-start.8
  9.5 0.7 %copy-done.8 = s32[4]{0:T(128)S(1)} copy-done((s32[4]{0:T(128)S(1)}, s32[4]{0:T(128)}, u32[]{:S(2)}) %copy-start.8) | copy-done | bytes 40
  10.1 0.0 copy-start.9
  10.1 0.7 %copy-done.9 = s32[4]{0:T(128)S(1)} copy-done((s32[4]{0:T(128)S(1)}, s32[4]{0:T(128)}, u32[]{:S(2)}) %copy-start.9) | copy-done | bytes 40
  10.8 0.0 copy-start.5
  10.8 0.0 copy-start.6
  10.8 0.8 %tables.1 = (f32[8,128]{1,0:T(8,128)S(1)}, bf16[64,128]{1,0:T(8,128)(2,1)S(1)}, bf16[64,3200]{1,0:T(8,128)(2,1)S(1)}) custom-call(bf16[256,2048]{1,0:T(8,128)(2,1)S(1)} %copy-done.2, bf16[64,3200]{1,0:T(8,128)(2,1)S(1)} %copy-done.4, s32[4]{0:T(128)S(1)} %copy-done.8, s32[4]{0:T(128)S(1)} %copy-done.9, s32[1]{0:T(128)S(6)} %copy.10.counts), custom_call_target="tpu_custom_call" | custom-call | tf_op jit(solution)/shard_map/tables/pallas_call | solution.py:243
  11.6 3.2 %collective-permute-start.6 = (bf16[64,3200]{1,0:T(8,128)(2,1)S(1)}, bf16[64,3200]{1,0:T(8,128)(2,1)S(1)}, u32[]{:S(2)}, u32[]{:S(2)}) collective-permute-start(bf16[64,3200]{1,0:T(8,128)(2,1)S(1)} %get-tuple-element.25.own), channel_id=1, source_target_pairs={{0,3},{3,0},{1,1},{2,2},{4,7},{7,4},{5,5},{6,6},{8,11},{11,8},{9,9... | collective-permute-start | bytes 1228808 | tf_op jit(solution)/shard_map/ppermute | solution.py:210
  14.8 0.0 copy-start
  14.9 4.7 %copy-done = bf16[3200,2048]{1,0:T(8,128)(2,1)S(1)} copy-done((bf16[3200,2048]{1,0:T(8,128)(2,1)S(1)}, bf16[3200,2048]{1,0:T(8,128)(2,1)}, u32[]{:S(2)}) %copy-start) | copy-done | bytes 13107224
  19.6 0.0 copy-start.1
  19.6 0.0 collective-permute-done.3.inner
  19.6 0.0 collective-permute-done.4.outer
  19.6 0.1 collective-permute-start.5
  19.7 2.0 %collective-permute-start = (bf16[64,128]{1,0:T(8,128)(2,1)S(1)}, bf16[64,128]{1,0:T(8,128)(2,1)S(1)}, u32[]{:S(2)}, u32[]{:S(2)}) collective-permute-start(bf16[64,128]{1,0:T(8,128)(2,1)S(1)} %get-tuple-element.24.i0), channel_id=1, source_target_pairs={{0,1},{1,0},{2,3},{3,2},{4,5},{5,4},{6,7},{7,6},{8,9},{9,8},{10,11... | collective-permute-start | bytes 49160 | tf_op jit(solution)/shard_map/ppermute | solution.py:202
  21.7 2.5 %collective-permute-start.1 = (bf16[64,128]{1,0:T(8,128)(2,1)S(1)}, bf16[64,128]{1,0:T(8,128)(2,1)S(1)}, u32[]{:S(2)}, u32[]{:S(2)}) collective-permute-start(bf16[64,128]{1,0:T(8,128)(2,1)S(1)} %get-tuple-element.24.i0), channel_id=1, source_target_pairs={{0,3},{1,2},{2,1},{3,0},{4,7},{5,6},{6,5},{7,4},{8,11},{9,10},{10,... | collective-permute-start | bytes 49160 | tf_op jit(solution)/shard_map/ppermute | solution.py:214
  24.2 0.0 collective-permute-start.2
  24.2 3.6 %collective-permute-done.6.ends = bf16[64,3200]{1,0:T(8,128)(2,1)S(1)} collective-permute-done((bf16[64,3200]{1,0:T(8,128)(2,1)S(1)}, bf16[64,3200]{1,0:T(8,128)(2,1)S(1)}, u32[]{:S(2)}, u32[]{:S(2)}) %collective-permute-start.6) | collective-permute-done | bytes 409632 | tf_op jit(solution)/shard_map/ppermute | solution.py:210
  27.8 0.0 copy-done.5
  27.8 0.0 copy-done.6
  27.8 0.0 copy-done.1
  27.8 0.0 copy-start.3
  27.8 0.0 copy-start.7
  27.8 3.3 %early.1 = bf16[192,2048]{1,0:T(8,128)(2,1)S(1)} custom-call(bf16[64,3200]{1,0:T(8,128)(2,1)S(1)} %get-tuple-element.25.own, bf16[64,3200]{1,0:T(8,128)(2,1)S(1)} %collective-permute-done.4.outer, bf16[64,3200]{1,0:T(8,128)(2,1)S(1)} %collective-permute-done.3.inner, bf16[64,3200]{1,0:T(8,128)(2,1)S(1)} %collective-permute-done.6.ends, f32[3200]{0:T(1024)S(1)} %copy-done.5, ...), custom_call_target="tpu_custom_call" | custom-call | flops 2516582400 | bytes 13107200 | tf_op jit(solution)/shard_map/early/pallas_call | solution.py:277
  31.1 4.1 %collective-permute-done.i1 = bf16[64,128]{1,0:T(8,128)(2,1)S(1)} collective-permute-done((bf16[64,128]{1,0:T(8,128)(2,1)S(1)}, bf16[64,128]{1,0:T(8,128)(2,1)S(1)}, u32[]{:S(2)}, u32[]{:S(2)}) %collective-permute-start) | collective-permute-done | bytes 16416 | tf_op jit(solution)/shard_map/ppermute | solution.py:202
  35.2 0.4 collective-permute-done.1.i2
  35.6 0.5 collective-permute-done.2.i3
  36.1 0.0 collective-permute-done.5.last
  36.1 2.9 %project.1 = (bf16[64,2048]{1,0:T(8,128)(2,1)S(1)}, bf16[64,2048]{1,0:T(8,128)(2,1)S(1)}, bf16[64,2048]{1,0:T(8,128)(2,1)S(1)}, bf16[64,2048]{1,0:T(8,128)(2,1)S(1)}, f32[256,128]{1,0:T(8,128)S(1)}) custom-call(bf16[64,128]{1,0:T(8,128)(2,1)S(1)} %get-tuple-element.24.i0, bf16[64,128]{1,0:T(8,128)(2,1)S(1)} %collective-permute-done.i1, ...), custom_call_target="tpu_custom_call" | custom-call | flops 2516582400 | bytes 13107200 | tf_op jit(solution)/shard_map/project/pallas_call | solution.py:288
  39.0 1.6 %collective-permute-start.7 = (bf16[64,2048]{1,0:T(8,128)(2,1)S(1)}, bf16[64,2048]{1,0:T(8,128)(2,1)S(1)}, u32[]{:S(2)}, u32[]{:S(2)}) collective-permute-start(bf16[64,2048]{1,0:T(8,128)(2,1)S(1)} %get-tuple-element.32), channel_id=1, source_target_pairs={{0,8},{4,12},{8,0},{12,4},{16,24},{20,28},{24,16},{28,20},{1,9},{5... | collective-permute-start | bytes 786440 | tf_op jit(solution)/shard_map/ppermute | solution.py:226
  40.6 1.5 %collective-permute-start.8 = (bf16[64,2048]{1,0:T(8,128)(2,1)S(1)}, bf16[64,2048]{1,0:T(8,128)(2,1)S(1)}, u32[]{:S(2)}, u32[]{:S(2)}) collective-permute-start(bf16[64,2048]{1,0:T(8,128)(2,1)S(1)} %get-tuple-element.33), channel_id=1, source_target_pairs={{0,16},{4,20},{8,24},{12,28},{16,0},{20,4},{24,8},{28,12},{1,17},{... | collective-permute-start | bytes 786440 | tf_op jit(solution)/shard_map/ppermute | solution.py:226
  42.1 0.5 collective-permute-start.9
  42.6 13.0 %all_to_all.11 = f32[32,8,128]{2,1,0:T(8,128)S(1)} all-to-all(f32[32,8,128]{2,1,0:T(8,128)S(1)} %bitcast.5), channel_id=1, replica_groups=mesh['grp'=8,'dp'=4] {'grp','dp'}, dimensions={0} | all-to-all | bytes 262144 | tf_op jit(solution)/shard_map/all_to_all | solution.py:303
  55.6 0.0 collective-permute-done.7.refs_1_.rest_1_
  55.6 0.0 collective-permute-done.8.refs_2_.rest_2_
  55.6 0.0 collective-permute-done.9.refs_3_.rest_3_
  55.6 0.1 collective-permute-start.10
  55.7 0.0 copy-done.3
  55.7 0.0 copy-done.7
  55.7 0.8 %base.1 = (bf16[256,2048]{1,0:T(8,128)(2,1)S(1)}, bf16[256,128]{1,0:T(8,128)(2,1)S(1)}) custom-call(f32[64,128]{1,0:T(8,128)S(1)} %scale.1.scales, f32[1,2048]{1,0:T(1,128)S(1)} %bitcast.8, bf16[256,2048]{1,0:T(8,128)(2,1)S(1)} %copy-done.3, bf16[64,2048]{1,0:T(8,128)(2,1)S(1)} %get-tuple-element.37.refs_0_.rest_0_, ...), custom_call_target="tpu_custom_call" | custom-call | bytes 13107200 | tf_op jit(solution)/shard_map/base/pallas_call | solution.py:321
  56.5 1.1 %collective-permute-done.10.odd = bf16[128,2048]{1,0:T(8,128)(2,1)S(1)} collective-permute-done((bf16[128,2048]{1,0:T(8,128)(2,1)S(1)}, bf16[128,2048]{1,0:T(8,128)(2,1)S(1)}, u32[]{:S(2)}, u32[]{:S(2)}) %collective-permute-start.10) | collective-permute-done | bytes 524320 | tf_op jit(solution)/shard_map/ppermute | solution.py:226
  57.6 1.6 %place.1 = bf16[256,2048]{1,0:T(8,128)(2,1)} custom-call(f32[64,128]{1,0:T(8,128)S(1)} %scale.1.scales, f32[1,2048]{1,0:T(1,128)S(1)} %bitcast.9, bf16[128,2048]{1,0:T(8,128)(2,1)S(1)} %collective-permute-done.10.odd, bf16[256,2048]{1,0:T(8,128)(2,1)S(1)} %get-tuple-element.41.base, bf16[256,128]{1,0:T(8,128)(2,1)S(1)} %get-tuple-element.42.order), custom_call_target="tpu_custom_call" | custom-call | tf_op jit(solution)/shard_map/place/pallas_call | solution.py:334
  (4 shorter events, 0.1 us)
Async XLA Ops:
  0.0 19.6 %collective-permute-start.3 = (bf16[64,3200]{1,0:T(8,128)(2,1)}, bf16[64,3200]{1,0:T(8,128)(2,1)S(1)}, u32[]{:S(2)}, u32[]{:S(2)}) collective-permute-start(bf16[64,3200]{1,0:T(8,128)(2,1)} %vis.1), channel_id=1, source_target_pairs={{1,2},{2,1},{0,0},{3,3},{5,6},{6,5},{4,4},{7,7},{9,10},{10,9},{8,8... | collective-permute-start | bytes 1228808 | tf_op jit(solution)/shard_map/ppermute | solution.py:206
  1.6 18.0 %collective-permute-start.4 = (bf16[64,3200]{1,0:T(8,128)(2,1)}, bf16[64,3200]{1,0:T(8,128)(2,1)S(1)}, u32[]{:S(2)}, u32[]{:S(2)}) collective-permute-start(bf16[64,3200]{1,0:T(8,128)(2,1)} %vis.1), channel_id=1, source_target_pairs={{0,1},{1,0},{2,3},{3,2},{4,5},{5,4},{6,7},{7,6},{8,9},{9,8},{10,11... | collective-permute-start | bytes 1228808 | tf_op jit(solution)/shard_map/ppermute | solution.py:202
  7.2 1.2 %copy-start.2 = (bf16[256,2048]{1,0:T(8,128)(2,1)S(1)}, bf16[256,2048]{1,0:T(8,128)(2,1)}, u32[]{:S(2)}) copy-start(bf16[256,2048]{1,0:T(8,128)(2,1)} %text.3) | copy-start | bytes 3145732
  8.4 1.0 %copy-start.4 = (bf16[64,3200]{1,0:T(8,128)(2,1)S(1)}, bf16[64,3200]{1,0:T(8,128)(2,1)}, u32[]{:S(2)}) copy-start(bf16[64,3200]{1,0:T(8,128)(2,1)} %vis.1) | copy-start | bytes 1228804
  9.5 0.7 %copy-start.8 = (s32[4]{0:T(128)S(1)}, s32[4]{0:T(128)}, u32[]{:S(2)}) copy-start(s32[4]{0:T(128)} %owners.1) | copy-start | bytes 52
  10.1 0.7 %copy-start.9 = (s32[4]{0:T(128)S(1)}, s32[4]{0:T(128)}, u32[]{:S(2)}) copy-start(s32[4]{0:T(128)} %offsets.1) | copy-start | bytes 52
  10.8 17.0 %copy-start.5 = (f32[3200]{0:T(1024)S(1)}, f32[3200]{0:T(1024)}, u32[]{:S(2)}) copy-start(f32[3200]{0:T(1024)} %gain.3) | copy-start | bytes 38404
  10.8 17.0 %copy-start.6 = (f32[2048]{0:T(1024)S(1)}, f32[2048]{0:T(1024)}, u32[]{:S(2)}) copy-start(f32[2048]{0:T(1024)} %param.12) | copy-start | bytes 24580
  11.6 16.2 %collective-permute-start.6 = (bf16[64,3200]{1,0:T(8,128)(2,1)S(1)}, bf16[64,3200]{1,0:T(8,128)(2,1)S(1)}, u32[]{:S(2)}, u32[]{:S(2)}) collective-permute-start(bf16[64,3200]{1,0:T(8,128)(2,1)S(1)} %get-tuple-element.25.own), channel_id=1, source_target_pairs={{0,3},{3,0},{1,1},{2,2},{4,7},{7,4},{5,5},{6,6},{8,11},{11,8},{9,9... | collective-permute-start | bytes 1228808 | tf_op jit(solution)/shard_map/ppermute | solution.py:210
  14.8 4.7 %copy-start = (bf16[3200,2048]{1,0:T(8,128)(2,1)S(1)}, bf16[3200,2048]{1,0:T(8,128)(2,1)}, u32[]{:S(2)}) copy-start(bf16[3200,2048]{1,0:T(8,128)(2,1)} %weight.5) | copy-start | bytes 39321604
  19.6 8.2 %copy-start.1 = (bf16[3200,2048]{1,0:T(8,128)(2,1)S(1)}, bf16[3200,2048]{1,0:T(8,128)(2,1)}, u32[]{:S(2)}) copy-start(bf16[3200,2048]{1,0:T(8,128)(2,1)} %weight.5) | copy-start | bytes 39321604
  19.6 16.5 %collective-permute-start.5 = (bf16[64,3200]{1,0:T(8,128)(2,1)S(1)}, bf16[64,3200]{1,0:T(8,128)(2,1)S(1)}, u32[]{:S(2)}, u32[]{:S(2)}) collective-permute-start(bf16[64,3200]{1,0:T(8,128)(2,1)S(1)} %pass.1), channel_id=1, source_target_pairs={{0,2},{1,0},{2,3},{3,1},{4,6},{5,4},{6,7},{7,5},{8,10},{9,8},{10,1... | collective-permute-start | bytes 1228808 | tf_op jit(solution)/shard_map/ppermute | solution.py:222
  19.7 15.5 %collective-permute-start = (bf16[64,128]{1,0:T(8,128)(2,1)S(1)}, bf16[64,128]{1,0:T(8,128)(2,1)S(1)}, u32[]{:S(2)}, u32[]{:S(2)}) collective-permute-start(bf16[64,128]{1,0:T(8,128)(2,1)S(1)} %get-tuple-element.24.i0), channel_id=1, source_target_pairs={{0,1},{1,0},{2,3},{3,2},{4,5},{5,4},{6,7},{7,6},{8,9},{9,8},{10,11... | collective-permute-start | bytes 49160 | tf_op jit(solution)/shard_map/ppermute | solution.py:202
  21.7 13.9 %collective-permute-start.1 = (bf16[64,128]{1,0:T(8,128)(2,1)S(1)}, bf16[64,128]{1,0:T(8,128)(2,1)S(1)}, u32[]{:S(2)}, u32[]{:S(2)}) collective-permute-start(bf16[64,128]{1,0:T(8,128)(2,1)S(1)} %get-tuple-element.24.i0), channel_id=1, source_target_pairs={{0,3},{1,2},{2,1},{3,0},{4,7},{5,6},{6,5},{7,4},{8,11},{9,10},{10,... | collective-permute-start | bytes 49160 | tf_op jit(solution)/shard_map/ppermute | solution.py:214
  24.2 11.9 %collective-permute-start.2 = (bf16[64,128]{1,0:T(8,128)(2,1)S(1)}, bf16[64,128]{1,0:T(8,128)(2,1)S(1)}, u32[]{:S(2)}, u32[]{:S(2)}) collective-permute-start(bf16[64,128]{1,0:T(8,128)(2,1)S(1)} %get-tuple-element.24.i0), channel_id=1, source_target_pairs={{0,2},{1,3},{2,0},{3,1},{4,6},{5,7},{6,4},{7,5},{8,10},{9,11},{10,... | collective-permute-start | bytes 49160 | tf_op jit(solution)/shard_map/ppermute | solution.py:218
  27.8 27.9 %copy-start.3 = (bf16[256,2048]{1,0:T(8,128)(2,1)S(1)}, bf16[256,2048]{1,0:T(8,128)(2,1)}, u32[]{:S(2)}) copy-start(bf16[256,2048]{1,0:T(8,128)(2,1)} %text.3) | copy-start | bytes 3145732
  27.8 27.9 %copy-start.7 = (f32[2048]{0:T(1024)S(1)}, f32[2048]{0:T(1024)}, u32[]{:S(2)}) copy-start(f32[2048]{0:T(1024)} %param.14) | copy-start | bytes 24580
  39.0 16.6 %collective-permute-start.7 = (bf16[64,2048]{1,0:T(8,128)(2,1)S(1)}, bf16[64,2048]{1,0:T(8,128)(2,1)S(1)}, u32[]{:S(2)}, u32[]{:S(2)}) collective-permute-start(bf16[64,2048]{1,0:T(8,128)(2,1)S(1)} %get-tuple-element.32), channel_id=1, source_target_pairs={{0,8},{4,12},{8,0},{12,4},{16,24},{20,28},{24,16},{28,20},{1,9},{5... | collective-permute-start | bytes 786440 | tf_op jit(solution)/shard_map/ppermute | solution.py:226
  40.6 15.0 %collective-permute-start.8 = (bf16[64,2048]{1,0:T(8,128)(2,1)S(1)}, bf16[64,2048]{1,0:T(8,128)(2,1)S(1)}, u32[]{:S(2)}, u32[]{:S(2)}) collective-permute-start(bf16[64,2048]{1,0:T(8,128)(2,1)S(1)} %get-tuple-element.33), channel_id=1, source_target_pairs={{0,16},{4,20},{8,24},{12,28},{16,0},{20,4},{24,8},{28,12},{1,17},{... | collective-permute-start | bytes 786440 | tf_op jit(solution)/shard_map/ppermute | solution.py:226
  42.1 13.5 %collective-permute-start.9 = (bf16[64,2048]{1,0:T(8,128)(2,1)S(1)}, bf16[64,2048]{1,0:T(8,128)(2,1)S(1)}, u32[]{:S(2)}, u32[]{:S(2)}) collective-permute-start(bf16[64,2048]{1,0:T(8,128)(2,1)S(1)} %get-tuple-element.34), channel_id=1, source_target_pairs={{0,24},{4,28},{8,16},{12,20},{16,8},{20,12},{24,0},{28,4},{1,25},{... | collective-permute-start | bytes 786440 | tf_op jit(solution)/shard_map/ppermute | solution.py:226
  55.6 2.0 %collective-permute-start.10 = (bf16[128,2048]{1,0:T(8,128)(2,1)S(1)}, bf16[128,2048]{1,0:T(8,128)(2,1)S(1)}, u32[]{:S(2)}, u32[]{:S(2)}) collective-permute-start(bf16[128,2048]{1,0:T(8,128)(2,1)S(1)} %pack.1), channel_id=1, source_target_pairs={{0,4},{4,0},{8,12},{12,8},{16,20},{20,16},{24,28},{28,24},{1,5},{5... | collective-permute-start | bytes 1572872 | tf_op jit(solution)/shard_map/ppermute | solution.py:226

commit v4 on v3

--- a/solution.py
+++ b/solution.py
@@ -40,9 +40,13 @@
     own[...] = vis[...]
 
 
-def pass_kernel(own, inner, sent):
+def pass_kernel(own, inner, gain, sent, later):
     row = lax.axis_index("dp")
-    sent[...] = jnp.where(jnp.logical_or(row == 1, row == 2), inner[...], own[...])
+    depth, stretch = inner.shape[1], sent.shape[1]
+    rows = jnp.where(jnp.logical_or(row == 1, row == 2), inner[...], own[...])
+    rows = normed(rows, gain[...].reshape(1, depth))
+    sent[...] = rows[:, :stretch]
+    later[...] = rows[:, stretch:]
 
 
 def hold_kernel(weight, tile, out):
@@ -71,52 +75,55 @@
         y[:, at] = (jnp.dot(x[...], weight[:, at], preferred_element_type=F32) + bias[:, at]).astype(BF16)
 
 
-def project_kernel(groups, cap, size, i0, i1, i2, i3, last, gain, weight, bias, early, text_squares, *rest):
+def late_kernel(last, weight, bias, total):
+    depth = last.shape[1]
+    total[...] = jnp.dot(last[...], weight[:depth, :], preferred_element_type=F32) + bias[...]
+
+
+def project_kernel(groups, cap, size, i0, i1, i2, i3, last, weight, total, early, text_squares, *rest):
     *parts, tiles, y, z, codes = rest
     me = lax.axis_index("grp")
     depth, columns = weight.shape
-    known = jnp.concatenate([i0[...], i1[...], i2[...], i3[...]], axis=0)
-    total = known.shape[0]
-    down = known.astype(F32)
+    stretch = last.shape[1]
+    down = jnp.concatenate([i0[...], i1[...], i2[...], i3[...]], axis=0).astype(F32)
+    rows = down.shape[0]
     across = down.T
     owner_down, slot_down = down[:, 0:1], down[:, 1:2]
     owner, slot = across[0:1, :], across[1:2, :]
     earlier = jnp.logical_and(owner_down == owner, slot_down < slot)
     rank = jnp.sum(earlier.astype(F32), axis=0, keepdims=True).astype(jnp.int32) // size
     place = owner.astype(jnp.int32) ^ me
-    position = lax.broadcasted_iota(jnp.int32, (1, total), 1) % size
+    position = lax.broadcasted_iota(jnp.int32, (1, rows), 1) % size
     seat = (place * cap + rank) * size + position
     first = position == 0
-    image = lax.broadcasted_iota(jnp.int32, (1, total), 1) // size
-    seats = [
+    image = lax.broadcasted_iota(jnp.int32, (1, rows), 1) // size
+    at = [
         pl.multiple_of(jnp.sum(jnp.where(jnp.logical_and(first, image == i), seat, 0)), size)
-        for i in range(total // size)
+        for i in range(rows // size)
     ]
-    x = normed(last[...], gain[...].reshape(1, depth))
-    count = last.shape[0]
-    for i in range((total - count) // size):
-        y[pl.ds(seats[i], size), :] = early[i * size : (i + 1) * size]
     block = 256
     for n in range(columns // block):
-        at = slice(n * block, (n + 1) * block)
-        z[:, at] = (jnp.dot(x, weight[:, at], preferred_element_type=F32) + bias[:, at]).astype(BF16)
-    for i in range(count // size):
-        y[pl.ds(seats[(total - count) // size + i], size), :] = z[i * size : (i + 1) * size]
-    for i in range(total // size):
-        codes[pl.ds(seats[i], size), :] = down[i * size : (i + 1) * size]
-    rows = total // len(parts)
+        part = slice(n * block, (n + 1) * block)
+        more = jnp.dot(last[...], weight[depth - stretch :, part], preferred_element_type=F32)
+        z[:, part] = (total[:, part] + more).astype(BF16)
+    count = early.shape[0] // size
+    for i in range(rows // size):
+        source, n = (early, i) if i < count else (z, i - count)
+        y[pl.ds(at[i], size), :] = source[n * size : (n + 1) * size]
+        codes[pl.ds(at[i], size), :] = down[i * size : (i + 1) * size]
+    chunk = rows // len(parts)
     for m, part in enumerate(parts):
-        part[...] = y[m * rows : (m + 1) * rows]
+        part[...] = y[m * chunk : (m + 1) * chunk]
     lane = lanes()
     copies = tiles.shape[0] // (8 * groups)
     for k in range(groups):
         tile = jnp.zeros(TILE, F32)
         for r in range(cap):
-            at = (k * cap + r) * size
-            wide = y[at : at + size, :].astype(F32)
+            start = (k * cap + r) * size
+            wide = y[start : start + size, :].astype(F32)
+            tile = jnp.where(lane == 2 * cap + r, codes[start : start + 8, 2:3], tile)
             sums = jnp.sum(wide * wide, axis=1, keepdims=True)
             tile = jnp.where(lane == 2 * r, sums[:8], jnp.where(lane == 2 * r + 1, sums[8:], tile))
-            tile = jnp.where(lane == 2 * cap + r, codes[at : at + 8, 2:3], tile)
         if k == 0:
             tile = jnp.where(lane < 3 * cap, tile, pltpu.roll(text_squares[...], 3 * cap, 1))
         for q in range(copies):
@@ -248,7 +255,7 @@
         compiler_params=small,
         name="tables",
     )(text, vis, owners, offsets, counts)
-    x_ends = ends(own)
+    x_ends = ends(vis)
     weight = pltpu.with_memory_space_constraint(weight, pltpu.VMEM)
     text_squares = pl.pallas_call(
         hold_kernel,
@@ -260,17 +267,21 @@
         name="hold",
     )(weight, text_squares)
     x_inner, text_squares = lax.optimization_barrier((x_inner, text_squares))
-    sent = pl.pallas_call(
+    stretches = depth // 3 // 128 * 128
+    stretches = (depth - stretches, stretches)
+    stretch = depth // 3 // 128 * 128
+    sent, later = pl.pallas_call(
         pass_kernel,
-        in_specs=[VMEM] * 2,
-        out_specs=VMEM,
-        out_shape=jax.ShapeDtypeStruct(vis.shape, BF16),
+        in_specs=[VMEM] * 3,
+        out_specs=[VMEM] * 2,
+        out_shape=[jax.ShapeDtypeStruct((count, n), BF16) for n in (depth - stretch, stretch)],
         compiler_params=small,
         name="pass",
-    )(own, x_inner)
-    sent, x_outer = lax.optimization_barrier((sent, x_outer))
-    x_far = far(sent)
+    )(own, x_inner, vis_gain)
+    sent, later, x_outer = lax.optimization_barrier((sent, later, x_outer))
+    last_a = far(sent)
     known = (info, outer(info), mirror(info), second(info))
+    last_b = far(later)
     cost = pl.CostEstimate(
         flops=2 * 3 * count * depth * columns, bytes_accessed=2 * weight.size, transcendentals=0
     )
@@ -285,9 +296,18 @@
         name="early",
     )(own, x_outer, x_inner, x_ends, vis_gain, weight, bias)
     pairs = groups // 2
+    total = pl.pallas_call(
+        late_kernel,
+        in_specs=[VMEM] * 3,
+        out_specs=VMEM,
+        out_shape=jax.ShapeDtypeStruct((count, columns), F32),
+        compiler_params=small,
+        cost_estimate=cost,
+        name="late",
+    )(last_a, weight, bias)
     *parts, squares = pl.pallas_call(
         functools.partial(project_kernel, groups, cap, size),
-        in_specs=[VMEM] * 10,
+        in_specs=[VMEM] * 9,
         out_specs=[VMEM] * (pairs + 1),
         out_shape=[jax.ShapeDtypeStruct((2 * cap * size, columns), BF16)] * pairs
         + [jax.ShapeDtypeStruct((devices * 8, 128), F32)],
@@ -299,7 +319,7 @@
         compiler_params=small,
         cost_estimate=cost,
         name="project",
-    )(*known, x_far, vis_gain, weight, bias, early, text_squares)
+    )(*known, last_b, weight, total, early, text_squares)
     squares = lax.all_to_all(squares, ("grp", "dp"), 0, 0, tiled=True)
     scales = pl.pallas_call(
         functools.partial(scale_kernel, groups, dp, cap, columns * dp),

time: 59.5 us -> 57.7 us (0.970)
  waiting for transfers between devices: 9.69 us -> 7.69 us
    ppermute x2, waiting for transfers between devices: 4.15 us -> 0.01 us  [outer(): return lax.ppermute(x, 'dp', [(0, 1), (1, 0), (2, 3), (3, 2)])]
    pallas_call x1 -> x2, Pallas kernels: 0.05 us -> 1.92 us  [the longest x1 1.7 us: fast(): pl.pallas_call(late_kernel, in_specs=[VMEM] * 3, out_specs=VMEM, out_shap...]
    pallas_call x1, Pallas kernels: 2.9 us -> 1.24 us  [fast(): pl.pallas_call(functools.partial(project_kernel, groups, cap, size), in_s...]
    ppermute x1, waiting for transfers between devices: 0.48 us -> 2 us  [second(): return lax.ppermute(x, 'dp', [(0, 2), (1, 3), (2, 0), (3, 1)])]
    ppermute x1 -> x2, waiting for transfers between devices: 0.01 us -> 1.39 us  [far(): return lax.ppermute(x, 'dp', [(0, 2), (1, 0), (2, 3), (3, 1)])]
  transfers between devices with their start and end apart: 11 -> 12, of which waited for: 5 -> 5; matrix products, arithmetic and copies ran while one was open for 0% -> 0% of each run, Pallas kernels for 8% -> 12%
where the time goes in v4:
time: 57.7 us; the launch traced here: 57.4 us
  starting transfers between devices  18 us (31%)
  blocking collectives  12.9 us (22%)
  Pallas kernels  9.66 us (17%)
  local copies, waits for them, and re-layouts  8.28 us (14%)
  waiting for transfers between devices  7.69 us (13%)
  between operations  0.82 us (1%)
    all_to_all x1, blocking collectives, fast(): squares = lax.all_to_all(squares, ('grp', 'dp'), 0, 0, tiled=True)  12.9 us
    unnamed x20, local copies, waits for them, and re-layouts  8.28 us
    ppermute x2, starting transfers between devices, outer(): return lax.ppermute(x, 'dp', [(0, 1), (1, 0), (2, 3), (3, 2)])  6.93 us
    ppermute x4, starting transfers between devices, across(): lax.ppermute(x, 'grp', [(i, i ^ k) for i in range(lax.axis_size('grp'))])  3.62 us
    pallas_call x1, Pallas kernels, fast(): pl.pallas_call(early_kernel, in_specs=[VMEM] * 7, out_specs=VMEM, out_sha...  3.26 us
    ppermute x1, starting transfers between devices, ends(): return lax.ppermute(x, 'dp', [(0, 3), (3, 0), (1, 1), (2, 2)])  3.24 us
    ppermute x1, waiting for transfers between devices, ends(): return lax.ppermute(x, 'dp', [(0, 3), (3, 0), (1, 1), (2, 2)])  3 us
    ppermute x1, starting transfers between devices, mirror(): return lax.ppermute(x, 'dp', [(0, 3), (1, 2), (2, 1), (3, 0)])  2.48 us
  transfers between devices with their start and end apart: 12, of which 5 were waited for; matrix products, arithmetic and copies ran while one was open for 0% of the time, Pallas kernels for 12%

profile of v4, /device:TPU:0, one launch (start us, length us, event | category | flops | bytes accessed | tf_op | source)
XLA Modules:
  0.0 57.4 jit_solution(11556354407910424853)
XLA Ops:
  0.0 1.6 %collective-permute-start.3 = (bf16[64,3200]{1,0:T(8,128)(2,1)}, bf16[64,3200]{1,0:T(8,128)(2,1)S(1)}, u32[]{:S(2)}, u32[]{:S(2)}) collective-permute-start(bf16[64,3200]{1,0:T(8,128)(2,1)} %vis.1), channel_id=1, source_target_pairs={{1,2},{2,1},{0,0},{3,3},{5,6},{6,5},{4,4},{7,7},{9,10},{10,9},{8,8... | collective-permute-start | bytes 1228808 | tf_op jit(solution)/shard_map/ppermute | solution.py:213
  1.6 4.9 %collective-permute-start.4 = (bf16[64,3200]{1,0:T(8,128)(2,1)}, bf16[64,3200]{1,0:T(8,128)(2,1)S(1)}, u32[]{:S(2)}, u32[]{:S(2)}) collective-permute-start(bf16[64,3200]{1,0:T(8,128)(2,1)} %vis.1), channel_id=1, source_target_pairs={{0,1},{1,0},{2,3},{3,2},{4,5},{5,4},{6,7},{7,6},{8,9},{9,8},{10,11... | collective-permute-start | bytes 1228808 | tf_op jit(solution)/shard_map/ppermute | solution.py:209
  6.6 3.2 %collective-permute-start.7 = (bf16[64,3200]{1,0:T(8,128)(2,1)}, bf16[64,3200]{1,0:T(8,128)(2,1)S(1)}, u32[]{:S(2)}, u32[]{:S(2)}) collective-permute-start(bf16[64,3200]{1,0:T(8,128)(2,1)} %vis.1), channel_id=1, source_target_pairs={{0,3},{3,0},{1,1},{2,2},{4,7},{7,4},{5,5},{6,6},{8,11},{11,8},{9,9... | collective-permute-start | bytes 1228808 | tf_op jit(solution)/shard_map/ppermute | solution.py:217
  10.5 0.0 copy-start.2
  10.5 1.2 %copy-done.2 = bf16[256,2048]{1,0:T(8,128)(2,1)S(1)} copy-done((bf16[256,2048]{1,0:T(8,128)(2,1)S(1)}, bf16[256,2048]{1,0:T(8,128)(2,1)}, u32[]{:S(2)}) %copy-start.2) | copy-done | bytes 1048600
  11.7 0.0 copy-start.4
  11.7 1.0 %copy-done.4 = bf16[64,3200]{1,0:T(8,128)(2,1)S(1)} copy-done((bf16[64,3200]{1,0:T(8,128)(2,1)S(1)}, bf16[64,3200]{1,0:T(8,128)(2,1)}, u32[]{:S(2)}) %copy-start.4) | copy-done | bytes 409624
  12.7 0.0 copy-start.8
  12.7 0.7 %copy-done.8 = s32[4]{0:T(128)S(1)} copy-done((s32[4]{0:T(128)S(1)}, s32[4]{0:T(128)}, u32[]{:S(2)}) %copy-start.8) | copy-done | bytes 40
  13.4 0.0 copy-start.9
  13.4 0.7 %copy-done.9 = s32[4]{0:T(128)S(1)} copy-done((s32[4]{0:T(128)S(1)}, s32[4]{0:T(128)}, u32[]{:S(2)}) %copy-start.9) | copy-done | bytes 40
  14.0 0.0 copy-start.5
  14.0 0.0 copy-start.6
  14.0 0.8 %tables.1 = (f32[8,128]{1,0:T(8,128)S(1)}, bf16[64,128]{1,0:T(8,128)(2,1)S(1)}, bf16[64,3200]{1,0:T(8,128)(2,1)S(1)}) custom-call(bf16[256,2048]{1,0:T(8,128)(2,1)S(1)} %copy-done.2, bf16[64,3200]{1,0:T(8,128)(2,1)S(1)} %copy-done.4, s32[4]{0:T(128)S(1)} %copy-done.8, s32[4]{0:T(128)S(1)} %copy-done.9, s32[1]{0:T(128)S(6)} %copy.10.counts), custom_call_target="tpu_custom_call" | custom-call | tf_op jit(solution)/shard_map/tables/pallas_call | solution.py:250
  14.8 0.0 copy-start
  14.8 4.7 %copy-done = bf16[3200,2048]{1,0:T(8,128)(2,1)S(1)} copy-done((bf16[3200,2048]{1,0:T(8,128)(2,1)S(1)}, bf16[3200,2048]{1,0:T(8,128)(2,1)}, u32[]{:S(2)}) %copy-start) | copy-done | bytes 13107224
  19.6 0.0 copy-start.1
  19.6 0.0 collective-permute-done.3.inner
  19.6 0.0 copy-done.5
  19.6 0.2 pass.1
  19.8 0.0 collective-permute-done.4.outer
  19.8 0.1 collective-permute-start.6
  19.9 2.0 %collective-permute-start = (bf16[64,128]{1,0:T(8,128)(2,1)S(1)}, bf16[64,128]{1,0:T(8,128)(2,1)S(1)}, u32[]{:S(2)}, u32[]{:S(2)}) collective-permute-start(bf16[64,128]{1,0:T(8,128)(2,1)S(1)} %get-tuple-element.27.i0), channel_id=1, source_target_pairs={{0,1},{1,0},{2,3},{3,2},{4,5},{5,4},{6,7},{7,6},{8,9},{9,8},{10,11... | collective-permute-start | bytes 49160 | tf_op jit(solution)/shard_map/ppermute | solution.py:209
  21.9 2.5 %collective-permute-start.1 = (bf16[64,128]{1,0:T(8,128)(2,1)S(1)}, bf16[64,128]{1,0:T(8,128)(2,1)S(1)}, u32[]{:S(2)}, u32[]{:S(2)}) collective-permute-start(bf16[64,128]{1,0:T(8,128)(2,1)S(1)} %get-tuple-element.27.i0), channel_id=1, source_target_pairs={{0,3},{1,2},{2,1},{3,0},{4,7},{5,6},{6,5},{7,4},{8,11},{9,10},{10,... | collective-permute-start | bytes 49160 | tf_op jit(solution)/shard_map/ppermute | solution.py:221
  24.4 0.0 collective-permute-start.2
  24.4 3.0 %collective-permute-done.7.ends = bf16[64,3200]{1,0:T(8,128)(2,1)S(1)} collective-permute-done((bf16[64,3200]{1,0:T(8,128)(2,1)}, bf16[64,3200]{1,0:T(8,128)(2,1)S(1)}, u32[]{:S(2)}, u32[]{:S(2)}) %collective-permute-start.7) | collective-permute-done | bytes 409632 | tf_op jit(solution)/shard_map/ppermute | solution.py:217
  27.4 0.0 collective-permute-start.5
  27.4 0.0 copy-done.6
  27.4 0.0 copy-done.1
  27.4 3.3 %early.1 = bf16[192,2048]{1,0:T(8,128)(2,1)S(1)} custom-call(bf16[64,3200]{1,0:T(8,128)(2,1)S(1)} %get-tuple-element.28.own, bf16[64,3200]{1,0:T(8,128)(2,1)S(1)} %collective-permute-done.4.outer, bf16[64,3200]{1,0:T(8,128)(2,1)S(1)} %collective-permute-done.3.inner, bf16[64,3200]{1,0:T(8,128)(2,1)S(1)} %collective-permute-done.7.ends, f32[3200]{0:T(1024)S(1)} %copy-done.5, ...), custom_call_target="tpu_custom_call" | custom-call | flops 2516582400 | bytes 13107200 | tf_op jit(solution)/shard_map/early/pallas_call | solution.py:288
  30.6 0.0 copy-start.3
  30.7 0.0 copy-start.7
  30.7 1.4 %collective-permute-done.6.last = bf16[64,2176]{1,0:T(8,128)(2,1)S(1)} collective-permute-done((bf16[64,2176]{1,0:T(8,128)(2,1)S(1)}, bf16[64,2176]{1,0:T(8,128)(2,1)S(1)}, u32[]{:S(2)}, u32[]{:S(2)}) %collective-permute-start.6) | collective-permute-done | bytes 278560 | tf_op jit(solution)/shard_map/ppermute | solution.py:229
  32.1 1.7 %late.1.total = f32[64,2048]{1,0:T(8,128)S(1)} custom-call(bf16[64,2176]{1,0:T(8,128)(2,1)S(1)} %collective-permute-done.6.last, bf16[3200,2048]{1,0:T(8,128)(2,1)S(1)} %copy-done.1, f32[1,2048]{1,0:T(1,128)S(1)} %bitcast.7), custom_call_target="tpu_custom_call" | custom-call | flops 2516582400 | bytes 13107200 | tf_op jit(solution)/shard_map/late/pallas_call | solution.py:299
  33.8 0.0 collective-permute-done.i1
  33.8 0.2 collective-permute-done.1.i2
  34.0 2.0 %collective-permute-done.2.i3 = bf16[64,128]{1,0:T(8,128)(2,1)S(1)} collective-permute-done((bf16[64,128]{1,0:T(8,128)(2,1)S(1)}, bf16[64,128]{1,0:T(8,128)(2,1)S(1)}, u32[]{:S(2)}, u32[]{:S(2)}) %collective-permute-start.2) | collective-permute-done | bytes 16416 | tf_op jit(solution)/shard_map/ppermute | solution.py:225
  36.0 0.0 collective-permute-done.5.last
  36.0 1.2 %project.1 = (bf16[64,2048]{1,0:T(8,128)(2,1)S(1)}, bf16[64,2048]{1,0:T(8,128)(2,1)S(1)}, bf16[64,2048]{1,0:T(8,128)(2,1)S(1)}, bf16[64,2048]{1,0:T(8,128)(2,1)S(1)}, f32[256,128]{1,0:T(8,128)S(1)}) custom-call(bf16[64,128]{1,0:T(8,128)(2,1)S(1)} %get-tuple-element.27.i0, bf16[64,128]{1,0:T(8,128)(2,1)S(1)} %collective-permute-done.i1, ...), custom_call_target="tpu_custom_call" | custom-call | flops 2516582400 | bytes 13107200 | tf_op jit(solution)/shard_map/project/pallas_call | solution.py:308
  37.2 2.5 %collective-permute-start.10 = (bf16[64,2048]{1,0:T(8,128)(2,1)S(1)}, bf16[64,2048]{1,0:T(8,128)(2,1)S(1)}, u32[]{:S(2)}, u32[]{:S(2)}) collective-permute-start(bf16[64,2048]{1,0:T(8,128)(2,1)S(1)} %get-tuple-element.40), channel_id=1, source_target_pairs={{0,24},{4,28},{8,16},{12,20},{16,8},{20,12},{24,0},{28,4},{1,25},{... | collective-permute-start | bytes 786440 | tf_op jit(solution)/shard_map/ppermute | solution.py:233
  39.8 0.5 collective-permute-start.8
  40.3 0.5 collective-permute-start.9
  40.8 12.9 %all_to_all.11 = f32[32,8,128]{2,1,0:T(8,128)S(1)} all-to-all(f32[32,8,128]{2,1,0:T(8,128)S(1)} %bitcast.5), channel_id=1, replica_groups=mesh['grp'=8,'dp'=4] {'grp','dp'}, dimensions={0} | all-to-all | bytes 262144 | tf_op jit(solution)/shard_map/all_to_all | solution.py:323
  53.7 0.0 collective-permute-done.10.refs_3_.rest_3_
  53.8 0.0 collective-permute-done.8.refs_1_.rest_1_
  53.8 0.0 collective-permute-done.9.refs_2_.rest_2_
  53.8 0.1 collective-permute-start.11
  53.9 0.0 copy-done.3
  53.9 0.0 copy-done.7
  53.9 0.8 %base.1 = (bf16[256,2048]{1,0:T(8,128)(2,1)S(1)}, bf16[256,128]{1,0:T(8,128)(2,1)S(1)}) custom-call(f32[64,128]{1,0:T(8,128)S(1)} %scale.1.scales, f32[1,2048]{1,0:T(1,128)S(1)} %bitcast.8, bf16[256,2048]{1,0:T(8,128)(2,1)S(1)} %copy-done.3, bf16[64,2048]{1,0:T(8,128)(2,1)S(1)} %get-tuple-element.43.refs_0_.rest_0_, ...), custom_call_target="tpu_custom_call" | custom-call | bytes 13107200 | tf_op jit(solution)/shard_map/base/pallas_call | solution.py:341
  54.7 1.1 %collective-permute-done.11.odd = bf16[128,2048]{1,0:T(8,128)(2,1)S(1)} collective-permute-done((bf16[128,2048]{1,0:T(8,128)(2,1)S(1)}, bf16[128,2048]{1,0:T(8,128)(2,1)S(1)}, u32[]{:S(2)}, u32[]{:S(2)}) %collective-permute-start.11) | collective-permute-done | bytes 524320 | tf_op jit(solution)/shard_map/ppermute | solution.py:233
  55.8 1.6 %place.1 = bf16[256,2048]{1,0:T(8,128)(2,1)} custom-call(f32[64,128]{1,0:T(8,128)S(1)} %scale.1.scales, f32[1,2048]{1,0:T(1,128)S(1)} %bitcast.9, bf16[128,2048]{1,0:T(8,128)(2,1)S(1)} %collective-permute-done.11.odd, bf16[256,2048]{1,0:T(8,128)(2,1)S(1)} %get-tuple-element.47.base, bf16[256,128]{1,0:T(8,128)(2,1)S(1)} %get-tuple-element.48.order), custom_call_target="tpu_custom_call" | custom-call | tf_op jit(solution)/shard_map/place/pallas_call | solution.py:354
  (3 shorter events, 0.1 us)
Async XLA Ops:
  0.0 19.6 %collective-permute-start.3 = (bf16[64,3200]{1,0:T(8,128)(2,1)}, bf16[64,3200]{1,0:T(8,128)(2,1)S(1)}, u32[]{:S(2)}, u32[]{:S(2)}) collective-permute-start(bf16[64,3200]{1,0:T(8,128)(2,1)} %vis.1), channel_id=1, source_target_pairs={{1,2},{2,1},{0,0},{3,3},{5,6},{6,5},{4,4},{7,7},{9,10},{10,9},{8,8... | collective-permute-start | bytes 1228808 | tf_op jit(solution)/shard_map/ppermute | solution.py:213
  1.6 18.2 %collective-permute-start.4 = (bf16[64,3200]{1,0:T(8,128)(2,1)}, bf16[64,3200]{1,0:T(8,128)(2,1)S(1)}, u32[]{:S(2)}, u32[]{:S(2)}) collective-permute-start(bf16[64,3200]{1,0:T(8,128)(2,1)} %vis.1), channel_id=1, source_target_pairs={{0,1},{1,0},{2,3},{3,2},{4,5},{5,4},{6,7},{7,6},{8,9},{9,8},{10,11... | collective-permute-start | bytes 1228808 | tf_op jit(solution)/shard_map/ppermute | solution.py:209
  6.6 20.8 %collective-permute-start.7 = (bf16[64,3200]{1,0:T(8,128)(2,1)}, bf16[64,3200]{1,0:T(8,128)(2,1)S(1)}, u32[]{:S(2)}, u32[]{:S(2)}) collective-permute-start(bf16[64,3200]{1,0:T(8,128)(2,1)} %vis.1), channel_id=1, source_target_pairs={{0,3},{3,0},{1,1},{2,2},{4,7},{7,4},{5,5},{6,6},{8,11},{11,8},{9,9... | collective-permute-start | bytes 1228808 | tf_op jit(solution)/shard_map/ppermute | solution.py:217
  10.5 1.2 %copy-start.2 = (bf16[256,2048]{1,0:T(8,128)(2,1)S(1)}, bf16[256,2048]{1,0:T(8,128)(2,1)}, u32[]{:S(2)}) copy-start(bf16[256,2048]{1,0:T(8,128)(2,1)} %text.3) | copy-start | bytes 3145732
  11.7 1.0 %copy-start.4 = (bf16[64,3200]{1,0:T(8,128)(2,1)S(1)}, bf16[64,3200]{1,0:T(8,128)(2,1)}, u32[]{:S(2)}) copy-start(bf16[64,3200]{1,0:T(8,128)(2,1)} %vis.1) | copy-start | bytes 1228804
  12.7 0.7 %copy-start.8 = (s32[4]{0:T(128)S(1)}, s32[4]{0:T(128)}, u32[]{:S(2)}) copy-start(s32[4]{0:T(128)} %owners.1) | copy-start | bytes 52
  13.4 0.7 %copy-start.9 = (s32[4]{0:T(128)S(1)}, s32[4]{0:T(128)}, u32[]{:S(2)}) copy-start(s32[4]{0:T(128)} %offsets.1) | copy-start | bytes 52
  14.0 5.6 %copy-start.5 = (f32[3200]{0:T(1024)S(1)}, f32[3200]{0:T(1024)}, u32[]{:S(2)}) copy-start(f32[3200]{0:T(1024)} %gain.3) | copy-start | bytes 38404
  14.0 13.4 %copy-start.6 = (f32[2048]{0:T(1024)S(1)}, f32[2048]{0:T(1024)}, u32[]{:S(2)}) copy-start(f32[2048]{0:T(1024)} %param.12) | copy-start | bytes 24580
  14.8 4.7 %copy-start = (bf16[3200,2048]{1,0:T(8,128)(2,1)S(1)}, bf16[3200,2048]{1,0:T(8,128)(2,1)}, u32[]{:S(2)}) copy-start(bf16[3200,2048]{1,0:T(8,128)(2,1)} %weight.7) | copy-start | bytes 39321604
  19.6 7.8 %copy-start.1 = (bf16[3200,2048]{1,0:T(8,128)(2,1)S(1)}, bf16[3200,2048]{1,0:T(8,128)(2,1)}, u32[]{:S(2)}) copy-start(bf16[3200,2048]{1,0:T(8,128)(2,1)} %weight.7) | copy-start | bytes 39321604
  19.8 12.3 %collective-permute-start.6 = (bf16[64,2176]{1,0:T(8,128)(2,1)S(1)}, bf16[64,2176]{1,0:T(8,128)(2,1)S(1)}, u32[]{:S(2)}, u32[]{:S(2)}) collective-permute-start(bf16[64,2176]{1,0:T(8,128)(2,1)S(1)} %get-tuple-element.34), channel_id=1, source_target_pairs={{0,2},{1,0},{2,3},{3,1},{4,6},{5,4},{6,7},{7,5},{8,10},{9,8},{10,1... | collective-permute-start | bytes 835592 | tf_op jit(solution)/shard_map/ppermute | solution.py:229
  19.9 13.9 %collective-permute-start = (bf16[64,128]{1,0:T(8,128)(2,1)S(1)}, bf16[64,128]{1,0:T(8,128)(2,1)S(1)}, u32[]{:S(2)}, u32[]{:S(2)}) collective-permute-start(bf16[64,128]{1,0:T(8,128)(2,1)S(1)} %get-tuple-element.27.i0), channel_id=1, source_target_pairs={{0,1},{1,0},{2,3},{3,2},{4,5},{5,4},{6,7},{7,6},{8,9},{9,8},{10,11... | collective-permute-start | bytes 49160 | tf_op jit(solution)/shard_map/ppermute | solution.py:209
  21.9 12.1 %collective-permute-start.1 = (bf16[64,128]{1,0:T(8,128)(2,1)S(1)}, bf16[64,128]{1,0:T(8,128)(2,1)S(1)}, u32[]{:S(2)}, u32[]{:S(2)}) collective-permute-start(bf16[64,128]{1,0:T(8,128)(2,1)S(1)} %get-tuple-element.27.i0), channel_id=1, source_target_pairs={{0,3},{1,2},{2,1},{3,0},{4,7},{5,6},{6,5},{7,4},{8,11},{9,10},{10,... | collective-permute-start | bytes 49160 | tf_op jit(solution)/shard_map/ppermute | solution.py:221
  24.4 11.6 %collective-permute-start.2 = (bf16[64,128]{1,0:T(8,128)(2,1)S(1)}, bf16[64,128]{1,0:T(8,128)(2,1)S(1)}, u32[]{:S(2)}, u32[]{:S(2)}) collective-permute-start(bf16[64,128]{1,0:T(8,128)(2,1)S(1)} %get-tuple-element.27.i0), channel_id=1, source_target_pairs={{0,2},{1,3},{2,0},{3,1},{4,6},{5,7},{6,4},{7,5},{8,10},{9,11},{10,... | collective-permute-start | bytes 49160 | tf_op jit(solution)/shard_map/ppermute | solution.py:225
  27.4 8.6 %collective-permute-start.5 = (bf16[64,1024]{1,0:T(8,128)(2,1)S(1)}, bf16[64,1024]{1,0:T(8,128)(2,1)S(1)}, u32[]{:S(2)}, u32[]{:S(2)}) collective-permute-start(bf16[64,1024]{1,0:T(8,128)(2,1)S(1)} %get-tuple-element.33), channel_id=1, source_target_pairs={{0,2},{1,0},{2,3},{3,1},{4,6},{5,4},{6,7},{7,5},{8,10},{9,8},{10,1... | collective-permute-start | bytes 393224 | tf_op jit(solution)/shard_map/ppermute | solution.py:229
  30.6 23.3 %copy-start.3 = (bf16[256,2048]{1,0:T(8,128)(2,1)S(1)}, bf16[256,2048]{1,0:T(8,128)(2,1)}, u32[]{:S(2)}) copy-start(bf16[256,2048]{1,0:T(8,128)(2,1)} %text.3) | copy-start | bytes 3145732
  30.7 23.2 %copy-start.7 = (f32[2048]{0:T(1024)S(1)}, f32[2048]{0:T(1024)}, u32[]{:S(2)}) copy-start(f32[2048]{0:T(1024)} %param.14) | copy-start | bytes 24580
  37.2 16.5 %collective-permute-start.10 = (bf16[64,2048]{1,0:T(8,128)(2,1)S(1)}, bf16[64,2048]{1,0:T(8,128)(2,1)S(1)}, u32[]{:S(2)}, u32[]{:S(2)}) collective-permute-start(bf16[64,2048]{1,0:T(8,128)(2,1)S(1)} %get-tuple-element.40), channel_id=1, source_target_pairs={{0,24},{4,28},{8,16},{12,20},{16,8},{20,12},{24,0},{28,4},{1,25},{... | collective-permute-start | bytes 786440 | tf_op jit(solution)/shard_map/ppermute | solution.py:233
  39.8 14.0 %collective-permute-start.8 = (bf16[64,2048]{1,0:T(8,128)(2,1)S(1)}, bf16[64,2048]{1,0:T(8,128)(2,1)S(1)}, u32[]{:S(2)}, u32[]{:S(2)}) collective-permute-start(bf16[64,2048]{1,0:T(8,128)(2,1)S(1)} %get-tuple-element.38), channel_id=1, source_target_pairs={{0,8},{4,12},{8,0},{12,4},{16,24},{20,28},{24,16},{28,20},{1,9},{5... | collective-permute-start | bytes 786440 | tf_op jit(solution)/shard_map/ppermute | solution.py:233
  40.3 13.5 %collective-permute-start.9 = (bf16[64,2048]{1,0:T(8,128)(2,1)S(1)}, bf16[64,2048]{1,0:T(8,128)(2,1)S(1)}, u32[]{:S(2)}, u32[]{:S(2)}) collective-permute-start(bf16[64,2048]{1,0:T(8,128)(2,1)S(1)} %get-tuple-element.39), channel_id=1, source_target_pairs={{0,16},{4,20},{8,24},{12,28},{16,0},{20,4},{24,8},{28,12},{1,17},{... | collective-permute-start | bytes 786440 | tf_op jit(solution)/shard_map/ppermute | solution.py:233
  53.8 2.0 %collective-permute-start.11 = (bf16[128,2048]{1,0:T(8,128)(2,1)S(1)}, bf16[128,2048]{1,0:T(8,128)(2,1)S(1)}, u32[]{:S(2)}, u32[]{:S(2)}) collective-permute-start(bf16[128,2048]{1,0:T(8,128)(2,1)S(1)} %pack.1), channel_id=1, source_target_pairs={{0,4},{4,0},{8,12},{12,8},{16,20},{20,16},{24,28},{28,24},{1,5},{5... | collective-permute-start | bytes 1572872 | tf_op jit(solution)/shard_map/ppermute | solution.py:233

commit v5 on v4

--- a/solution.py
+++ b/solution.py
@@ -80,7 +80,7 @@
     total[...] = jnp.dot(last[...], weight[:depth, :], preferred_element_type=F32) + bias[...]
 
 
-def project_kernel(groups, cap, size, i0, i1, i2, i3, last, weight, total, early, text_squares, *rest):
+def project_kernel(groups, cap, size, i3, i2, i1, i0, last, weight, total, early, text_squares, *rest):
     *parts, tiles, y, z, codes = rest
     me = lax.axis_index("grp")
     depth, columns = weight.shape
@@ -195,14 +195,23 @@
         base[part, :] = jnp.where(covered[part] > 0, moved[part], x).astype(BF16)
 
 
-def place_kernel(groups, cap, size, scales, gain, odd, base, order, out, rows):
-    g = gain[...]
-    for n, k in enumerate(range(1, groups, 2)):
-        at = n * cap * size
-        for r, x in enumerate(scaled(cap, size, k, odd[at : at + cap * size], scales, g)):
-            rows[at + r * size : at + (r + 1) * size, :] = x
-    moved = jnp.dot(order[...], rows[...], preferred_element_type=F32)
-    out[...] = (base[...].astype(F32) + moved).astype(BF16)
+def place_kernel(groups, cap, size, scales, gain, odd, base, order, out, rows, done, sems):
+    columns = out.shape[1]
+    block = columns // sems.shape[0]
+    copies = []
+    for c in range(sems.shape[0]):
+        part = slice(c * block, (c + 1) * block)
+        g = gain[:, part]
+        for n, k in enumerate(range(1, groups, 2)):
+            at = n * cap * size
+            for r, x in enumerate(scaled(cap, size, k, odd[at : at + cap * size, part], scales, g)):
+                rows[at + r * size : at + (r + 1) * size, part] = x
+        moved = jnp.dot(order[...], rows[:, part], preferred_element_type=F32)
+        done[:, part] = (base[:, part].astype(F32) + moved).astype(BF16)
+        copies.append(pltpu.make_async_copy(done.at[:, part], out.at[:, part], sems.at[c]))
+        copies[-1].start()
+    for copy in copies:
+        copy.wait()
 
 
 def outer(x):
@@ -280,7 +289,7 @@
     )(own, x_inner, vis_gain)
     sent, later, x_outer = lax.optimization_barrier((sent, later, x_outer))
     last_a = far(sent)
-    known = (info, outer(info), mirror(info), second(info))
+    known = (second(info), mirror(info), outer(info), info)
     last_b = far(later)
     cost = pl.CostEstimate(
         flops=2 * 3 * count * depth * columns, bytes_accessed=2 * weight.size, transcendentals=0
@@ -292,7 +301,7 @@
         out_shape=jax.ShapeDtypeStruct((3 * count, columns), BF16),
         scratch_shapes=[pltpu.VMEM((3 * count, depth), BF16)],
         compiler_params=small,
-        cost_estimate=cost,
+        cost_estimate=pl.CostEstimate(flops=0, bytes_accessed=0, transcendentals=0),
         name="early",
     )(own, x_outer, x_inner, x_ends, vis_gain, weight, bias)
     pairs = groups // 2
@@ -302,7 +311,7 @@
         out_specs=VMEM,
         out_shape=jax.ShapeDtypeStruct((count, columns), F32),
         compiler_params=small,
-        cost_estimate=cost,
+        cost_estimate=pl.CostEstimate(flops=0, bytes_accessed=0, transcendentals=0),
         name="late",
     )(last_a, weight, bias)
     *parts, squares = pl.pallas_call(
@@ -354,9 +363,13 @@
     return pl.pallas_call(
         functools.partial(place_kernel, groups, cap, size),
         in_specs=[VMEM] * 5,
-        out_specs=VMEM,
+        out_specs=ANY,
         out_shape=jax.ShapeDtypeStruct(text.shape, BF16),
-        scratch_shapes=[pltpu.VMEM(arrived.shape, BF16)],
+        scratch_shapes=[
+            pltpu.VMEM(arrived.shape, BF16),
+            pltpu.VMEM(text.shape, BF16),
+            pltpu.SemaphoreType.DMA((4,)),
+        ],
         compiler_params=small,
         name="place",
     )(scales, gain, odd, base, order)

time: 57.7 us -> 57.4 us (level)
    ppermute x2, starting transfers between devices: 0.06 us -> 3.08 us  [far(): return lax.ppermute(x, 'dp', [(0, 2), (1, 0), (2, 3), (3, 1)])]
    ppermute x2, starting transfers between devices: 6.93 us -> 4.92 us  [outer(): return lax.ppermute(x, 'dp', [(0, 1), (1, 0), (2, 3), (3, 2)])]
    ppermute x1, starting transfers between devices: 2.48 us -> 1.35 us  [mirror(): return lax.ppermute(x, 'dp', [(0, 3), (1, 2), (2, 1), (3, 0)])]
  transfers between devices with their start and end apart: 12 -> 12, of which waited for: 5 -> 4; matrix products, arithmetic and copies ran while one was open for 0% -> 0% of each run, Pallas kernels for 12% -> 12%
where the time goes in v5:
time: 57.4 us; the launch traced here: 57 us
  starting transfers between devices  17.9 us (31%)
  blocking collectives  13 us (23%)
  Pallas kernels  9.54 us (17%)
  local copies, waits for them, and re-layouts  8.28 us (14%)
  waiting for transfers between devices  7.5 us (13%)
  between operations  0.82 us (1%)
    all_to_all x1, blocking collectives, fast(): squares = lax.all_to_all(squares, ('grp', 'dp'), 0, 0, tiled=True)  13 us
    unnamed x20, local copies, waits for them, and re-layouts  8.28 us
    ppermute x2, starting transfers between devices, outer(): return lax.ppermute(x, 'dp', [(0, 1), (1, 0), (2, 3), (3, 2)])  4.92 us
    ppermute x4, starting transfers between devices, across(): lax.ppermute(x, 'grp', [(i, i ^ k) for i in range(lax.axis_size('grp'))])  3.62 us
    pallas_call x1, Pallas kernels, fast(): pl.pallas_call(early_kernel, in_specs=[VMEM] * 7, out_specs=VMEM, out_sha...  3.26 us
    ppermute x1, starting transfers between devices, ends(): return lax.ppermute(x, 'dp', [(0, 3), (3, 0), (1, 1), (2, 2)])  3.24 us
    ppermute x2, starting transfers between devices, far(): return lax.ppermute(x, 'dp', [(0, 2), (1, 0), (2, 3), (3, 1)])  3.08 us
    ppermute x1, waiting for transfers between devices, ends(): return lax.ppermute(x, 'dp', [(0, 3), (3, 0), (1, 1), (2, 2)])  3.05 us
  transfers between devices with their start and end apart: 12, of which 4 were waited for; matrix products, arithmetic and copies ran while one was open for 0% of the time, Pallas kernels for 12%

profile of v5, /device:TPU:0, one launch (start us, length us, event | category | flops | bytes accessed | tf_op | source)
XLA Modules:
  0.0 57.0 jit_solution(11591102629167377888)
XLA Ops:
  0.0 1.6 %collective-permute-start.3 = (bf16[64,3200]{1,0:T(8,128)(2,1)}, bf16[64,3200]{1,0:T(8,128)(2,1)S(1)}, u32[]{:S(2)}, u32[]{:S(2)}) collective-permute-start(bf16[64,3200]{1,0:T(8,128)(2,1)} %vis.1), channel_id=1, source_target_pairs={{1,2},{2,1},{0,0},{3,3},{5,6},{6,5},{4,4},{7,7},{9,10},{10,9},{8,8... | collective-permute-start | bytes 1228808 | tf_op jit(solution)/shard_map/ppermute | solution.py:222
  1.6 4.9 %collective-permute-start.4 = (bf16[64,3200]{1,0:T(8,128)(2,1)}, bf16[64,3200]{1,0:T(8,128)(2,1)S(1)}, u32[]{:S(2)}, u32[]{:S(2)}) collective-permute-start(bf16[64,3200]{1,0:T(8,128)(2,1)} %vis.1), channel_id=1, source_target_pairs={{0,1},{1,0},{2,3},{3,2},{4,5},{5,4},{6,7},{7,6},{8,9},{9,8},{10,11... | collective-permute-start | bytes 1228808 | tf_op jit(solution)/shard_map/ppermute | solution.py:218
  6.6 3.2 %collective-permute-start.7 = (bf16[64,3200]{1,0:T(8,128)(2,1)}, bf16[64,3200]{1,0:T(8,128)(2,1)S(1)}, u32[]{:S(2)}, u32[]{:S(2)}) collective-permute-start(bf16[64,3200]{1,0:T(8,128)(2,1)} %vis.1), channel_id=1, source_target_pairs={{0,3},{3,0},{1,1},{2,2},{4,7},{7,4},{5,5},{6,6},{8,11},{11,8},{9,9... | collective-permute-start | bytes 1228808 | tf_op jit(solution)/shard_map/ppermute | solution.py:226
  10.5 0.0 copy-start.2
  10.5 1.2 %copy-done.2 = bf16[256,2048]{1,0:T(8,128)(2,1)S(1)} copy-done((bf16[256,2048]{1,0:T(8,128)(2,1)S(1)}, bf16[256,2048]{1,0:T(8,128)(2,1)}, u32[]{:S(2)}) %copy-start.2) | copy-done | bytes 1048600
  11.7 0.0 copy-start.4
  11.7 1.0 %copy-done.4 = bf16[64,3200]{1,0:T(8,128)(2,1)S(1)} copy-done((bf16[64,3200]{1,0:T(8,128)(2,1)S(1)}, bf16[64,3200]{1,0:T(8,128)(2,1)}, u32[]{:S(2)}) %copy-start.4) | copy-done | bytes 409624
  12.7 0.0 copy-start.8
  12.7 0.7 %copy-done.8 = s32[4]{0:T(128)S(1)} copy-done((s32[4]{0:T(128)S(1)}, s32[4]{0:T(128)}, u32[]{:S(2)}) %copy-start.8) | copy-done | bytes 40
  13.4 0.0 copy-start.9
  13.4 0.7 %copy-done.9 = s32[4]{0:T(128)S(1)} copy-done((s32[4]{0:T(128)S(1)}, s32[4]{0:T(128)}, u32[]{:S(2)}) %copy-start.9) | copy-done | bytes 40
  14.0 0.0 copy-start.5
  14.0 0.0 copy-start.6
  14.0 0.8 %tables.1 = (f32[8,128]{1,0:T(8,128)S(1)}, bf16[64,128]{1,0:T(8,128)(2,1)S(1)}, bf16[64,3200]{1,0:T(8,128)(2,1)S(1)}) custom-call(bf16[256,2048]{1,0:T(8,128)(2,1)S(1)} %copy-done.2, bf16[64,3200]{1,0:T(8,128)(2,1)S(1)} %copy-done.4, s32[4]{0:T(128)S(1)} %copy-done.8, s32[4]{0:T(128)S(1)} %copy-done.9, s32[1]{0:T(128)S(6)} %copy.10.counts), custom_call_target="tpu_custom_call" | custom-call | tf_op jit(solution)/shard_map/tables/pallas_call | solution.py:259
  14.8 0.0 copy-start
  14.8 4.7 %copy-done = bf16[3200,2048]{1,0:T(8,128)(2,1)S(1)} copy-done((bf16[3200,2048]{1,0:T(8,128)(2,1)S(1)}, bf16[3200,2048]{1,0:T(8,128)(2,1)}, u32[]{:S(2)}) %copy-start) | copy-done | bytes 13107224
  19.6 0.0 copy-start.1
  19.6 0.0 collective-permute-done.3.inner
  19.6 0.0 copy-done.5
  19.6 0.2 pass.1
  19.8 0.0 collective-permute-done.4.outer
  19.8 0.1 collective-permute-start.6
  19.9 3.0 %collective-permute-start.5 = (bf16[64,1024]{1,0:T(8,128)(2,1)S(1)}, bf16[64,1024]{1,0:T(8,128)(2,1)S(1)}, u32[]{:S(2)}, u32[]{:S(2)}) collective-permute-start(bf16[64,1024]{1,0:T(8,128)(2,1)S(1)} %get-tuple-element.33), channel_id=1, source_target_pairs={{0,2},{1,0},{2,3},{3,1},{4,6},{5,4},{6,7},{7,5},{8,10},{9,8},{10,1... | collective-permute-start | bytes 393224 | tf_op jit(solution)/shard_map/ppermute | solution.py:238
  22.9 0.1 collective-permute-start
  23.0 1.3 %collective-permute-start.1 = (bf16[64,128]{1,0:T(8,128)(2,1)S(1)}, bf16[64,128]{1,0:T(8,128)(2,1)S(1)}, u32[]{:S(2)}, u32[]{:S(2)}) collective-permute-start(bf16[64,128]{1,0:T(8,128)(2,1)S(1)} %get-tuple-element.27.i0), channel_id=1, source_target_pairs={{0,3},{1,2},{2,1},{3,0},{4,7},{5,6},{6,5},{7,4},{8,11},{9,10},{10,... | collective-permute-start | bytes 49160 | tf_op jit(solution)/shard_map/ppermute | solution.py:230
  24.3 3.0 %collective-permute-done.7.ends = bf16[64,3200]{1,0:T(8,128)(2,1)S(1)} collective-permute-done((bf16[64,3200]{1,0:T(8,128)(2,1)}, bf16[64,3200]{1,0:T(8,128)(2,1)S(1)}, u32[]{:S(2)}, u32[]{:S(2)}) %collective-permute-start.7) | collective-permute-done | bytes 409632 | tf_op jit(solution)/shard_map/ppermute | solution.py:226
  27.4 0.0 collective-permute-start.2
  27.4 0.0 copy-done.6
  27.4 0.0 copy-done.1
  27.4 3.3 %early.1 = bf16[192,2048]{1,0:T(8,128)(2,1)S(1)} custom-call(bf16[64,3200]{1,0:T(8,128)(2,1)S(1)} %get-tuple-element.28.own, bf16[64,3200]{1,0:T(8,128)(2,1)S(1)} %collective-permute-done.4.outer, bf16[64,3200]{1,0:T(8,128)(2,1)S(1)} %collective-permute-done.3.inner, bf16[64,3200]{1,0:T(8,128)(2,1)S(1)} %collective-permute-done.7.ends, f32[3200]{0:T(1024)S(1)} %copy-done.5, ...), custom_call_target="tpu_custom_call" | custom-call | tf_op jit(solution)/shard_map/early/pallas_call | solution.py:297
  30.6 0.0 copy-start.3
  30.7 0.0 copy-start.7
  30.7 1.2 %collective-permute-done.6.last = bf16[64,2176]{1,0:T(8,128)(2,1)S(1)} collective-permute-done((bf16[64,2176]{1,0:T(8,128)(2,1)S(1)}, bf16[64,2176]{1,0:T(8,128)(2,1)S(1)}, u32[]{:S(2)}, u32[]{:S(2)}) %collective-permute-start.6) | collective-permute-done | bytes 278560 | tf_op jit(solution)/shard_map/ppermute | solution.py:238
  31.9 1.7 %late.1.total = f32[64,2048]{1,0:T(8,128)S(1)} custom-call(bf16[64,2176]{1,0:T(8,128)(2,1)S(1)} %collective-permute-done.6.last, bf16[3200,2048]{1,0:T(8,128)(2,1)S(1)} %copy-done.1, f32[1,2048]{1,0:T(1,128)S(1)} %bitcast.7), custom_call_target="tpu_custom_call" | custom-call | tf_op jit(solution)/shard_map/late/pallas_call | solution.py:308
  33.6 2.1 %collective-permute-done.i3 = bf16[64,128]{1,0:T(8,128)(2,1)S(1)} collective-permute-done((bf16[64,128]{1,0:T(8,128)(2,1)S(1)}, bf16[64,128]{1,0:T(8,128)(2,1)S(1)}, u32[]{:S(2)}, u32[]{:S(2)}) %collective-permute-start) | collective-permute-done | bytes 16416 | tf_op jit(solution)/shard_map/ppermute | solution.py:234
  35.7 0.0 collective-permute-done.1.i2
  35.7 0.0 collective-permute-done.2.i1
  35.7 0.0 collective-permute-done.5.last
  35.7 1.2 %project.1 = (bf16[64,2048]{1,0:T(8,128)(2,1)S(1)}, bf16[64,2048]{1,0:T(8,128)(2,1)S(1)}, bf16[64,2048]{1,0:T(8,128)(2,1)S(1)}, bf16[64,2048]{1,0:T(8,128)(2,1)S(1)}, f32[256,128]{1,0:T(8,128)S(1)}) custom-call(bf16[64,128]{1,0:T(8,128)(2,1)S(1)} %collective-permute-done.i3, bf16[64,128]{1,0:T(8,128)(2,1)S(1)} %collective-permute-done.1.i2, ...), custom_call_target="tpu_custom_call" | custom-call | flops 2516582400 | bytes 13107200 | tf_op jit(solution)/shard_map/project/pallas_call | solution.py:317
  37.0 2.5 %collective-permute-start.10 = (bf16[64,2048]{1,0:T(8,128)(2,1)S(1)}, bf16[64,2048]{1,0:T(8,128)(2,1)S(1)}, u32[]{:S(2)}, u32[]{:S(2)}) collective-permute-start(bf16[64,2048]{1,0:T(8,128)(2,1)S(1)} %get-tuple-element.40), channel_id=1, source_target_pairs={{0,24},{4,28},{8,16},{12,20},{16,8},{20,12},{24,0},{28,4},{1,25},{... | collective-permute-start | bytes 786440 | tf_op jit(solution)/shard_map/ppermute | solution.py:242
  39.5 0.5 collective-permute-start.8
  40.0 0.5 collective-permute-start.9
  40.5 13.0 %all_to_all.11 = f32[32,8,128]{2,1,0:T(8,128)S(1)} all-to-all(f32[32,8,128]{2,1,0:T(8,128)S(1)} %bitcast.5), channel_id=1, replica_groups=mesh['grp'=8,'dp'=4] {'grp','dp'}, dimensions={0} | all-to-all | bytes 262144 | tf_op jit(solution)/shard_map/all_to_all | solution.py:332
  53.5 0.0 collective-permute-done.10.refs_3_.rest_3_
  53.6 0.0 collective-permute-done.8.refs_1_.rest_1_
  53.6 0.0 collective-permute-done.9.refs_2_.rest_2_
  53.6 0.1 collective-permute-start.11
  53.7 0.0 copy-done.3
  53.7 0.0 copy-done.7
  53.7 0.8 %base.1 = (bf16[256,2048]{1,0:T(8,128)(2,1)S(1)}, bf16[256,128]{1,0:T(8,128)(2,1)S(1)}) custom-call(f32[64,128]{1,0:T(8,128)S(1)} %scale.1.scales, f32[1,2048]{1,0:T(1,128)S(1)} %bitcast.8, bf16[256,2048]{1,0:T(8,128)(2,1)S(1)} %copy-done.3, bf16[64,2048]{1,0:T(8,128)(2,1)S(1)} %get-tuple-element.43.refs_0_.rest_0_, ...), custom_call_target="tpu_custom_call" | custom-call | bytes 13107200 | tf_op jit(solution)/shard_map/base/pallas_call | solution.py:350
  54.5 1.1 %collective-permute-done.11.odd = bf16[128,2048]{1,0:T(8,128)(2,1)S(1)} collective-permute-done((bf16[128,2048]{1,0:T(8,128)(2,1)S(1)}, bf16[128,2048]{1,0:T(8,128)(2,1)S(1)}, u32[]{:S(2)}, u32[]{:S(2)}) %collective-permute-start.11) | collective-permute-done | bytes 524320 | tf_op jit(solution)/shard_map/ppermute | solution.py:242
  55.6 1.4 %place.1 = bf16[256,2048]{1,0:T(8,128)(2,1)} custom-call(f32[64,128]{1,0:T(8,128)S(1)} %scale.1.scales, f32[1,2048]{1,0:T(1,128)S(1)} %bitcast.9, bf16[128,2048]{1,0:T(8,128)(2,1)S(1)} %collective-permute-done.11.odd, bf16[256,2048]{1,0:T(8,128)(2,1)S(1)} %get-tuple-element.47.base, bf16[256,128]{1,0:T(8,128)(2,1)S(1)} %get-tuple-element.48.order), custom_call_target="tpu_custom_call" | custom-call | tf_op jit(solution)/shard_map/place/pallas_call | solution.py:363
  (3 shorter events, 0.1 us)
Async XLA Ops:
  0.0 19.6 %collective-permute-start.3 = (bf16[64,3200]{1,0:T(8,128)(2,1)}, bf16[64,3200]{1,0:T(8,128)(2,1)S(1)}, u32[]{:S(2)}, u32[]{:S(2)}) collective-permute-start(bf16[64,3200]{1,0:T(8,128)(2,1)} %vis.1), channel_id=1, source_target_pairs={{1,2},{2,1},{0,0},{3,3},{5,6},{6,5},{4,4},{7,7},{9,10},{10,9},{8,8... | collective-permute-start | bytes 1228808 | tf_op jit(solution)/shard_map/ppermute | solution.py:222
  1.6 18.2 %collective-permute-start.4 = (bf16[64,3200]{1,0:T(8,128)(2,1)}, bf16[64,3200]{1,0:T(8,128)(2,1)S(1)}, u32[]{:S(2)}, u32[]{:S(2)}) collective-permute-start(bf16[64,3200]{1,0:T(8,128)(2,1)} %vis.1), channel_id=1, source_target_pairs={{0,1},{1,0},{2,3},{3,2},{4,5},{5,4},{6,7},{7,6},{8,9},{9,8},{10,11... | collective-permute-start | bytes 1228808 | tf_op jit(solution)/shard_map/ppermute | solution.py:218
  6.6 20.8 %collective-permute-start.7 = (bf16[64,3200]{1,0:T(8,128)(2,1)}, bf16[64,3200]{1,0:T(8,128)(2,1)S(1)}, u32[]{:S(2)}, u32[]{:S(2)}) collective-permute-start(bf16[64,3200]{1,0:T(8,128)(2,1)} %vis.1), channel_id=1, source_target_pairs={{0,3},{3,0},{1,1},{2,2},{4,7},{7,4},{5,5},{6,6},{8,11},{11,8},{9,9... | collective-permute-start | bytes 1228808 | tf_op jit(solution)/shard_map/ppermute | solution.py:226
  10.5 1.2 %copy-start.2 = (bf16[256,2048]{1,0:T(8,128)(2,1)S(1)}, bf16[256,2048]{1,0:T(8,128)(2,1)}, u32[]{:S(2)}) copy-start(bf16[256,2048]{1,0:T(8,128)(2,1)} %text.3) | copy-start | bytes 3145732
  11.7 1.0 %copy-start.4 = (bf16[64,3200]{1,0:T(8,128)(2,1)S(1)}, bf16[64,3200]{1,0:T(8,128)(2,1)}, u32[]{:S(2)}) copy-start(bf16[64,3200]{1,0:T(8,128)(2,1)} %vis.1) | copy-start | bytes 1228804
  12.7 0.7 %copy-start.8 = (s32[4]{0:T(128)S(1)}, s32[4]{0:T(128)}, u32[]{:S(2)}) copy-start(s32[4]{0:T(128)} %owners.1) | copy-start | bytes 52
  13.4 0.7 %copy-start.9 = (s32[4]{0:T(128)S(1)}, s32[4]{0:T(128)}, u32[]{:S(2)}) copy-start(s32[4]{0:T(128)} %offsets.1) | copy-start | bytes 52
  14.0 5.6 %copy-start.5 = (f32[3200]{0:T(1024)S(1)}, f32[3200]{0:T(1024)}, u32[]{:S(2)}) copy-start(f32[3200]{0:T(1024)} %gain.3) | copy-start | bytes 38404
  14.0 13.4 %copy-start.6 = (f32[2048]{0:T(1024)S(1)}, f32[2048]{0:T(1024)}, u32[]{:S(2)}) copy-start(f32[2048]{0:T(1024)} %param.12) | copy-start | bytes 24580
  14.8 4.7 %copy-start = (bf16[3200,2048]{1,0:T(8,128)(2,1)S(1)}, bf16[3200,2048]{1,0:T(8,128)(2,1)}, u32[]{:S(2)}) copy-start(bf16[3200,2048]{1,0:T(8,128)(2,1)} %weight.7) | copy-start | bytes 39321604
  19.6 7.8 %copy-start.1 = (bf16[3200,2048]{1,0:T(8,128)(2,1)S(1)}, bf16[3200,2048]{1,0:T(8,128)(2,1)}, u32[]{:S(2)}) copy-start(bf16[3200,2048]{1,0:T(8,128)(2,1)} %weight.7) | copy-start | bytes 39321604
  19.8 12.1 %collective-permute-start.6 = (bf16[64,2176]{1,0:T(8,128)(2,1)S(1)}, bf16[64,2176]{1,0:T(8,128)(2,1)S(1)}, u32[]{:S(2)}, u32[]{:S(2)}) collective-permute-start(bf16[64,2176]{1,0:T(8,128)(2,1)S(1)} %get-tuple-element.34), channel_id=1, source_target_pairs={{0,2},{1,0},{2,3},{3,1},{4,6},{5,4},{6,7},{7,5},{8,10},{9,8},{10,1... | collective-permute-start | bytes 835592 | tf_op jit(solution)/shard_map/ppermute | solution.py:238
  19.9 15.9 %collective-permute-start.5 = (bf16[64,1024]{1,0:T(8,128)(2,1)S(1)}, bf16[64,1024]{1,0:T(8,128)(2,1)S(1)}, u32[]{:S(2)}, u32[]{:S(2)}) collective-permute-start(bf16[64,1024]{1,0:T(8,128)(2,1)S(1)} %get-tuple-element.33), channel_id=1, source_target_pairs={{0,2},{1,0},{2,3},{3,1},{4,6},{5,4},{6,7},{7,5},{8,10},{9,8},{10,1... | collective-permute-start | bytes 393224 | tf_op jit(solution)/shard_map/ppermute | solution.py:238
  22.9 12.8 %collective-permute-start = (bf16[64,128]{1,0:T(8,128)(2,1)S(1)}, bf16[64,128]{1,0:T(8,128)(2,1)S(1)}, u32[]{:S(2)}, u32[]{:S(2)}) collective-permute-start(bf16[64,128]{1,0:T(8,128)(2,1)S(1)} %get-tuple-element.27.i0), channel_id=1, source_target_pairs={{0,2},{1,3},{2,0},{3,1},{4,6},{5,7},{6,4},{7,5},{8,10},{9,11},{10,... | collective-permute-start | bytes 49160 | tf_op jit(solution)/shard_map/ppermute | solution.py:234
  23.0 12.8 %collective-permute-start.1 = (bf16[64,128]{1,0:T(8,128)(2,1)S(1)}, bf16[64,128]{1,0:T(8,128)(2,1)S(1)}, u32[]{:S(2)}, u32[]{:S(2)}) collective-permute-start(bf16[64,128]{1,0:T(8,128)(2,1)S(1)} %get-tuple-element.27.i0), channel_id=1, source_target_pairs={{0,3},{1,2},{2,1},{3,0},{4,7},{5,6},{6,5},{7,4},{8,11},{9,10},{10,... | collective-permute-start | bytes 49160 | tf_op jit(solution)/shard_map/ppermute | solution.py:230
  27.4 8.4 %collective-permute-start.2 = (bf16[64,128]{1,0:T(8,128)(2,1)S(1)}, bf16[64,128]{1,0:T(8,128)(2,1)S(1)}, u32[]{:S(2)}, u32[]{:S(2)}) collective-permute-start(bf16[64,128]{1,0:T(8,128)(2,1)S(1)} %get-tuple-element.27.i0), channel_id=1, source_target_pairs={{0,1},{1,0},{2,3},{3,2},{4,5},{5,4},{6,7},{7,6},{8,9},{9,8},{10,11... | collective-permute-start | bytes 49160 | tf_op jit(solution)/shard_map/ppermute | solution.py:218
  30.6 23.0 %copy-start.3 = (bf16[256,2048]{1,0:T(8,128)(2,1)S(1)}, bf16[256,2048]{1,0:T(8,128)(2,1)}, u32[]{:S(2)}) copy-start(bf16[256,2048]{1,0:T(8,128)(2,1)} %text.3) | copy-start | bytes 3145732
  30.7 23.0 %copy-start.7 = (f32[2048]{0:T(1024)S(1)}, f32[2048]{0:T(1024)}, u32[]{:S(2)}) copy-start(f32[2048]{0:T(1024)} %param.14) | copy-start | bytes 24580
  37.0 16.6 %collective-permute-start.10 = (bf16[64,2048]{1,0:T(8,128)(2,1)S(1)}, bf16[64,2048]{1,0:T(8,128)(2,1)S(1)}, u32[]{:S(2)}, u32[]{:S(2)}) collective-permute-start(bf16[64,2048]{1,0:T(8,128)(2,1)S(1)} %get-tuple-element.40), channel_id=1, source_target_pairs={{0,24},{4,28},{8,16},{12,20},{16,8},{20,12},{24,0},{28,4},{1,25},{... | collective-permute-start | bytes 786440 | tf_op jit(solution)/shard_map/ppermute | solution.py:242
  39.5 14.0 %collective-permute-start.8 = (bf16[64,2048]{1,0:T(8,128)(2,1)S(1)}, bf16[64,2048]{1,0:T(8,128)(2,1)S(1)}, u32[]{:S(2)}, u32[]{:S(2)}) collective-permute-start(bf16[64,2048]{1,0:T(8,128)(2,1)S(1)} %get-tuple-element.38), channel_id=1, source_target_pairs={{0,8},{4,12},{8,0},{12,4},{16,24},{20,28},{24,16},{28,20},{1,9},{5... | collective-permute-start | bytes 786440 | tf_op jit(solution)/shard_map/ppermute | solution.py:242
  40.0 13.5 %collective-permute-start.9 = (bf16[64,2048]{1,0:T(8,128)(2,1)S(1)}, bf16[64,2048]{1,0:T(8,128)(2,1)S(1)}, u32[]{:S(2)}, u32[]{:S(2)}) collective-permute-start(bf16[64,2048]{1,0:T(8,128)(2,1)S(1)} %get-tuple-element.39), channel_id=1, source_target_pairs={{0,16},{4,20},{8,24},{12,28},{16,0},{20,4},{24,8},{28,12},{1,17},{... | collective-permute-start | bytes 786440 | tf_op jit(solution)/shard_map/ppermute | solution.py:242
  53.6 2.0 %collective-permute-start.11 = (bf16[128,2048]{1,0:T(8,128)(2,1)S(1)}, bf16[128,2048]{1,0:T(8,128)(2,1)S(1)}, u32[]{:S(2)}, u32[]{:S(2)}) collective-permute-start(bf16[128,2048]{1,0:T(8,128)(2,1)S(1)} %pack.1), channel_id=1, source_target_pairs={{0,4},{4,0},{8,12},{12,8},{16,20},{20,16},{24,28},{28,24},{1,5},{5... | collective-permute-start | bytes 1572872 | tf_op jit(solution)/shard_map/ppermute | solution.py:242

commit v6 on v5

--- a/solution.py
+++ b/solution.py
@@ -10,6 +10,7 @@
 EPS_VIS = 1e-06
 EPS_OUT = 1e-05
 TILE = (8, 128)
+TEXT = 64
 F32 = jnp.float32
 BF16 = jnp.bfloat16
 VMEM = pl.BlockSpec(memory_space=pltpu.VMEM)
@@ -22,7 +23,7 @@
     return lax.broadcasted_iota(jnp.int32, TILE, 1)
 
 
-def tables_kernel(slots, size, text, vis, owners, offsets, counts, squares, info, own):
+def tables_kernel(slots, size, text, vis, owners, offsets, counts, info, own, squares):
     lane = lanes()
     tile = jnp.zeros(TILE, F32)
     for c in range(text.shape[0] // 16):
@@ -32,12 +33,23 @@
         tile = jnp.where(lane == 2 * c + 1, sums[8:], tile)
     squares[...] = tile
     row = lax.axis_index("dp")
-    lane = lax.broadcasted_iota(jnp.int32, (size, 128), 1)
+    known = jnp.zeros(TILE, jnp.int32)
     for i in range(slots):
         code = jnp.where(i < counts[0], offsets[i] // size + 1, 0)
-        known = jnp.where(lane == 0, owners[i], jnp.where(lane == 1, row * slots + i, jnp.where(lane == 2, code, 0)))
-        info[i * size : (i + 1) * size, :] = known.astype(F32).astype(BF16)
+        for n, value in enumerate((owners[i], row * slots + i, code)):
+            known = jnp.where(lane == n * slots + i, value, known)
+    info[...] = known.astype(F32) + pltpu.roll(tile, TEXT, 1)
     own[...] = vis[...]
+
+
+def spread(slots, size, tiles):
+    lane = lax.broadcasted_iota(jnp.int32, (size, 128), 1)
+    rows = []
+    for tile in tiles:
+        for i in range(slots):
+            owner, slot, code = [tile[0:1, n * slots + i : n * slots + i + 1] for n in range(3)]
+            rows.append(jnp.where(lane == 0, owner, jnp.where(lane == 1, slot, jnp.where(lane == 2, code, 0))))
+    return jnp.concatenate(rows, axis=0)
 
 
 def pass_kernel(own, inner, gain, sent, later):
@@ -80,12 +92,12 @@
     total[...] = jnp.dot(last[...], weight[:depth, :], preferred_element_type=F32) + bias[...]
 
 
-def project_kernel(groups, cap, size, i3, i2, i1, i0, last, weight, total, early, text_squares, *rest):
-    *parts, tiles, y, z, codes = rest
+def project_kernel(groups, cap, size, width, i3, i2, i1, i0, last, weight, total, early, text, *rest):
+    *parts, tiles, text_scale, y, z, codes = rest
     me = lax.axis_index("grp")
     depth, columns = weight.shape
     stretch = last.shape[1]
-    down = jnp.concatenate([i0[...], i1[...], i2[...], i3[...]], axis=0).astype(F32)
+    down = spread(last.shape[0] // size, size, [i0[...], i1[...], i2[...], i3[...]])
     rows = down.shape[0]
     across = down.T
     owner_down, slot_down = down[:, 0:1], down[:, 1:2]
@@ -115,32 +127,38 @@
     for m, part in enumerate(parts):
         part[...] = y[m * chunk : (m + 1) * chunk]
     lane = lanes()
-    copies = tiles.shape[0] // (8 * groups)
+    others = pltpu.roll(i1[...] + i2[...] + i3[...], 128 - TEXT, 1)
+    text_scale[...] = lax.rsqrt((text[...] + others) / width + EPS_OUT)
+    columns = []
     for k in range(groups):
-        tile = jnp.zeros(TILE, F32)
-        for r in range(cap):
-            start = (k * cap + r) * size
-            wide = y[start : start + size, :].astype(F32)
-            tile = jnp.where(lane == 2 * cap + r, codes[start : start + 8, 2:3], tile)
-            sums = jnp.sum(wide * wide, axis=1, keepdims=True)
-            tile = jnp.where(lane == 2 * r, sums[:8], jnp.where(lane == 2 * r + 1, sums[8:], tile))
-        if k == 0:
-            tile = jnp.where(lane < 3 * cap, tile, pltpu.roll(text_squares[...], 3 * cap, 1))
+        wide = y[k * cap * size : (k + 1) * cap * size, :].astype(F32)
+        sums = jnp.sum(wide * wide, axis=1, keepdims=True)
+        code = [codes[(k * cap + r) * size : (k * cap + r) * size + 1, 2:3] for r in range(cap)]
+        fill = jnp.zeros((128 - cap * size - cap, 1), F32)
+        columns.append(jnp.concatenate([sums, *code, fill], axis=0))
+    lane = lax.broadcasted_iota(jnp.int32, (128, 128), 1)
+    told = jnp.zeros((128, 128), F32)
+    for k in range(groups):
+        told = jnp.where(lane == k, columns[k], told)
+    told = told.T
+    copies = tiles.shape[0] // groups
+    for k in range(groups):
         for q in range(copies):
-            tiles[pl.ds(pl.multiple_of(((me ^ k) * copies + q) * 8, 8), 8), :] = tile
-
-
-def scale_kernel(groups, dp, cap, width, squares, scales):
+            tiles[pl.ds((me ^ k) * copies + q, 1), :] = told[k : k + 1, :]
+
+
+def scale_kernel(groups, dp, rows, width, squares, scales):
     me = lax.axis_index("grp")
-    lane = lanes()
-    is_code = jnp.logical_and(lane >= 2 * cap, lane < 3 * cap)
+    source = lax.broadcasted_iota(jnp.int32, squares.shape, 0)
+    lane = lax.broadcasted_iota(jnp.int32, (1, 128), 1)
+    told = []
     for k in range(groups):
-        base = (me ^ k) * (dp * 8)
-        tile = squares[pl.ds(pl.multiple_of(base, 8), 8), :]
-        code = tile
-        for d in range(1, dp):
-            tile = tile + squares[pl.ds(pl.multiple_of(base + d * 8, 8), 8), :]
-        scales[k * 8 : (k + 1) * 8, :] = jnp.where(is_code, code, lax.rsqrt(tile / width + EPS_OUT))
+        mine = source // dp == (me ^ k)
+        total = jnp.sum(jnp.where(mine, squares[...], 0), axis=0, keepdims=True)
+        code = jnp.sum(jnp.where(source == (me ^ k) * dp, squares[...], 0), axis=0, keepdims=True)
+        told.append(jnp.where(lane < rows, lax.rsqrt(total / width + EPS_OUT), code))
+    told.append(jnp.zeros((128 - groups, 128), F32))
+    scales[...] = jnp.concatenate(told, axis=0).T
 
 
 def pack_kernel(*refs):
@@ -151,18 +169,17 @@
 
 
 def scaled(cap, size, k, rows, scales, gain):
-    scale = scales[k * 8 : (k + 1) * 8, :]
     out = []
     for r in range(cap):
-        inverse = jnp.concatenate([scale[:, 2 * r : 2 * r + 1], scale[:, 2 * r + 1 : 2 * r + 2]], axis=0)
+        inverse = scales[r * size : (r + 1) * size, k : k + 1]
         out.append((rows[r * size : (r + 1) * size, :].astype(F32) * inverse * gain).astype(BF16))
     return out
 
 
 def moves(seq_len, cap, size, senders, scales):
-    lane = 2 * cap
+    at = cap * size
     codes = [
-        jnp.broadcast_to(scales[k * 8 : (k + 1) * 8, lane + r : lane + r + 1], TILE)
+        jnp.broadcast_to(scales[at + r : at + r + 1, k : k + 1], TILE)
         for k in senders
         for r in range(cap)
         for _ in range(size // 8)
@@ -173,7 +190,7 @@
     return (lax.broadcasted_iota(jnp.int32, (seq_len, code.shape[1]), 0) == target).astype(F32)
 
 
-def base_kernel(groups, cap, size, scales, gain, text, *rest):
+def base_kernel(groups, cap, size, scales, text_scale, gain, text, *rest):
     *even, base, order_odd, rows = rest
     seq_len = text.shape[0]
     g = gain[...]
@@ -186,10 +203,8 @@
             at = (n * cap + r) * size
             rows[at : at + size, :] = x
     moved = jnp.dot(order.astype(BF16), rows[...], preferred_element_type=F32)
-    own = scales[0:8, :]
     for c in range(seq_len // 16):
-        at = 3 * cap + 2 * c
-        inverse = jnp.concatenate([own[:, at : at + 1], own[:, at + 1 : at + 2]], axis=0)
+        inverse = jnp.concatenate([text_scale[:, 2 * c : 2 * c + 1], text_scale[:, 2 * c + 1 : 2 * c + 2]], axis=0)
         part = slice(c * 16, (c + 1) * 16)
         x = text[part, :].astype(F32) * inverse * g
         base[part, :] = jnp.where(covered[part] > 0, moved[part], x).astype(BF16)
@@ -256,17 +271,17 @@
     bias = bias[None, :]
 
     x_inner, x_outer = inner(vis), outer(vis)
-    text_squares, info, own = pl.pallas_call(
+    info, own, held = pl.pallas_call(
         functools.partial(tables_kernel, slots, size),
         in_specs=[VMEM, VMEM, SMEM, SMEM, SMEM],
         out_specs=[VMEM] * 3,
-        out_shape=[tile, jax.ShapeDtypeStruct((count, 128), BF16), jax.ShapeDtypeStruct(vis.shape, BF16)],
+        out_shape=[tile, jax.ShapeDtypeStruct(vis.shape, BF16), tile],
         compiler_params=small,
         name="tables",
     )(text, vis, owners, offsets, counts)
     x_ends = ends(vis)
     weight = pltpu.with_memory_space_constraint(weight, pltpu.VMEM)
-    text_squares = pl.pallas_call(
+    held = pl.pallas_call(
         hold_kernel,
         in_specs=[ANY, VMEM],
         out_specs=VMEM,
@@ -274,8 +289,8 @@
         compiler_params=small,
         cost_estimate=pl.CostEstimate(flops=0, bytes_accessed=2 * weight.size, transcendentals=0),
         name="hold",
-    )(weight, text_squares)
-    x_inner, text_squares = lax.optimization_barrier((x_inner, text_squares))
+    )(weight, held)
+    x_inner, held = lax.optimization_barrier((x_inner, held))
     stretches = depth // 3 // 128 * 128
     stretches = (depth - stretches, stretches)
     stretch = depth // 3 // 128 * 128
@@ -314,12 +329,12 @@
         cost_estimate=pl.CostEstimate(flops=0, bytes_accessed=0, transcendentals=0),
         name="late",
     )(last_a, weight, bias)
-    *parts, squares = pl.pallas_call(
-        functools.partial(project_kernel, groups, cap, size),
+    *parts, squares, text_scale = pl.pallas_call(
+        functools.partial(project_kernel, groups, cap, size, columns * dp),
         in_specs=[VMEM] * 9,
-        out_specs=[VMEM] * (pairs + 1),
+        out_specs=[VMEM] * (pairs + 2),
         out_shape=[jax.ShapeDtypeStruct((2 * cap * size, columns), BF16)] * pairs
-        + [jax.ShapeDtypeStruct((devices * 8, 128), F32)],
+        + [jax.ShapeDtypeStruct((devices, 128), F32), tile],
         scratch_shapes=[
             pltpu.VMEM((dp * count, columns), BF16),
             pltpu.VMEM((count, columns), BF16),
@@ -328,13 +343,13 @@
         compiler_params=small,
         cost_estimate=cost,
         name="project",
-    )(*known, last_b, weight, total, early, text_squares)
+    )(*known, last_b, weight, total, early, held)
     squares = lax.all_to_all(squares, ("grp", "dp"), 0, 0, tiled=True)
     scales = pl.pallas_call(
-        functools.partial(scale_kernel, groups, dp, cap, columns * dp),
+        functools.partial(scale_kernel, groups, dp, cap * size, columns * dp),
         in_specs=[VMEM],
         out_specs=VMEM,
-        out_shape=jax.ShapeDtypeStruct((groups * 8, 128), F32),
+        out_shape=jax.ShapeDtypeStruct((128, 128), F32),
         compiler_params=small,
         cost_estimate=pl.CostEstimate(flops=0, bytes_accessed=4 * weight.size, transcendentals=0),
         name="scale",
@@ -349,7 +364,7 @@
     gain = out_gain[None, :]
     base, order = pl.pallas_call(
         functools.partial(base_kernel, groups, cap, size),
-        in_specs=[VMEM] * (3 + pairs),
+        in_specs=[VMEM] * (4 + pairs),
         out_specs=[VMEM] * 2,
         out_shape=[
             jax.ShapeDtypeStruct(text.shape, BF16),
@@ -359,7 +374,7 @@
         compiler_params=small,
         cost_estimate=pl.CostEstimate(flops=0, bytes_accessed=2 * weight.size, transcendentals=0),
         name="base",
-    )(scales, gain, text, *even)
+    )(scales, text_scale, gain, text, *even)
     return pl.pallas_call(
         functools.partial(place_kernel, groups, cap, size),
         in_specs=[VMEM] * 5,
@@ -444,7 +459,7 @@
     per_image = vis.shape[0] // owners.shape[0]
     cap = text.shape[0] // (groups * per_image)
     full = dp * owners.shape[0] == groups * cap and groups * cap * per_image == text.shape[0]
-    fits = dp == 4 and groups & (groups - 1) == 0 and per_image == 16 and cap == 2 and text.shape[0] <= 512
+    fits = dp == 4 and groups & (groups - 1) == 0 and per_image == 16 and cap == 2 and text.shape[0] <= 512 and 3 * owners.shape[0] <= TEXT
     fits = fits and owners.shape[0] % 4 == 0 and weight.shape[1] % 1024 == 0
     form = fast if full and fits else general
     return form(vis, vis_gain, weight, bias, text, out_gain, counts, owners, offsets)

time: 57.4 us -> 55.4 us (0.965)
  blocking collectives: 13 us -> 11.7 us
  waiting for transfers between devices: 7.5 us -> 6.62 us
    all_to_all x1, blocking collectives: 13 us -> 11.7 us  [fast(): squares = lax.all_to_all(squares, ('grp', 'dp'), 0, 0, tiled=True)]
    ppermute x1, waiting for transfers between devices: 2.1 us -> 1.34 us  [second(): return lax.ppermute(x, 'dp', [(0, 2), (1, 3), (2, 0), (3, 1)])]
  transfers between devices with their start and end apart: 12 -> 12, of which waited for: 4 -> 4; matrix products, arithmetic and copies ran while one was open for 0% -> 0% of each run, Pallas kernels for 12% -> 13%
where the time goes in v6:
time: 55.4 us; the launch traced here: 55.1 us
  starting transfers between devices  17.9 us (32%)
  blocking collectives  11.7 us (21%)
  Pallas kernels  9.69 us (17%)
  local copies, waits for them, and re-layouts  8.28 us (15%)
  waiting for transfers between devices  6.62 us (12%)
  between operations  0.8 us (1%)
    all_to_all x1, blocking collectives, fast(): squares = lax.all_to_all(squares, ('grp', 'dp'), 0, 0, tiled=True)  11.7 us
    unnamed x20, local copies, waits for them, and re-layouts  8.28 us
    ppermute x2, starting transfers between devices, outer(): return lax.ppermute(x, 'dp', [(0, 1), (1, 0), (2, 3), (3, 2)])  4.92 us
    ppermute x4, starting transfers between devices, across(): lax.ppermute(x, 'grp', [(i, i ^ k) for i in range(lax.axis_size('grp'))])  3.62 us
    pallas_call x1, Pallas kernels, fast(): pl.pallas_call(early_kernel, in_specs=[VMEM] * 7, out_specs=VMEM, out_sha...  3.25 us
    ppermute x1, starting transfers between devices, ends(): return lax.ppermute(x, 'dp', [(0, 3), (3, 0), (1, 1), (2, 2)])  3.24 us
    ppermute x2, starting transfers between devices, far(): return lax.ppermute(x, 'dp', [(0, 2), (1, 0), (2, 3), (3, 1)])  3.08 us
    ppermute x1, waiting for transfers between devices, ends(): return lax.ppermute(x, 'dp', [(0, 3), (3, 0), (1, 1), (2, 2)])  2.97 us
  transfers between devices with their start and end apart: 12, of which 4 were waited for; matrix products, arithmetic and copies ran while one was open for 0% of the time, Pallas kernels for 13%

profile of v6, /device:TPU:0, one launch (start us, length us, event | category | flops | bytes accessed | tf_op | source)
XLA Modules:
  0.0 55.1 jit_solution(5655107923571615521)
XLA Ops:
  0.0 1.6 %collective-permute-start.3 = (bf16[64,3200]{1,0:T(8,128)(2,1)}, bf16[64,3200]{1,0:T(8,128)(2,1)S(1)}, u32[]{:S(2)}, u32[]{:S(2)}) collective-permute-start(bf16[64,3200]{1,0:T(8,128)(2,1)} %vis.1), channel_id=1, source_target_pairs={{1,2},{2,1},{0,0},{3,3},{5,6},{6,5},{4,4},{7,7},{9,10},{10,9},{8,8... | collective-permute-start | bytes 1228808 | tf_op jit(solution)/shard_map/ppermute | solution.py:237
  1.6 4.9 %collective-permute-start.4 = (bf16[64,3200]{1,0:T(8,128)(2,1)}, bf16[64,3200]{1,0:T(8,128)(2,1)S(1)}, u32[]{:S(2)}, u32[]{:S(2)}) collective-permute-start(bf16[64,3200]{1,0:T(8,128)(2,1)} %vis.1), channel_id=1, source_target_pairs={{0,1},{1,0},{2,3},{3,2},{4,5},{5,4},{6,7},{7,6},{8,9},{9,8},{10,11... | collective-permute-start | bytes 1228808 | tf_op jit(solution)/shard_map/ppermute | solution.py:233
  6.6 3.2 %collective-permute-start.7 = (bf16[64,3200]{1,0:T(8,128)(2,1)}, bf16[64,3200]{1,0:T(8,128)(2,1)S(1)}, u32[]{:S(2)}, u32[]{:S(2)}) collective-permute-start(bf16[64,3200]{1,0:T(8,128)(2,1)} %vis.1), channel_id=1, source_target_pairs={{0,3},{3,0},{1,1},{2,2},{4,7},{7,4},{5,5},{6,6},{8,11},{11,8},{9,9... | collective-permute-start | bytes 1228808 | tf_op jit(solution)/shard_map/ppermute | solution.py:241
  10.5 0.0 copy-start.2
  10.5 1.2 %copy-done.2 = bf16[256,2048]{1,0:T(8,128)(2,1)S(1)} copy-done((bf16[256,2048]{1,0:T(8,128)(2,1)S(1)}, bf16[256,2048]{1,0:T(8,128)(2,1)}, u32[]{:S(2)}) %copy-start.2) | copy-done | bytes 1048600
  11.7 0.0 copy-start.4
  11.7 1.0 %copy-done.4 = bf16[64,3200]{1,0:T(8,128)(2,1)S(1)} copy-done((bf16[64,3200]{1,0:T(8,128)(2,1)S(1)}, bf16[64,3200]{1,0:T(8,128)(2,1)}, u32[]{:S(2)}) %copy-start.4) | copy-done | bytes 409624
  12.7 0.0 copy-start.8
  12.7 0.7 %copy-done.8 = s32[4]{0:T(128)S(1)} copy-done((s32[4]{0:T(128)S(1)}, s32[4]{0:T(128)}, u32[]{:S(2)}) %copy-start.8) | copy-done | bytes 40
  13.4 0.0 copy-start.9
  13.4 0.7 %copy-done.9 = s32[4]{0:T(128)S(1)} copy-done((s32[4]{0:T(128)S(1)}, s32[4]{0:T(128)}, u32[]{:S(2)}) %copy-start.9) | copy-done | bytes 40
  14.0 0.0 copy-start.5
  14.0 0.0 copy-start.6
  14.0 0.9 %tables.1 = (f32[8,128]{1,0:T(8,128)S(1)}, bf16[64,3200]{1,0:T(8,128)(2,1)S(1)}, f32[8,128]{1,0:T(8,128)S(1)}) custom-call(bf16[256,2048]{1,0:T(8,128)(2,1)S(1)} %copy-done.2, bf16[64,3200]{1,0:T(8,128)(2,1)S(1)} %copy-done.4, s32[4]{0:T(128)S(1)} %copy-done.8, s32[4]{0:T(128)S(1)} %copy-done.9, s32[1]{0:T(128)S(6)} %copy.11.counts), custom_call_target="tpu_custom_call" | custom-call | tf_op jit(solution)/shard_map/tables/pallas_call | solution.py:274
  14.9 0.0 copy-start
  14.9 4.7 %copy-done = bf16[3200,2048]{1,0:T(8,128)(2,1)S(1)} copy-done((bf16[3200,2048]{1,0:T(8,128)(2,1)S(1)}, bf16[3200,2048]{1,0:T(8,128)(2,1)}, u32[]{:S(2)}) %copy-start) | copy-done | bytes 13107224
  19.6 0.0 copy-start.1
  19.6 0.0 collective-permute-done.3.inner
  19.6 0.0 copy-done.5
  19.6 0.2 pass.1
  19.9 0.0 collective-permute-done.4.outer
  19.9 0.1 collective-permute-start.6
  19.9 3.0 %collective-permute-start.5 = (bf16[64,1024]{1,0:T(8,128)(2,1)S(1)}, bf16[64,1024]{1,0:T(8,128)(2,1)S(1)}, u32[]{:S(2)}, u32[]{:S(2)}) collective-permute-start(bf16[64,1024]{1,0:T(8,128)(2,1)S(1)} %get-tuple-element.34), channel_id=1, source_target_pairs={{0,2},{1,0},{2,3},{3,1},{4,6},{5,4},{6,7},{7,5},{8,10},{9,8},{10,1... | collective-permute-start | bytes 393224 | tf_op jit(solution)/shard_map/ppermute | solution.py:253
  23.0 0.1 collective-permute-start
  23.0 1.3 %collective-permute-start.1 = (f32[8,128]{1,0:T(8,128)S(1)}, f32[8,128]{1,0:T(8,128)S(1)}, u32[]{:S(2)}, u32[]{:S(2)}) collective-permute-start(f32[8,128]{1,0:T(8,128)S(1)} %get-tuple-element.28.i0), channel_id=1, source_target_pairs={{0,3},{1,2},{2,1},{3,0},{4,7},{5,6},{6,5},{7,4},{8,11},{9,10},{10,... | collective-permute-start | bytes 12296 | tf_op jit(solution)/shard_map/ppermute | solution.py:245
  24.4 3.0 %collective-permute-done.7.ends = bf16[64,3200]{1,0:T(8,128)(2,1)S(1)} collective-permute-done((bf16[64,3200]{1,0:T(8,128)(2,1)}, bf16[64,3200]{1,0:T(8,128)(2,1)S(1)}, u32[]{:S(2)}, u32[]{:S(2)}) %collective-permute-start.7) | collective-permute-done | bytes 409632 | tf_op jit(solution)/shard_map/ppermute | solution.py:241
  27.4 0.0 collective-permute-start.2
  27.4 0.0 copy-done.6
  27.4 0.0 copy-done.1
  27.4 3.3 %early.1 = bf16[192,2048]{1,0:T(8,128)(2,1)S(1)} custom-call(bf16[64,3200]{1,0:T(8,128)(2,1)S(1)} %get-tuple-element.29.own, bf16[64,3200]{1,0:T(8,128)(2,1)S(1)} %collective-permute-done.4.outer, bf16[64,3200]{1,0:T(8,128)(2,1)S(1)} %collective-permute-done.3.inner, bf16[64,3200]{1,0:T(8,128)(2,1)S(1)} %collective-permute-done.7.ends, f32[3200]{0:T(1024)S(1)} %copy-done.5, ...), custom_call_target="tpu_custom_call" | custom-call | tf_op jit(solution)/shard_map/early/pallas_call | solution.py:312
  30.6 0.0 copy-start.3
  30.6 0.0 copy-start.7
  30.7 1.2 %collective-permute-done.6.last = bf16[64,2176]{1,0:T(8,128)(2,1)S(1)} collective-permute-done((bf16[64,2176]{1,0:T(8,128)(2,1)S(1)}, bf16[64,2176]{1,0:T(8,128)(2,1)S(1)}, u32[]{:S(2)}, u32[]{:S(2)}) %collective-permute-start.6) | collective-permute-done | bytes 278560 | tf_op jit(solution)/shard_map/ppermute | solution.py:253
  31.9 1.7 %late.1.total = f32[64,2048]{1,0:T(8,128)S(1)} custom-call(bf16[64,2176]{1,0:T(8,128)(2,1)S(1)} %collective-permute-done.6.last, bf16[3200,2048]{1,0:T(8,128)(2,1)S(1)} %copy-done.1, f32[1,2048]{1,0:T(1,128)S(1)} %bitcast.8), custom_call_target="tpu_custom_call" | custom-call | tf_op jit(solution)/shard_map/late/pallas_call | solution.py:323
  33.6 1.3 %collective-permute-done.i3 = f32[8,128]{1,0:T(8,128)S(1)} collective-permute-done((f32[8,128]{1,0:T(8,128)S(1)}, f32[8,128]{1,0:T(8,128)S(1)}, u32[]{:S(2)}, u32[]{:S(2)}) %collective-permute-start) | collective-permute-done | bytes 4128 | tf_op jit(solution)/shard_map/ppermute | solution.py:249
  34.9 0.0 collective-permute-done.1.i2
  34.9 0.0 collective-permute-done.2.i1
  34.9 0.0 collective-permute-done.5.last
  34.9 1.3 %project.1 = (bf16[64,2048]{1,0:T(8,128)(2,1)S(1)}, bf16[64,2048]{1,0:T(8,128)(2,1)S(1)}, bf16[64,2048]{1,0:T(8,128)(2,1)S(1)}, bf16[64,2048]{1,0:T(8,128)(2,1)S...) custom-call(f32[8,128]{1,0:T(8,128)S(1)} %collective-permute-done.i3, f32[8,128]{1,0:T(8,128)S(1)} %collective-permute-done.1.i2, ...), custom_call_target="tpu_custom_call" | custom-call | flops 2516582400 | bytes 13107200 | tf_op jit(solution)/shard_map/project/pallas_call | solution.py:332
  36.2 2.5 %collective-permute-start.10 = (bf16[64,2048]{1,0:T(8,128)(2,1)S(1)}, bf16[64,2048]{1,0:T(8,128)(2,1)S(1)}, u32[]{:S(2)}, u32[]{:S(2)}) collective-permute-start(bf16[64,2048]{1,0:T(8,128)(2,1)S(1)} %get-tuple-element.41), channel_id=1, source_target_pairs={{0,24},{4,28},{8,16},{12,20},{16,8},{20,12},{24,0},{28,4},{1,25},{... | collective-permute-start | bytes 786440 | tf_op jit(solution)/shard_map/ppermute | solution.py:257
  38.8 0.5 collective-permute-start.8
  39.3 0.5 collective-permute-start.9
  39.8 11.7 %all_to_all.11 = f32[32,1,128]{2,1,0:T(1,128)S(1)} all-to-all(f32[32,1,128]{2,1,0:T(1,128)S(1)} %bitcast.11), channel_id=1, replica_groups=mesh['grp'=8,'dp'=4] {'grp','dp'}, dimensions={0} | all-to-all | bytes 32768 | tf_op jit(solution)/shard_map/all_to_all | solution.py:347
  51.5 0.2 scale.1.scales
  51.7 0.0 collective-permute-done.10.refs_3_.rest_3_
  51.7 0.0 collective-permute-done.8.refs_1_.rest_1_
  51.7 0.0 collective-permute-done.9.refs_2_.rest_2_
  51.8 0.1 collective-permute-start.11
  51.8 0.0 copy-done.3
  51.9 0.0 copy-done.7
  51.9 0.8 %base.1 = (bf16[256,2048]{1,0:T(8,128)(2,1)S(1)}, bf16[256,128]{1,0:T(8,128)(2,1)S(1)}) custom-call(f32[128,128]{1,0:T(8,128)S(1)} %scale.1.scales, f32[8,128]{1,0:T(8,128)S(1)} %get-tuple-element.48.text_scale, f32[1,2048]{1,0:T(1,128)S(1)} %bitcast.9, bf16[256,2048]{1,0:T(8,128)(2,1)S(1)} %copy-done.3, ...), custom_call_target="tpu_custom_call" | custom-call | bytes 13107200 | tf_op jit(solution)/shard_map/base/pallas_call | solution.py:365
  52.7 1.1 %collective-permute-done.11.odd = bf16[128,2048]{1,0:T(8,128)(2,1)S(1)} collective-permute-done((bf16[128,2048]{1,0:T(8,128)(2,1)S(1)}, bf16[128,2048]{1,0:T(8,128)(2,1)S(1)}, u32[]{:S(2)}, u32[]{:S(2)}) %collective-permute-start.11) | collective-permute-done | bytes 524320 | tf_op jit(solution)/shard_map/ppermute | solution.py:257
  53.7 1.3 %place.1 = bf16[256,2048]{1,0:T(8,128)(2,1)} custom-call(f32[128,128]{1,0:T(8,128)S(1)} %scale.1.scales, f32[1,2048]{1,0:T(1,128)S(1)} %bitcast.10, bf16[128,2048]{1,0:T(8,128)(2,1)S(1)} %collective-permute-done.11.odd, bf16[256,2048]{1,0:T(8,128)(2,1)S(1)} %get-tuple-element.49.base, bf16[256,128]{1,0:T(8,128)(2,1)S(1)} %get-tuple-element.50.order), custom_call_target="tpu_custom_call" | custom-call | tf_op jit(solution)/shard_map/place/pallas_call | solution.py:378
  (2 shorter events, 0.0 us)
Async XLA Ops:
  0.0 19.6 %collective-permute-start.3 = (bf16[64,3200]{1,0:T(8,128)(2,1)}, bf16[64,3200]{1,0:T(8,128)(2,1)S(1)}, u32[]{:S(2)}, u32[]{:S(2)}) collective-permute-start(bf16[64,3200]{1,0:T(8,128)(2,1)} %vis.1), channel_id=1, source_target_pairs={{1,2},{2,1},{0,0},{3,3},{5,6},{6,5},{4,4},{7,7},{9,10},{10,9},{8,8... | collective-permute-start | bytes 1228808 | tf_op jit(solution)/shard_map/ppermute | solution.py:237
  1.6 18.2 %collective-permute-start.4 = (bf16[64,3200]{1,0:T(8,128)(2,1)}, bf16[64,3200]{1,0:T(8,128)(2,1)S(1)}, u32[]{:S(2)}, u32[]{:S(2)}) collective-permute-start(bf16[64,3200]{1,0:T(8,128)(2,1)} %vis.1), channel_id=1, source_target_pairs={{0,1},{1,0},{2,3},{3,2},{4,5},{5,4},{6,7},{7,6},{8,9},{9,8},{10,11... | collective-permute-start | bytes 1228808 | tf_op jit(solution)/shard_map/ppermute | solution.py:233
  6.6 20.8 %collective-permute-start.7 = (bf16[64,3200]{1,0:T(8,128)(2,1)}, bf16[64,3200]{1,0:T(8,128)(2,1)S(1)}, u32[]{:S(2)}, u32[]{:S(2)}) collective-permute-start(bf16[64,3200]{1,0:T(8,128)(2,1)} %vis.1), channel_id=1, source_target_pairs={{0,3},{3,0},{1,1},{2,2},{4,7},{7,4},{5,5},{6,6},{8,11},{11,8},{9,9... | collective-permute-start | bytes 1228808 | tf_op jit(solution)/shard_map/ppermute | solution.py:241
  10.5 1.2 %copy-start.2 = (bf16[256,2048]{1,0:T(8,128)(2,1)S(1)}, bf16[256,2048]{1,0:T(8,128)(2,1)}, u32[]{:S(2)}) copy-start(bf16[256,2048]{1,0:T(8,128)(2,1)} %text.3) | copy-start | bytes 3145732
  11.7 1.0 %copy-start.4 = (bf16[64,3200]{1,0:T(8,128)(2,1)S(1)}, bf16[64,3200]{1,0:T(8,128)(2,1)}, u32[]{:S(2)}) copy-start(bf16[64,3200]{1,0:T(8,128)(2,1)} %vis.1) | copy-start | bytes 1228804
  12.7 0.7 %copy-start.8 = (s32[4]{0:T(128)S(1)}, s32[4]{0:T(128)}, u32[]{:S(2)}) copy-start(s32[4]{0:T(128)} %owners.1) | copy-start | bytes 52
  13.4 0.7 %copy-start.9 = (s32[4]{0:T(128)S(1)}, s32[4]{0:T(128)}, u32[]{:S(2)}) copy-start(s32[4]{0:T(128)} %offsets.1) | copy-start | bytes 52
  14.0 5.6 %copy-start.5 = (f32[3200]{0:T(1024)S(1)}, f32[3200]{0:T(1024)}, u32[]{:S(2)}) copy-start(f32[3200]{0:T(1024)} %gain.3) | copy-start | bytes 38404
  14.0 13.4 %copy-start.6 = (f32[2048]{0:T(1024)S(1)}, f32[2048]{0:T(1024)}, u32[]{:S(2)}) copy-start(f32[2048]{0:T(1024)} %param.12) | copy-start | bytes 24580
  14.9 4.7 %copy-start = (bf16[3200,2048]{1,0:T(8,128)(2,1)S(1)}, bf16[3200,2048]{1,0:T(8,128)(2,1)}, u32[]{:S(2)}) copy-start(bf16[3200,2048]{1,0:T(8,128)(2,1)} %weight.7) | copy-start | bytes 39321604
  19.6 7.7 %copy-start.1 = (bf16[3200,2048]{1,0:T(8,128)(2,1)S(1)}, bf16[3200,2048]{1,0:T(8,128)(2,1)}, u32[]{:S(2)}) copy-start(bf16[3200,2048]{1,0:T(8,128)(2,1)} %weight.7) | copy-start | bytes 39321604
  19.9 12.0 %collective-permute-start.6 = (bf16[64,2176]{1,0:T(8,128)(2,1)S(1)}, bf16[64,2176]{1,0:T(8,128)(2,1)S(1)}, u32[]{:S(2)}, u32[]{:S(2)}) collective-permute-start(bf16[64,2176]{1,0:T(8,128)(2,1)S(1)} %get-tuple-element.35), channel_id=1, source_target_pairs={{0,2},{1,0},{2,3},{3,1},{4,6},{5,4},{6,7},{7,5},{8,10},{9,8},{10,1... | collective-permute-start | bytes 835592 | tf_op jit(solution)/shard_map/ppermute | solution.py:253
  19.9 15.0 %collective-permute-start.5 = (bf16[64,1024]{1,0:T(8,128)(2,1)S(1)}, bf16[64,1024]{1,0:T(8,128)(2,1)S(1)}, u32[]{:S(2)}, u32[]{:S(2)}) collective-permute-start(bf16[64,1024]{1,0:T(8,128)(2,1)S(1)} %get-tuple-element.34), channel_id=1, source_target_pairs={{0,2},{1,0},{2,3},{3,1},{4,6},{5,4},{6,7},{7,5},{8,10},{9,8},{10,1... | collective-permute-start | bytes 393224 | tf_op jit(solution)/shard_map/ppermute | solution.py:253
  23.0 11.9 %collective-permute-start = (f32[8,128]{1,0:T(8,128)S(1)}, f32[8,128]{1,0:T(8,128)S(1)}, u32[]{:S(2)}, u32[]{:S(2)}) collective-permute-start(f32[8,128]{1,0:T(8,128)S(1)} %get-tuple-element.28.i0), channel_id=1, source_target_pairs={{0,2},{1,3},{2,0},{3,1},{4,6},{5,7},{6,4},{7,5},{8,10},{9,11},{10,... | collective-permute-start | bytes 12296 | tf_op jit(solution)/shard_map/ppermute | solution.py:249
  23.0 11.9 %collective-permute-start.1 = (f32[8,128]{1,0:T(8,128)S(1)}, f32[8,128]{1,0:T(8,128)S(1)}, u32[]{:S(2)}, u32[]{:S(2)}) collective-permute-start(f32[8,128]{1,0:T(8,128)S(1)} %get-tuple-element.28.i0), channel_id=1, source_target_pairs={{0,3},{1,2},{2,1},{3,0},{4,7},{5,6},{6,5},{7,4},{8,11},{9,10},{10,... | collective-permute-start | bytes 12296 | tf_op jit(solution)/shard_map/ppermute | solution.py:245
  27.4 7.5 %collective-permute-start.2 = (f32[8,128]{1,0:T(8,128)S(1)}, f32[8,128]{1,0:T(8,128)S(1)}, u32[]{:S(2)}, u32[]{:S(2)}) collective-permute-start(f32[8,128]{1,0:T(8,128)S(1)} %get-tuple-element.28.i0), channel_id=1, source_target_pairs={{0,1},{1,0},{2,3},{3,2},{4,5},{5,4},{6,7},{7,6},{8,9},{9,8},{10,11... | collective-permute-start | bytes 12296 | tf_op jit(solution)/shard_map/ppermute | solution.py:233
  30.6 21.2 %copy-start.3 = (bf16[256,2048]{1,0:T(8,128)(2,1)S(1)}, bf16[256,2048]{1,0:T(8,128)(2,1)}, u32[]{:S(2)}) copy-start(bf16[256,2048]{1,0:T(8,128)(2,1)} %text.3) | copy-start | bytes 3145732
  30.6 21.2 %copy-start.7 = (f32[2048]{0:T(1024)S(1)}, f32[2048]{0:T(1024)}, u32[]{:S(2)}) copy-start(f32[2048]{0:T(1024)} %param.14) | copy-start | bytes 24580
  36.2 15.5 %collective-permute-start.10 = (bf16[64,2048]{1,0:T(8,128)(2,1)S(1)}, bf16[64,2048]{1,0:T(8,128)(2,1)S(1)}, u32[]{:S(2)}, u32[]{:S(2)}) collective-permute-start(bf16[64,2048]{1,0:T(8,128)(2,1)S(1)} %get-tuple-element.41), channel_id=1, source_target_pairs={{0,24},{4,28},{8,16},{12,20},{16,8},{20,12},{24,0},{28,4},{1,25},{... | collective-permute-start | bytes 786440 | tf_op jit(solution)/shard_map/ppermute | solution.py:257
  38.8 12.9 %collective-permute-start.8 = (bf16[64,2048]{1,0:T(8,128)(2,1)S(1)}, bf16[64,2048]{1,0:T(8,128)(2,1)S(1)}, u32[]{:S(2)}, u32[]{:S(2)}) collective-permute-start(bf16[64,2048]{1,0:T(8,128)(2,1)S(1)} %get-tuple-element.39), channel_id=1, source_target_pairs={{0,8},{4,12},{8,0},{12,4},{16,24},{20,28},{24,16},{28,20},{1,9},{5... | collective-permute-start | bytes 786440 | tf_op jit(solution)/shard_map/ppermute | solution.py:257
  39.3 12.4 %collective-permute-start.9 = (bf16[64,2048]{1,0:T(8,128)(2,1)S(1)}, bf16[64,2048]{1,0:T(8,128)(2,1)S(1)}, u32[]{:S(2)}, u32[]{:S(2)}) collective-permute-start(bf16[64,2048]{1,0:T(8,128)(2,1)S(1)} %get-tuple-element.40), channel_id=1, source_target_pairs={{0,16},{4,20},{8,24},{12,28},{16,0},{20,4},{24,8},{28,12},{1,17},{... | collective-permute-start | bytes 786440 | tf_op jit(solution)/shard_map/ppermute | solution.py:257
  51.8 2.0 %collective-permute-start.11 = (bf16[128,2048]{1,0:T(8,128)(2,1)S(1)}, bf16[128,2048]{1,0:T(8,128)(2,1)S(1)}, u32[]{:S(2)}, u32[]{:S(2)}) collective-permute-start(bf16[128,2048]{1,0:T(8,128)(2,1)S(1)} %pack.1), channel_id=1, source_target_pairs={{0,4},{4,0},{8,12},{12,8},{16,20},{20,16},{24,28},{28,24},{1,5},{5... | collective-permute-start | bytes 1572872 | tf_op jit(solution)/shard_map/ppermute | solution.py:257

commit v7 on v6

--- a/solution.py
+++ b/solution.py
@@ -191,13 +191,11 @@
 
 
 def base_kernel(groups, cap, size, scales, text_scale, gain, text, *rest):
-    *even, base, order_odd, rows = rest
+    *even, out, rows, done, sem = rest
     seq_len = text.shape[0]
     g = gain[...]
     order = moves(seq_len, cap, size, range(0, groups, 2), scales)
-    odd = moves(seq_len, cap, size, range(1, groups, 2), scales)
-    order_odd[...] = odd.astype(BF16)
-    covered = jnp.sum(order + odd, axis=1, keepdims=True)
+    covered = jnp.sum(order, axis=1, keepdims=True)
     for n, part in enumerate(even):
         for r, x in enumerate(scaled(cap, size, 2 * n, part, scales, g)):
             at = (n * cap + r) * size
@@ -207,26 +205,37 @@
         inverse = jnp.concatenate([text_scale[:, 2 * c : 2 * c + 1], text_scale[:, 2 * c + 1 : 2 * c + 2]], axis=0)
         part = slice(c * 16, (c + 1) * 16)
         x = text[part, :].astype(F32) * inverse * g
-        base[part, :] = jnp.where(covered[part] > 0, moved[part], x).astype(BF16)
-
-
-def place_kernel(groups, cap, size, scales, gain, odd, base, order, out, rows, done, sems):
-    columns = out.shape[1]
-    block = columns // sems.shape[0]
-    copies = []
-    for c in range(sems.shape[0]):
-        part = slice(c * block, (c + 1) * block)
-        g = gain[:, part]
-        for n, k in enumerate(range(1, groups, 2)):
-            at = n * cap * size
-            for r, x in enumerate(scaled(cap, size, k, odd[at : at + cap * size, part], scales, g)):
-                rows[at + r * size : at + (r + 1) * size, part] = x
-        moved = jnp.dot(order[...], rows[:, part], preferred_element_type=F32)
-        done[:, part] = (base[:, part].astype(F32) + moved).astype(BF16)
-        copies.append(pltpu.make_async_copy(done.at[:, part], out.at[:, part], sems.at[c]))
-        copies[-1].start()
-    for copy in copies:
-        copy.wait()
+        done[part, :] = jnp.where(covered[part] > 0, moved[part], x).astype(BF16)
+    copy = pltpu.make_async_copy(done, out, sem)
+    copy.start()
+    copy.wait()
+
+
+def place_kernel(groups, cap, size, scales, gain, odd, base, out, done, sems):
+    del base
+    at = cap * size
+    g = gain[...]
+    places = [(n, k, r) for n, k in enumerate(range(1, groups, 2)) for r in range(cap)]
+    starts = [jnp.sum(scales[at + r : at + r + 1, k : k + 1]).astype(jnp.int32) - 1 for _, k, r in places]
+
+    def copy(m):
+        there = pl.ds(pl.multiple_of(starts[m] * size, size), size)
+        return pltpu.make_async_copy(done.at[m * size : (m + 1) * size], out.at[there], sems.at[m])
+
+    for m, (n, k, r) in enumerate(places):
+        if r == 0:
+            rows = scaled(cap, size, k, odd[n * at : (n + 1) * at], scales, g)
+        done[m * size : (m + 1) * size, :] = rows[r]
+
+        @pl.when(starts[m] >= 0)
+        def _():
+            copy(m).start()
+
+    for m in range(len(places)):
+
+        @pl.when(starts[m] >= 0)
+        def _():
+            copy(m).wait()
 
 
 def outer(x):
@@ -355,39 +364,33 @@
         name="scale",
     )(squares)
     even = [parts[0]] + [across(parts[j], 2 * j) for j in range(1, pairs)]
-    *even, scales = lax.optimization_barrier((*even, scales))
+    *even, squares = lax.optimization_barrier((*even, squares))
     arrived = jax.ShapeDtypeStruct((pairs * cap * size, columns), BF16)
     odd = pl.pallas_call(
         pack_kernel, in_specs=[VMEM] * pairs, out_specs=VMEM, out_shape=arrived, compiler_params=small, name="pack"
     )(*even)
     odd = across(odd, 1)
     gain = out_gain[None, :]
-    base, order = pl.pallas_call(
+    base = pl.pallas_call(
         functools.partial(base_kernel, groups, cap, size),
         in_specs=[VMEM] * (4 + pairs),
-        out_specs=[VMEM] * 2,
-        out_shape=[
-            jax.ShapeDtypeStruct(text.shape, BF16),
-            jax.ShapeDtypeStruct((seq_len, pairs * cap * size), BF16),
-        ],
-        scratch_shapes=[pltpu.VMEM(arrived.shape, BF16)],
+        out_specs=ANY,
+        out_shape=jax.ShapeDtypeStruct(text.shape, BF16),
+        scratch_shapes=[pltpu.VMEM(arrived.shape, BF16), pltpu.VMEM(text.shape, BF16), pltpu.SemaphoreType.DMA],
         compiler_params=small,
         cost_estimate=pl.CostEstimate(flops=0, bytes_accessed=2 * weight.size, transcendentals=0),
         name="base",
     )(scales, text_scale, gain, text, *even)
     return pl.pallas_call(
         functools.partial(place_kernel, groups, cap, size),
-        in_specs=[VMEM] * 5,
+        in_specs=[VMEM] * 3 + [ANY],
         out_specs=ANY,
         out_shape=jax.ShapeDtypeStruct(text.shape, BF16),
-        scratch_shapes=[
-            pltpu.VMEM(arrived.shape, BF16),
-            pltpu.VMEM(text.shape, BF16),
-            pltpu.SemaphoreType.DMA((4,)),
-        ],
+        input_output_aliases={3: 0},
+        scratch_shapes=[pltpu.VMEM(arrived.shape, BF16), pltpu.SemaphoreType.DMA((pairs * cap,))],
         compiler_params=small,
         name="place",
-    )(scales, gain, odd, base, order)
+    )(scales, gain, odd, base)
 
 
 def general(

time: 55.4 us -> 55 us (level)
  waiting for transfers between devices: 6.62 us -> 5.55 us
  Pallas kernels: 9.69 us -> 10.3 us
    ppermute x4, waiting for transfers between devices: 1.07 us -> 0.01 us  [across(): lax.ppermute(x, 'grp', [(i, i ^ k) for i in range(lax.axis_size('grp'))])]
    pallas_call x1, Pallas kernels: 0.8 us -> 1.77 us  [fast(): pl.pallas_call(functools.partial(base_kernel, groups, cap, size), in_spec...]
  transfers between devices with their start and end apart: 12 -> 12, of which waited for: 4 -> 3; matrix products, arithmetic and copies ran while one was open for 0% -> 0% of each run, Pallas kernels for 13% -> 15%
where the time goes in v7:
time: 55 us; the launch traced here: 54.6 us
  starting transfers between devices  17.9 us (33%)
  blocking collectives  11.7 us (21%)
  Pallas kernels  10.3 us (19%)
  local copies, waits for them, and re-layouts  8.28 us (15%)
  waiting for transfers between devices  5.55 us (10%)
  between operations  0.79 us (1%)
    all_to_all x1, blocking collectives, fast(): squares = lax.all_to_all(squares, ('grp', 'dp'), 0, 0, tiled=True)  11.7 us
    unnamed x20, local copies, waits for them, and re-layouts  8.28 us
    ppermute x2, starting transfers between devices, outer(): return lax.ppermute(x, 'dp', [(0, 1), (1, 0), (2, 3), (3, 2)])  4.92 us
    ppermute x4, starting transfers between devices, across(): lax.ppermute(x, 'grp', [(i, i ^ k) for i in range(lax.axis_size('grp'))])  3.62 us
    pallas_call x1, Pallas kernels, fast(): pl.pallas_call(early_kernel, in_specs=[VMEM] * 7, out_specs=VMEM, out_sha...  3.25 us
    ppermute x1, starting transfers between devices, ends(): return lax.ppermute(x, 'dp', [(0, 3), (3, 0), (1, 1), (2, 2)])  3.24 us
    ppermute x2, starting transfers between devices, far(): return lax.ppermute(x, 'dp', [(0, 2), (1, 0), (2, 3), (3, 1)])  3.08 us
    ppermute x1, waiting for transfers between devices, ends(): return lax.ppermute(x, 'dp', [(0, 3), (3, 0), (1, 1), (2, 2)])  2.97 us
  transfers between devices with their start and end apart: 12, of which 3 were waited for; matrix products, arithmetic and copies ran while one was open for 0% of the time, Pallas kernels for 15%

profile of v7, /device:TPU:0, one launch (start us, length us, event | category | flops | bytes accessed | tf_op | source)
XLA Modules:
  0.0 54.6 jit_solution(12052145761866581665)
XLA Ops:
  0.0 1.6 %collective-permute-start.3 = (bf16[64,3200]{1,0:T(8,128)(2,1)}, bf16[64,3200]{1,0:T(8,128)(2,1)S(1)}, u32[]{:S(2)}, u32[]{:S(2)}) collective-permute-start(bf16[64,3200]{1,0:T(8,128)(2,1)} %vis.1), channel_id=1, source_target_pairs={{1,2},{2,1},{0,0},{3,3},{5,6},{6,5},{4,4},{7,7},{9,10},{10,9},{8,8... | collective-permute-start | bytes 1228808 | tf_op jit(solution)/shard_map/ppermute | solution.py:246
  1.6 4.9 %collective-permute-start.4 = (bf16[64,3200]{1,0:T(8,128)(2,1)}, bf16[64,3200]{1,0:T(8,128)(2,1)S(1)}, u32[]{:S(2)}, u32[]{:S(2)}) collective-permute-start(bf16[64,3200]{1,0:T(8,128)(2,1)} %vis.1), channel_id=1, source_target_pairs={{0,1},{1,0},{2,3},{3,2},{4,5},{5,4},{6,7},{7,6},{8,9},{9,8},{10,11... | collective-permute-start | bytes 1228808 | tf_op jit(solution)/shard_map/ppermute | solution.py:242
  6.6 3.2 %collective-permute-start.7 = (bf16[64,3200]{1,0:T(8,128)(2,1)}, bf16[64,3200]{1,0:T(8,128)(2,1)S(1)}, u32[]{:S(2)}, u32[]{:S(2)}) collective-permute-start(bf16[64,3200]{1,0:T(8,128)(2,1)} %vis.1), channel_id=1, source_target_pairs={{0,3},{3,0},{1,1},{2,2},{4,7},{7,4},{5,5},{6,6},{8,11},{11,8},{9,9... | collective-permute-start | bytes 1228808 | tf_op jit(solution)/shard_map/ppermute | solution.py:250
  10.5 0.0 copy-start.2
  10.5 1.2 %copy-done.2 = bf16[256,2048]{1,0:T(8,128)(2,1)S(1)} copy-done((bf16[256,2048]{1,0:T(8,128)(2,1)S(1)}, bf16[256,2048]{1,0:T(8,128)(2,1)}, u32[]{:S(2)}) %copy-start.2) | copy-done | bytes 1048600
  11.7 0.0 copy-start.4
  11.7 1.0 %copy-done.4 = bf16[64,3200]{1,0:T(8,128)(2,1)S(1)} copy-done((bf16[64,3200]{1,0:T(8,128)(2,1)S(1)}, bf16[64,3200]{1,0:T(8,128)(2,1)}, u32[]{:S(2)}) %copy-start.4) | copy-done | bytes 409624
  12.7 0.0 copy-start.8
  12.7 0.7 %copy-done.8 = s32[4]{0:T(128)S(1)} copy-done((s32[4]{0:T(128)S(1)}, s32[4]{0:T(128)}, u32[]{:S(2)}) %copy-start.8) | copy-done | bytes 40
  13.4 0.0 copy-start.9
  13.4 0.7 %copy-done.9 = s32[4]{0:T(128)S(1)} copy-done((s32[4]{0:T(128)S(1)}, s32[4]{0:T(128)}, u32[]{:S(2)}) %copy-start.9) | copy-done | bytes 40
  14.0 0.0 copy-start.5
  14.0 0.0 copy-start.6
  14.0 0.9 %tables.1 = (f32[8,128]{1,0:T(8,128)S(1)}, bf16[64,3200]{1,0:T(8,128)(2,1)S(1)}, f32[8,128]{1,0:T(8,128)S(1)}) custom-call(bf16[256,2048]{1,0:T(8,128)(2,1)S(1)} %copy-done.2, bf16[64,3200]{1,0:T(8,128)(2,1)S(1)} %copy-done.4, s32[4]{0:T(128)S(1)} %copy-done.8, s32[4]{0:T(128)S(1)} %copy-done.9, s32[1]{0:T(128)S(6)} %copy.13.counts), custom_call_target="tpu_custom_call" | custom-call | tf_op jit(solution)/shard_map/tables/pallas_call | solution.py:283
  14.9 0.0 copy-start
  14.9 4.7 %copy-done = bf16[3200,2048]{1,0:T(8,128)(2,1)S(1)} copy-done((bf16[3200,2048]{1,0:T(8,128)(2,1)S(1)}, bf16[3200,2048]{1,0:T(8,128)(2,1)}, u32[]{:S(2)}) %copy-start) | copy-done | bytes 13107224
  19.6 0.0 copy-start.1
  19.6 0.0 collective-permute-done.3.inner
  19.6 0.0 copy-done.5
  19.6 0.2 pass.1
  19.9 0.0 collective-permute-done.4.outer
  19.9 0.1 collective-permute-start.6
  19.9 3.0 %collective-permute-start.5 = (bf16[64,1024]{1,0:T(8,128)(2,1)S(1)}, bf16[64,1024]{1,0:T(8,128)(2,1)S(1)}, u32[]{:S(2)}, u32[]{:S(2)}) collective-permute-start(bf16[64,1024]{1,0:T(8,128)(2,1)S(1)} %get-tuple-element.31), channel_id=1, source_target_pairs={{0,2},{1,0},{2,3},{3,1},{4,6},{5,4},{6,7},{7,5},{8,10},{9,8},{10,1... | collective-permute-start | bytes 393224 | tf_op jit(solution)/shard_map/ppermute | solution.py:262
  23.0 0.1 collective-permute-start
  23.0 1.3 %collective-permute-start.1 = (f32[8,128]{1,0:T(8,128)S(1)}, f32[8,128]{1,0:T(8,128)S(1)}, u32[]{:S(2)}, u32[]{:S(2)}) collective-permute-start(f32[8,128]{1,0:T(8,128)S(1)} %get-tuple-element.25.i0), channel_id=1, source_target_pairs={{0,3},{1,2},{2,1},{3,0},{4,7},{5,6},{6,5},{7,4},{8,11},{9,10},{10,... | collective-permute-start | bytes 12296 | tf_op jit(solution)/shard_map/ppermute | solution.py:254
  24.4 3.0 %collective-permute-done.7.ends = bf16[64,3200]{1,0:T(8,128)(2,1)S(1)} collective-permute-done((bf16[64,3200]{1,0:T(8,128)(2,1)}, bf16[64,3200]{1,0:T(8,128)(2,1)S(1)}, u32[]{:S(2)}, u32[]{:S(2)}) %collective-permute-start.7) | collective-permute-done | bytes 409632 | tf_op jit(solution)/shard_map/ppermute | solution.py:250
  27.4 0.0 collective-permute-start.2
  27.4 0.0 copy-done.6
  27.4 0.0 copy-done.1
  27.4 3.3 %early.1 = bf16[192,2048]{1,0:T(8,128)(2,1)S(1)} custom-call(bf16[64,3200]{1,0:T(8,128)(2,1)S(1)} %get-tuple-element.26.own, bf16[64,3200]{1,0:T(8,128)(2,1)S(1)} %collective-permute-done.4.outer, bf16[64,3200]{1,0:T(8,128)(2,1)S(1)} %collective-permute-done.3.inner, bf16[64,3200]{1,0:T(8,128)(2,1)S(1)} %collective-permute-done.7.ends, f32[3200]{0:T(1024)S(1)} %copy-done.5, ...), custom_call_target="tpu_custom_call" | custom-call | tf_op jit(solution)/shard_map/early/pallas_call | solution.py:321
  30.6 0.0 copy-start.3
  30.6 0.0 copy-start.7
  30.7 1.2 %collective-permute-done.6.last = bf16[64,2176]{1,0:T(8,128)(2,1)S(1)} collective-permute-done((bf16[64,2176]{1,0:T(8,128)(2,1)S(1)}, bf16[64,2176]{1,0:T(8,128)(2,1)S(1)}, u32[]{:S(2)}, u32[]{:S(2)}) %collective-permute-start.6) | collective-permute-done | bytes 278560 | tf_op jit(solution)/shard_map/ppermute | solution.py:262
  31.9 1.7 %late.1.total = f32[64,2048]{1,0:T(8,128)S(1)} custom-call(bf16[64,2176]{1,0:T(8,128)(2,1)S(1)} %collective-permute-done.6.last, bf16[3200,2048]{1,0:T(8,128)(2,1)S(1)} %copy-done.1, f32[1,2048]{1,0:T(1,128)S(1)} %bitcast.8), custom_call_target="tpu_custom_call" | custom-call | tf_op jit(solution)/shard_map/late/pallas_call | solution.py:332
  33.6 1.3 %collective-permute-done.i3 = f32[8,128]{1,0:T(8,128)S(1)} collective-permute-done((f32[8,128]{1,0:T(8,128)S(1)}, f32[8,128]{1,0:T(8,128)S(1)}, u32[]{:S(2)}, u32[]{:S(2)}) %collective-permute-start) | collective-permute-done | bytes 4128 | tf_op jit(solution)/shard_map/ppermute | solution.py:258
  34.9 0.0 collective-permute-done.1.i2
  34.9 0.0 collective-permute-done.2.i1
  34.9 0.0 collective-permute-done.5.last
  34.9 1.3 %project.1 = (bf16[64,2048]{1,0:T(8,128)(2,1)S(1)}, bf16[64,2048]{1,0:T(8,128)(2,1)S(1)}, bf16[64,2048]{1,0:T(8,128)(2,1)S(1)}, bf16[64,2048]{1,0:T(8,128)(2,1)S...) custom-call(f32[8,128]{1,0:T(8,128)S(1)} %collective-permute-done.i3, f32[8,128]{1,0:T(8,128)S(1)} %collective-permute-done.1.i2, ...), custom_call_target="tpu_custom_call" | custom-call | flops 2516582400 | bytes 13107200 | tf_op jit(solution)/shard_map/project/pallas_call | solution.py:341
  36.2 2.5 %collective-permute-start.10 = (bf16[64,2048]{1,0:T(8,128)(2,1)S(1)}, bf16[64,2048]{1,0:T(8,128)(2,1)S(1)}, u32[]{:S(2)}, u32[]{:S(2)}) collective-permute-start(bf16[64,2048]{1,0:T(8,128)(2,1)S(1)} %get-tuple-element.39), channel_id=1, source_target_pairs={{0,24},{4,28},{8,16},{12,20},{16,8},{20,12},{24,0},{28,4},{1,25},{... | collective-permute-start | bytes 786440 | tf_op jit(solution)/shard_map/ppermute | solution.py:266
  38.8 0.5 collective-permute-start.8
  39.3 0.5 collective-permute-start.9
  39.8 11.7 %all_to_all.11 = f32[32,1,128]{2,1,0:T(1,128)S(1)} all-to-all(f32[32,1,128]{2,1,0:T(1,128)S(1)} %bitcast.11), channel_id=1, replica_groups=mesh['grp'=8,'dp'=4] {'grp','dp'}, dimensions={0} | all-to-all | bytes 32768 | tf_op jit(solution)/shard_map/all_to_all | solution.py:356
  51.5 0.0 collective-permute-done.10.refs_3_.rest_3_
  51.5 0.0 collective-permute-done.8.refs_1_.rest_1_
  51.5 0.0 collective-permute-done.9.refs_2_.rest_2_
  51.6 0.1 collective-permute-start.11
  51.7 0.2 scale.1.scales
  51.8 0.0 copy-done.3
  51.8 0.0 copy-done.7
  51.9 1.8 %base.1 = bf16[256,2048]{1,0:T(8,128)(2,1)} custom-call(f32[128,128]{1,0:T(8,128)S(1)} %scale.1.scales, f32[8,128]{1,0:T(8,128)S(1)} %get-tuple-element.44.text_scale, f32[1,2048]{1,0:T(1,128)S(1)} %bitcast.9, bf16[256,2048]{1,0:T(8,128)(2,1)S(1)} %copy-done.3, bf16[64,2048]{1,0:T(8,128)(2,1)S(1)} %get-tuple-element.40.refs_0_.rest_0_, ...), custom_call_target="tpu_custom_call" | custom-call | bytes 13107200 | tf_op jit(solution)/shard_map/base/pallas_call | solution.py:374
  53.6 0.0 collective-permute-done.11.odd
  53.6 0.9 %place.1 = bf16[256,2048]{1,0:T(8,128)(2,1)} custom-call(f32[128,128]{1,0:T(8,128)S(1)} %scale.1.scales, f32[1,2048]{1,0:T(1,128)S(1)} %bitcast.10, bf16[128,2048]{1,0:T(8,128)(2,1)S(1)} %collective-permute-done.11.odd, bf16[256,2048]{1,0:T(8,128)(2,1)} %base.1), custom_call_target="tpu_custom_call", output_to_operand_aliasing={{}: (3, {})} | custom-call | tf_op jit(solution)/shard_map/place/pallas_call | solution.py:384
  (2 shorter events, 0.0 us)
Async XLA Ops:
  0.0 19.6 %collective-permute-start.3 = (bf16[64,3200]{1,0:T(8,128)(2,1)}, bf16[64,3200]{1,0:T(8,128)(2,1)S(1)}, u32[]{:S(2)}, u32[]{:S(2)}) collective-permute-start(bf16[64,3200]{1,0:T(8,128)(2,1)} %vis.1), channel_id=1, source_target_pairs={{1,2},{2,1},{0,0},{3,3},{5,6},{6,5},{4,4},{7,7},{9,10},{10,9},{8,8... | collective-permute-start | bytes 1228808 | tf_op jit(solution)/shard_map/ppermute | solution.py:246
  1.6 18.2 %collective-permute-start.4 = (bf16[64,3200]{1,0:T(8,128)(2,1)}, bf16[64,3200]{1,0:T(8,128)(2,1)S(1)}, u32[]{:S(2)}, u32[]{:S(2)}) collective-permute-start(bf16[64,3200]{1,0:T(8,128)(2,1)} %vis.1), channel_id=1, source_target_pairs={{0,1},{1,0},{2,3},{3,2},{4,5},{5,4},{6,7},{7,6},{8,9},{9,8},{10,11... | collective-permute-start | bytes 1228808 | tf_op jit(solution)/shard_map/ppermute | solution.py:242
  6.6 20.8 %collective-permute-start.7 = (bf16[64,3200]{1,0:T(8,128)(2,1)}, bf16[64,3200]{1,0:T(8,128)(2,1)S(1)}, u32[]{:S(2)}, u32[]{:S(2)}) collective-permute-start(bf16[64,3200]{1,0:T(8,128)(2,1)} %vis.1), channel_id=1, source_target_pairs={{0,3},{3,0},{1,1},{2,2},{4,7},{7,4},{5,5},{6,6},{8,11},{11,8},{9,9... | collective-permute-start | bytes 1228808 | tf_op jit(solution)/shard_map/ppermute | solution.py:250
  10.5 1.2 %copy-start.2 = (bf16[256,2048]{1,0:T(8,128)(2,1)S(1)}, bf16[256,2048]{1,0:T(8,128)(2,1)}, u32[]{:S(2)}) copy-start(bf16[256,2048]{1,0:T(8,128)(2,1)} %text.3) | copy-start | bytes 3145732
  11.7 1.0 %copy-start.4 = (bf16[64,3200]{1,0:T(8,128)(2,1)S(1)}, bf16[64,3200]{1,0:T(8,128)(2,1)}, u32[]{:S(2)}) copy-start(bf16[64,3200]{1,0:T(8,128)(2,1)} %vis.1) | copy-start | bytes 1228804
  12.7 0.7 %copy-start.8 = (s32[4]{0:T(128)S(1)}, s32[4]{0:T(128)}, u32[]{:S(2)}) copy-start(s32[4]{0:T(128)} %owners.1) | copy-start | bytes 52
  13.4 0.7 %copy-start.9 = (s32[4]{0:T(128)S(1)}, s32[4]{0:T(128)}, u32[]{:S(2)}) copy-start(s32[4]{0:T(128)} %offsets.1) | copy-start | bytes 52
  14.0 5.6 %copy-start.5 = (f32[3200]{0:T(1024)S(1)}, f32[3200]{0:T(1024)}, u32[]{:S(2)}) copy-start(f32[3200]{0:T(1024)} %gain.3) | copy-start | bytes 38404
  14.0 13.4 %copy-start.6 = (f32[2048]{0:T(1024)S(1)}, f32[2048]{0:T(1024)}, u32[]{:S(2)}) copy-start(f32[2048]{0:T(1024)} %param.12) | copy-start | bytes 24580
  14.9 4.7 %copy-start = (bf16[3200,2048]{1,0:T(8,128)(2,1)S(1)}, bf16[3200,2048]{1,0:T(8,128)(2,1)}, u32[]{:S(2)}) copy-start(bf16[3200,2048]{1,0:T(8,128)(2,1)} %weight.7) | copy-start | bytes 39321604
  19.6 7.7 %copy-start.1 = (bf16[3200,2048]{1,0:T(8,128)(2,1)S(1)}, bf16[3200,2048]{1,0:T(8,128)(2,1)}, u32[]{:S(2)}) copy-start(bf16[3200,2048]{1,0:T(8,128)(2,1)} %weight.7) | copy-start | bytes 39321604
  19.9 12.0 %collective-permute-start.6 = (bf16[64,2176]{1,0:T(8,128)(2,1)S(1)}, bf16[64,2176]{1,0:T(8,128)(2,1)S(1)}, u32[]{:S(2)}, u32[]{:S(2)}) collective-permute-start(bf16[64,2176]{1,0:T(8,128)(2,1)S(1)} %get-tuple-element.32), channel_id=1, source_target_pairs={{0,2},{1,0},{2,3},{3,1},{4,6},{5,4},{6,7},{7,5},{8,10},{9,8},{10,1... | collective-permute-start | bytes 835592 | tf_op jit(solution)/shard_map/ppermute | solution.py:262
  19.9 15.0 %collective-permute-start.5 = (bf16[64,1024]{1,0:T(8,128)(2,1)S(1)}, bf16[64,1024]{1,0:T(8,128)(2,1)S(1)}, u32[]{:S(2)}, u32[]{:S(2)}) collective-permute-start(bf16[64,1024]{1,0:T(8,128)(2,1)S(1)} %get-tuple-element.31), channel_id=1, source_target_pairs={{0,2},{1,0},{2,3},{3,1},{4,6},{5,4},{6,7},{7,5},{8,10},{9,8},{10,1... | collective-permute-start | bytes 393224 | tf_op jit(solution)/shard_map/ppermute | solution.py:262
  23.0 11.9 %collective-permute-start = (f32[8,128]{1,0:T(8,128)S(1)}, f32[8,128]{1,0:T(8,128)S(1)}, u32[]{:S(2)}, u32[]{:S(2)}) collective-permute-start(f32[8,128]{1,0:T(8,128)S(1)} %get-tuple-element.25.i0), channel_id=1, source_target_pairs={{0,2},{1,3},{2,0},{3,1},{4,6},{5,7},{6,4},{7,5},{8,10},{9,11},{10,... | collective-permute-start | bytes 12296 | tf_op jit(solution)/shard_map/ppermute | solution.py:258
  23.0 11.9 %collective-permute-start.1 = (f32[8,128]{1,0:T(8,128)S(1)}, f32[8,128]{1,0:T(8,128)S(1)}, u32[]{:S(2)}, u32[]{:S(2)}) collective-permute-start(f32[8,128]{1,0:T(8,128)S(1)} %get-tuple-element.25.i0), channel_id=1, source_target_pairs={{0,3},{1,2},{2,1},{3,0},{4,7},{5,6},{6,5},{7,4},{8,11},{9,10},{10,... | collective-permute-start | bytes 12296 | tf_op jit(solution)/shard_map/ppermute | solution.py:254
  27.4 7.5 %collective-permute-start.2 = (f32[8,128]{1,0:T(8,128)S(1)}, f32[8,128]{1,0:T(8,128)S(1)}, u32[]{:S(2)}, u32[]{:S(2)}) collective-permute-start(f32[8,128]{1,0:T(8,128)S(1)} %get-tuple-element.25.i0), channel_id=1, source_target_pairs={{0,1},{1,0},{2,3},{3,2},{4,5},{5,4},{6,7},{7,6},{8,9},{9,8},{10,11... | collective-permute-start | bytes 12296 | tf_op jit(solution)/shard_map/ppermute | solution.py:242
  30.6 21.2 %copy-start.3 = (bf16[256,2048]{1,0:T(8,128)(2,1)S(1)}, bf16[256,2048]{1,0:T(8,128)(2,1)}, u32[]{:S(2)}) copy-start(bf16[256,2048]{1,0:T(8,128)(2,1)} %text.3) | copy-start | bytes 3145732
  30.6 21.2 %copy-start.7 = (f32[2048]{0:T(1024)S(1)}, f32[2048]{0:T(1024)}, u32[]{:S(2)}) copy-start(f32[2048]{0:T(1024)} %param.14) | copy-start | bytes 24580
  36.2 15.3 %collective-permute-start.10 = (bf16[64,2048]{1,0:T(8,128)(2,1)S(1)}, bf16[64,2048]{1,0:T(8,128)(2,1)S(1)}, u32[]{:S(2)}, u32[]{:S(2)}) collective-permute-start(bf16[64,2048]{1,0:T(8,128)(2,1)S(1)} %get-tuple-element.39), channel_id=1, source_target_pairs={{0,24},{4,28},{8,16},{12,20},{16,8},{20,12},{24,0},{28,4},{1,25},{... | collective-permute-start | bytes 786440 | tf_op jit(solution)/shard_map/ppermute | solution.py:266
  38.8 12.8 %collective-permute-start.8 = (bf16[64,2048]{1,0:T(8,128)(2,1)S(1)}, bf16[64,2048]{1,0:T(8,128)(2,1)S(1)}, u32[]{:S(2)}, u32[]{:S(2)}) collective-permute-start(bf16[64,2048]{1,0:T(8,128)(2,1)S(1)} %get-tuple-element.37), channel_id=1, source_target_pairs={{0,8},{4,12},{8,0},{12,4},{16,24},{20,28},{24,16},{28,20},{1,9},{5... | collective-permute-start | bytes 786440 | tf_op jit(solution)/shard_map/ppermute | solution.py:266
  39.3 12.3 %collective-permute-start.9 = (bf16[64,2048]{1,0:T(8,128)(2,1)S(1)}, bf16[64,2048]{1,0:T(8,128)(2,1)S(1)}, u32[]{:S(2)}, u32[]{:S(2)}) collective-permute-start(bf16[64,2048]{1,0:T(8,128)(2,1)S(1)} %get-tuple-element.38), channel_id=1, source_target_pairs={{0,16},{4,20},{8,24},{12,28},{16,0},{20,4},{24,8},{28,12},{1,17},{... | collective-permute-start | bytes 786440 | tf_op jit(solution)/shard_map/ppermute | solution.py:266
  51.6 2.0 %collective-permute-start.11 = (bf16[128,2048]{1,0:T(8,128)(2,1)S(1)}, bf16[128,2048]{1,0:T(8,128)(2,1)S(1)}, u32[]{:S(2)}, u32[]{:S(2)}) collective-permute-start(bf16[128,2048]{1,0:T(8,128)(2,1)S(1)} %pack.1), channel_id=1, source_target_pairs={{0,4},{4,0},{8,12},{12,8},{16,20},{20,16},{24,28},{28,24},{1,5},{5... | collective-permute-start | bytes 1572872 | tf_op jit(solution)/shard_map/ppermute | solution.py:266

commit v8 on v7

--- a/solution.py
+++ b/solution.py
@@ -191,7 +191,7 @@
 
 
 def base_kernel(groups, cap, size, scales, text_scale, gain, text, *rest):
-    *even, out, rows, done, sem = rest
+    *even, out, rows, done, sems = rest
     seq_len = text.shape[0]
     g = gain[...]
     order = moves(seq_len, cap, size, range(0, groups, 2), scales)
@@ -201,14 +201,18 @@
             at = (n * cap + r) * size
             rows[at : at + size, :] = x
     moved = jnp.dot(order.astype(BF16), rows[...], preferred_element_type=F32)
+    copies, stretch = [], seq_len // sems.shape[0]
     for c in range(seq_len // 16):
         inverse = jnp.concatenate([text_scale[:, 2 * c : 2 * c + 1], text_scale[:, 2 * c + 1 : 2 * c + 2]], axis=0)
         part = slice(c * 16, (c + 1) * 16)
         x = text[part, :].astype(F32) * inverse * g
         done[part, :] = jnp.where(covered[part] > 0, moved[part], x).astype(BF16)
-    copy = pltpu.make_async_copy(done, out, sem)
-    copy.start()
-    copy.wait()
+        if (c + 1) * 16 % stretch == 0:
+            there = slice((c + 1) * 16 - stretch, (c + 1) * 16)
+            copies.append(pltpu.make_async_copy(done.at[there], out.at[there], sems.at[len(copies)]))
+            copies[-1].start()
+    for copy in copies:
+        copy.wait()
 
 
 def place_kernel(groups, cap, size, scales, gain, odd, base, out, done, sems):
@@ -302,7 +306,7 @@
     x_inner, held = lax.optimization_barrier((x_inner, held))
     stretches = depth // 3 // 128 * 128
     stretches = (depth - stretches, stretches)
-    stretch = depth // 3 // 128 * 128
+    stretch = depth // 4 // 128 * 128
     sent, later = pl.pallas_call(
         pass_kernel,
         in_specs=[VMEM] * 3,
@@ -363,7 +367,7 @@
         cost_estimate=pl.CostEstimate(flops=0, bytes_accessed=4 * weight.size, transcendentals=0),
         name="scale",
     )(squares)
-    even = [parts[0]] + [across(parts[j], 2 * j) for j in range(1, pairs)]
+    even = [parts[0]] + [across(parts[j], 2 * j) for j in range(pairs - 1, 0, -1)][::-1]
     *even, squares = lax.optimization_barrier((*even, squares))
     arrived = jax.ShapeDtypeStruct((pairs * cap * size, columns), BF16)
     odd = pl.pallas_call(
@@ -376,7 +380,7 @@
         in_specs=[VMEM] * (4 + pairs),
         out_specs=ANY,
         out_shape=jax.ShapeDtypeStruct(text.shape, BF16),
-        scratch_shapes=[pltpu.VMEM(arrived.shape, BF16), pltpu.VMEM(text.shape, BF16), pltpu.SemaphoreType.DMA],
+        scratch_shapes=[pltpu.VMEM(arrived.shape, BF16), pltpu.VMEM(text.shape, BF16), pltpu.SemaphoreType.DMA((4,))],
         compiler_params=small,
         cost_estimate=pl.CostEstimate(flops=0, bytes_accessed=2 * weight.size, transcendentals=0),
         name="base",

time: 55 us -> 54.7 us (level)
    ppermute x1, waiting for transfers between devices: 1.34 us -> 0.45 us  [second(): return lax.ppermute(x, 'dp', [(0, 2), (1, 3), (2, 0), (3, 1)])]
    ppermute x2, waiting for transfers between devices: 1.23 us -> 1.93 us  [far(): return lax.ppermute(x, 'dp', [(0, 2), (1, 0), (2, 3), (3, 1)])]
where the time goes in v8:
time: 54.7 us; the launch traced here: 54.3 us
  starting transfers between devices  17.9 us (33%)
  blocking collectives  11.7 us (21%)
  Pallas kernels  10.2 us (19%)
  local copies, waits for them, and re-layouts  8.28 us (15%)
  waiting for transfers between devices  5.38 us (10%)
  between operations  0.78 us (1%)
    all_to_all x1, blocking collectives, fast(): squares = lax.all_to_all(squares, ('grp', 'dp'), 0, 0, tiled=True)  11.7 us
    unnamed x20, local copies, waits for them, and re-layouts  8.28 us
    ppermute x2, starting transfers between devices, outer(): return lax.ppermute(x, 'dp', [(0, 1), (1, 0), (2, 3), (3, 2)])  4.92 us
    ppermute x4, starting transfers between devices, across(): lax.ppermute(x, 'grp', [(i, i ^ k) for i in range(lax.axis_size('grp'))])  3.62 us
    pallas_call x1, Pallas kernels, fast(): pl.pallas_call(early_kernel, in_specs=[VMEM] * 7, out_specs=VMEM, out_sha...  3.25 us
    ppermute x1, starting transfers between devices, ends(): return lax.ppermute(x, 'dp', [(0, 3), (3, 0), (1, 1), (2, 2)])  3.24 us
    ppermute x2, starting transfers between devices, far(): return lax.ppermute(x, 'dp', [(0, 2), (1, 0), (2, 3), (3, 1)])  3.08 us
    ppermute x1, waiting for transfers between devices, ends(): return lax.ppermute(x, 'dp', [(0, 3), (3, 0), (1, 1), (2, 2)])  2.97 us
  transfers between devices with their start and end apart: 12, of which 3 were waited for; matrix products, arithmetic and copies ran while one was open for 0% of the time, Pallas kernels for 15%

profile of v8, /device:TPU:0, one launch (start us, length us, event | category | flops | bytes accessed | tf_op | source)
XLA Modules:
  0.0 54.3 jit_solution(15735950388571576999)
XLA Ops:
  0.0 1.6 %collective-permute-start.3 = (bf16[64,3200]{1,0:T(8,128)(2,1)}, bf16[64,3200]{1,0:T(8,128)(2,1)S(1)}, u32[]{:S(2)}, u32[]{:S(2)}) collective-permute-start(bf16[64,3200]{1,0:T(8,128)(2,1)} %vis.1), channel_id=1, source_target_pairs={{1,2},{2,1},{0,0},{3,3},{5,6},{6,5},{4,4},{7,7},{9,10},{10,9},{8,8... | collective-permute-start | bytes 1228808 | tf_op jit(solution)/shard_map/ppermute | solution.py:250
  1.6 4.9 %collective-permute-start.4 = (bf16[64,3200]{1,0:T(8,128)(2,1)}, bf16[64,3200]{1,0:T(8,128)(2,1)S(1)}, u32[]{:S(2)}, u32[]{:S(2)}) collective-permute-start(bf16[64,3200]{1,0:T(8,128)(2,1)} %vis.1), channel_id=1, source_target_pairs={{0,1},{1,0},{2,3},{3,2},{4,5},{5,4},{6,7},{7,6},{8,9},{9,8},{10,11... | collective-permute-start | bytes 1228808 | tf_op jit(solution)/shard_map/ppermute | solution.py:246
  6.6 3.2 %collective-permute-start.7 = (bf16[64,3200]{1,0:T(8,128)(2,1)}, bf16[64,3200]{1,0:T(8,128)(2,1)S(1)}, u32[]{:S(2)}, u32[]{:S(2)}) collective-permute-start(bf16[64,3200]{1,0:T(8,128)(2,1)} %vis.1), channel_id=1, source_target_pairs={{0,3},{3,0},{1,1},{2,2},{4,7},{7,4},{5,5},{6,6},{8,11},{11,8},{9,9... | collective-permute-start | bytes 1228808 | tf_op jit(solution)/shard_map/ppermute | solution.py:254
  10.5 0.0 copy-start.2
  10.5 1.2 %copy-done.2 = bf16[256,2048]{1,0:T(8,128)(2,1)S(1)} copy-done((bf16[256,2048]{1,0:T(8,128)(2,1)S(1)}, bf16[256,2048]{1,0:T(8,128)(2,1)}, u32[]{:S(2)}) %copy-start.2) | copy-done | bytes 1048600
  11.7 0.0 copy-start.4
  11.7 1.0 %copy-done.4 = bf16[64,3200]{1,0:T(8,128)(2,1)S(1)} copy-done((bf16[64,3200]{1,0:T(8,128)(2,1)S(1)}, bf16[64,3200]{1,0:T(8,128)(2,1)}, u32[]{:S(2)}) %copy-start.4) | copy-done | bytes 409624
  12.7 0.0 copy-start.8
  12.7 0.7 %copy-done.8 = s32[4]{0:T(128)S(1)} copy-done((s32[4]{0:T(128)S(1)}, s32[4]{0:T(128)}, u32[]{:S(2)}) %copy-start.8) | copy-done | bytes 40
  13.4 0.0 copy-start.9
  13.4 0.7 %copy-done.9 = s32[4]{0:T(128)S(1)} copy-done((s32[4]{0:T(128)S(1)}, s32[4]{0:T(128)}, u32[]{:S(2)}) %copy-start.9) | copy-done | bytes 40
  14.0 0.0 copy-start.5
  14.0 0.0 copy-start.6
  14.0 0.9 %tables.1 = (f32[8,128]{1,0:T(8,128)S(1)}, bf16[64,3200]{1,0:T(8,128)(2,1)S(1)}, f32[8,128]{1,0:T(8,128)S(1)}) custom-call(bf16[256,2048]{1,0:T(8,128)(2,1)S(1)} %copy-done.2, bf16[64,3200]{1,0:T(8,128)(2,1)S(1)} %copy-done.4, s32[4]{0:T(128)S(1)} %copy-done.8, s32[4]{0:T(128)S(1)} %copy-done.9, s32[1]{0:T(128)S(6)} %copy.13.counts), custom_call_target="tpu_custom_call" | custom-call | tf_op jit(solution)/shard_map/tables/pallas_call | solution.py:287
  14.9 0.0 copy-start
  14.9 4.7 %copy-done = bf16[3200,2048]{1,0:T(8,128)(2,1)S(1)} copy-done((bf16[3200,2048]{1,0:T(8,128)(2,1)S(1)}, bf16[3200,2048]{1,0:T(8,128)(2,1)}, u32[]{:S(2)}) %copy-start) | copy-done | bytes 13107224
  19.6 0.0 copy-start.1
  19.6 0.0 collective-permute-done.3.inner
  19.6 0.0 copy-done.5
  19.6 0.2 pass.1
  19.9 0.0 collective-permute-done.4.outer
  19.9 0.1 collective-permute-start.6
  19.9 3.0 %collective-permute-start.5 = (bf16[64,768]{1,0:T(8,128)(2,1)S(1)}, bf16[64,768]{1,0:T(8,128)(2,1)S(1)}, u32[]{:S(2)}, u32[]{:S(2)}) collective-permute-start(bf16[64,768]{1,0:T(8,128)(2,1)S(1)} %get-tuple-element.31), channel_id=1, source_target_pairs={{0,2},{1,0},{2,3},{3,1},{4,6},{5,4},{6,7},{7,5},{8,10},{9,8},{10,1... | collective-permute-start | bytes 294920 | tf_op jit(solution)/shard_map/ppermute | solution.py:266
  23.0 0.1 collective-permute-start
  23.0 1.3 %collective-permute-start.1 = (f32[8,128]{1,0:T(8,128)S(1)}, f32[8,128]{1,0:T(8,128)S(1)}, u32[]{:S(2)}, u32[]{:S(2)}) collective-permute-start(f32[8,128]{1,0:T(8,128)S(1)} %get-tuple-element.25.i0), channel_id=1, source_target_pairs={{0,3},{1,2},{2,1},{3,0},{4,7},{5,6},{6,5},{7,4},{8,11},{9,10},{10,... | collective-permute-start | bytes 12296 | tf_op jit(solution)/shard_map/ppermute | solution.py:258
  24.4 3.0 %collective-permute-done.7.ends = bf16[64,3200]{1,0:T(8,128)(2,1)S(1)} collective-permute-done((bf16[64,3200]{1,0:T(8,128)(2,1)}, bf16[64,3200]{1,0:T(8,128)(2,1)S(1)}, u32[]{:S(2)}, u32[]{:S(2)}) %collective-permute-start.7) | collective-permute-done | bytes 409632 | tf_op jit(solution)/shard_map/ppermute | solution.py:254
  27.4 0.0 collective-permute-start.2
  27.4 0.0 copy-done.6
  27.4 0.0 copy-done.1
  27.4 3.3 %early.1 = bf16[192,2048]{1,0:T(8,128)(2,1)S(1)} custom-call(bf16[64,3200]{1,0:T(8,128)(2,1)S(1)} %get-tuple-element.26.own, bf16[64,3200]{1,0:T(8,128)(2,1)S(1)} %collective-permute-done.4.outer, bf16[64,3200]{1,0:T(8,128)(2,1)S(1)} %collective-permute-done.3.inner, bf16[64,3200]{1,0:T(8,128)(2,1)S(1)} %collective-permute-done.7.ends, f32[3200]{0:T(1024)S(1)} %copy-done.5, ...), custom_call_target="tpu_custom_call" | custom-call | tf_op jit(solution)/shard_map/early/pallas_call | solution.py:325
  30.6 0.0 copy-start.3
  30.6 0.0 copy-start.7
  30.7 1.9 %collective-permute-done.6.last = bf16[64,2432]{1,0:T(8,128)(2,1)S(1)} collective-permute-done((bf16[64,2432]{1,0:T(8,128)(2,1)S(1)}, bf16[64,2432]{1,0:T(8,128)(2,1)S(1)}, u32[]{:S(2)}, u32[]{:S(2)}) %collective-permute-start.6) | collective-permute-done | bytes 311328 | tf_op jit(solution)/shard_map/ppermute | solution.py:266
  32.6 1.8 %late.1.total = f32[64,2048]{1,0:T(8,128)S(1)} custom-call(bf16[64,2432]{1,0:T(8,128)(2,1)S(1)} %collective-permute-done.6.last, bf16[3200,2048]{1,0:T(8,128)(2,1)S(1)} %copy-done.1, f32[1,2048]{1,0:T(1,128)S(1)} %bitcast.8), custom_call_target="tpu_custom_call" | custom-call | tf_op jit(solution)/shard_map/late/pallas_call | solution.py:336
  34.4 0.5 collective-permute-done.i3
  34.9 0.0 collective-permute-done.1.i2
  34.9 0.0 collective-permute-done.2.i1
  34.9 0.0 collective-permute-done.5.last
  34.9 1.2 %project.1 = (bf16[64,2048]{1,0:T(8,128)(2,1)S(1)}, bf16[64,2048]{1,0:T(8,128)(2,1)S(1)}, bf16[64,2048]{1,0:T(8,128)(2,1)S(1)}, bf16[64,2048]{1,0:T(8,128)(2,1)S...) custom-call(f32[8,128]{1,0:T(8,128)S(1)} %collective-permute-done.i3, f32[8,128]{1,0:T(8,128)S(1)} %collective-permute-done.1.i2, ...), custom_call_target="tpu_custom_call" | custom-call | flops 2516582400 | bytes 13107200 | tf_op jit(solution)/shard_map/project/pallas_call | solution.py:345
  36.1 2.5 %collective-permute-start.10 = (bf16[64,2048]{1,0:T(8,128)(2,1)S(1)}, bf16[64,2048]{1,0:T(8,128)(2,1)S(1)}, u32[]{:S(2)}, u32[]{:S(2)}) collective-permute-start(bf16[64,2048]{1,0:T(8,128)(2,1)S(1)} %get-tuple-element.39), channel_id=1, source_target_pairs={{0,24},{4,28},{8,16},{12,20},{16,8},{20,12},{24,0},{28,4},{1,25},{... | collective-permute-start | bytes 786440 | tf_op jit(solution)/shard_map/ppermute | solution.py:270
  38.6 0.5 collective-permute-start.8
  39.1 0.5 collective-permute-start.9
  39.6 11.7 %all_to_all.11 = f32[32,1,128]{2,1,0:T(1,128)S(1)} all-to-all(f32[32,1,128]{2,1,0:T(1,128)S(1)} %bitcast.11), channel_id=1, replica_groups=mesh['grp'=8,'dp'=4] {'grp','dp'}, dimensions={0} | all-to-all | bytes 32768 | tf_op jit(solution)/shard_map/all_to_all | solution.py:360
  51.4 0.0 collective-permute-done.10.refs_3_.rest_3_
  51.4 0.0 collective-permute-done.8.refs_1_.rest_1_
  51.4 0.0 collective-permute-done.9.refs_2_.rest_2_
  51.4 0.1 collective-permute-start.11
  51.5 0.2 scale.1.scales
  51.7 0.0 copy-done.3
  51.7 0.0 copy-done.7
  51.7 1.7 %base.1 = bf16[256,2048]{1,0:T(8,128)(2,1)} custom-call(f32[128,128]{1,0:T(8,128)S(1)} %scale.1.scales, f32[8,128]{1,0:T(8,128)S(1)} %get-tuple-element.44.text_scale, f32[1,2048]{1,0:T(1,128)S(1)} %bitcast.9, bf16[256,2048]{1,0:T(8,128)(2,1)S(1)} %copy-done.3, bf16[64,2048]{1,0:T(8,128)(2,1)S(1)} %get-tuple-element.40.refs_0_.rest_0_, ...), custom_call_target="tpu_custom_call" | custom-call | bytes 13107200 | tf_op jit(solution)/shard_map/base/pallas_call | solution.py:378
  53.4 0.0 collective-permute-done.11.odd
  53.4 0.9 %place.1 = bf16[256,2048]{1,0:T(8,128)(2,1)} custom-call(f32[128,128]{1,0:T(8,128)S(1)} %scale.1.scales, f32[1,2048]{1,0:T(1,128)S(1)} %bitcast.10, bf16[128,2048]{1,0:T(8,128)(2,1)S(1)} %collective-permute-done.11.odd, bf16[256,2048]{1,0:T(8,128)(2,1)} %base.1), custom_call_target="tpu_custom_call", output_to_operand_aliasing={{}: (3, {})} | custom-call | tf_op jit(solution)/shard_map/place/pallas_call | solution.py:388
  (2 shorter events, 0.0 us)
Async XLA Ops:
  0.0 19.6 %collective-permute-start.3 = (bf16[64,3200]{1,0:T(8,128)(2,1)}, bf16[64,3200]{1,0:T(8,128)(2,1)S(1)}, u32[]{:S(2)}, u32[]{:S(2)}) collective-permute-start(bf16[64,3200]{1,0:T(8,128)(2,1)} %vis.1), channel_id=1, source_target_pairs={{1,2},{2,1},{0,0},{3,3},{5,6},{6,5},{4,4},{7,7},{9,10},{10,9},{8,8... | collective-permute-start | bytes 1228808 | tf_op jit(solution)/shard_map/ppermute | solution.py:250
  1.6 18.2 %collective-permute-start.4 = (bf16[64,3200]{1,0:T(8,128)(2,1)}, bf16[64,3200]{1,0:T(8,128)(2,1)S(1)}, u32[]{:S(2)}, u32[]{:S(2)}) collective-permute-start(bf16[64,3200]{1,0:T(8,128)(2,1)} %vis.1), channel_id=1, source_target_pairs={{0,1},{1,0},{2,3},{3,2},{4,5},{5,4},{6,7},{7,6},{8,9},{9,8},{10,11... | collective-permute-start | bytes 1228808 | tf_op jit(solution)/shard_map/ppermute | solution.py:246
  6.6 20.8 %collective-permute-start.7 = (bf16[64,3200]{1,0:T(8,128)(2,1)}, bf16[64,3200]{1,0:T(8,128)(2,1)S(1)}, u32[]{:S(2)}, u32[]{:S(2)}) collective-permute-start(bf16[64,3200]{1,0:T(8,128)(2,1)} %vis.1), channel_id=1, source_target_pairs={{0,3},{3,0},{1,1},{2,2},{4,7},{7,4},{5,5},{6,6},{8,11},{11,8},{9,9... | collective-permute-start | bytes 1228808 | tf_op jit(solution)/shard_map/ppermute | solution.py:254
  10.5 1.2 %copy-start.2 = (bf16[256,2048]{1,0:T(8,128)(2,1)S(1)}, bf16[256,2048]{1,0:T(8,128)(2,1)}, u32[]{:S(2)}) copy-start(bf16[256,2048]{1,0:T(8,128)(2,1)} %text.3) | copy-start | bytes 3145732
  11.7 1.0 %copy-start.4 = (bf16[64,3200]{1,0:T(8,128)(2,1)S(1)}, bf16[64,3200]{1,0:T(8,128)(2,1)}, u32[]{:S(2)}) copy-start(bf16[64,3200]{1,0:T(8,128)(2,1)} %vis.1) | copy-start | bytes 1228804
  12.7 0.7 %copy-start.8 = (s32[4]{0:T(128)S(1)}, s32[4]{0:T(128)}, u32[]{:S(2)}) copy-start(s32[4]{0:T(128)} %owners.1) | copy-start | bytes 52
  13.4 0.7 %copy-start.9 = (s32[4]{0:T(128)S(1)}, s32[4]{0:T(128)}, u32[]{:S(2)}) copy-start(s32[4]{0:T(128)} %offsets.1) | copy-start | bytes 52
  14.0 5.6 %copy-start.5 = (f32[3200]{0:T(1024)S(1)}, f32[3200]{0:T(1024)}, u32[]{:S(2)}) copy-start(f32[3200]{0:T(1024)} %gain.3) | copy-start | bytes 38404
  14.0 13.4 %copy-start.6 = (f32[2048]{0:T(1024)S(1)}, f32[2048]{0:T(1024)}, u32[]{:S(2)}) copy-start(f32[2048]{0:T(1024)} %param.12) | copy-start | bytes 24580
  14.9 4.7 %copy-start = (bf16[3200,2048]{1,0:T(8,128)(2,1)S(1)}, bf16[3200,2048]{1,0:T(8,128)(2,1)}, u32[]{:S(2)}) copy-start(bf16[3200,2048]{1,0:T(8,128)(2,1)} %weight.7) | copy-start | bytes 39321604
  19.6 7.7 %copy-start.1 = (bf16[3200,2048]{1,0:T(8,128)(2,1)S(1)}, bf16[3200,2048]{1,0:T(8,128)(2,1)}, u32[]{:S(2)}) copy-start(bf16[3200,2048]{1,0:T(8,128)(2,1)} %weight.7) | copy-start | bytes 39321604
  19.9 12.7 %collective-permute-start.6 = (bf16[64,2432]{1,0:T(8,128)(2,1)S(1)}, bf16[64,2432]{1,0:T(8,128)(2,1)S(1)}, u32[]{:S(2)}, u32[]{:S(2)}) collective-permute-start(bf16[64,2432]{1,0:T(8,128)(2,1)S(1)} %get-tuple-element.32), channel_id=1, source_target_pairs={{0,2},{1,0},{2,3},{3,1},{4,6},{5,4},{6,7},{7,5},{8,10},{9,8},{10,1... | collective-permute-start | bytes 933896 | tf_op jit(solution)/shard_map/ppermute | solution.py:266
  19.9 15.0 %collective-permute-start.5 = (bf16[64,768]{1,0:T(8,128)(2,1)S(1)}, bf16[64,768]{1,0:T(8,128)(2,1)S(1)}, u32[]{:S(2)}, u32[]{:S(2)}) collective-permute-start(bf16[64,768]{1,0:T(8,128)(2,1)S(1)} %get-tuple-element.31), channel_id=1, source_target_pairs={{0,2},{1,0},{2,3},{3,1},{4,6},{5,4},{6,7},{7,5},{8,10},{9,8},{10,1... | collective-permute-start | bytes 294920 | tf_op jit(solution)/shard_map/ppermute | solution.py:266
  23.0 11.9 %collective-permute-start = (f32[8,128]{1,0:T(8,128)S(1)}, f32[8,128]{1,0:T(8,128)S(1)}, u32[]{:S(2)}, u32[]{:S(2)}) collective-permute-start(f32[8,128]{1,0:T(8,128)S(1)} %get-tuple-element.25.i0), channel_id=1, source_target_pairs={{0,2},{1,3},{2,0},{3,1},{4,6},{5,7},{6,4},{7,5},{8,10},{9,11},{10,... | collective-permute-start | bytes 12296 | tf_op jit(solution)/shard_map/ppermute | solution.py:262
  23.0 11.9 %collective-permute-start.1 = (f32[8,128]{1,0:T(8,128)S(1)}, f32[8,128]{1,0:T(8,128)S(1)}, u32[]{:S(2)}, u32[]{:S(2)}) collective-permute-start(f32[8,128]{1,0:T(8,128)S(1)} %get-tuple-element.25.i0), channel_id=1, source_target_pairs={{0,3},{1,2},{2,1},{3,0},{4,7},{5,6},{6,5},{7,4},{8,11},{9,10},{10,... | collective-permute-start | bytes 12296 | tf_op jit(solution)/shard_map/ppermute | solution.py:258
  27.4 7.5 %collective-permute-start.2 = (f32[8,128]{1,0:T(8,128)S(1)}, f32[8,128]{1,0:T(8,128)S(1)}, u32[]{:S(2)}, u32[]{:S(2)}) collective-permute-start(f32[8,128]{1,0:T(8,128)S(1)} %get-tuple-element.25.i0), channel_id=1, source_target_pairs={{0,1},{1,0},{2,3},{3,2},{4,5},{5,4},{6,7},{7,6},{8,9},{9,8},{10,11... | collective-permute-start | bytes 12296 | tf_op jit(solution)/shard_map/ppermute | solution.py:246
  30.6 21.0 %copy-start.3 = (bf16[256,2048]{1,0:T(8,128)(2,1)S(1)}, bf16[256,2048]{1,0:T(8,128)(2,1)}, u32[]{:S(2)}) copy-start(bf16[256,2048]{1,0:T(8,128)(2,1)} %text.3) | copy-start | bytes 3145732
  30.6 21.0 %copy-start.7 = (f32[2048]{0:T(1024)S(1)}, f32[2048]{0:T(1024)}, u32[]{:S(2)}) copy-start(f32[2048]{0:T(1024)} %param.14) | copy-start | bytes 24580
  36.1 15.3 %collective-permute-start.10 = (bf16[64,2048]{1,0:T(8,128)(2,1)S(1)}, bf16[64,2048]{1,0:T(8,128)(2,1)S(1)}, u32[]{:S(2)}, u32[]{:S(2)}) collective-permute-start(bf16[64,2048]{1,0:T(8,128)(2,1)S(1)} %get-tuple-element.39), channel_id=1, source_target_pairs={{0,24},{4,28},{8,16},{12,20},{16,8},{20,12},{24,0},{28,4},{1,25},{... | collective-permute-start | bytes 786440 | tf_op jit(solution)/shard_map/ppermute | solution.py:270
  38.6 12.8 %collective-permute-start.8 = (bf16[64,2048]{1,0:T(8,128)(2,1)S(1)}, bf16[64,2048]{1,0:T(8,128)(2,1)S(1)}, u32[]{:S(2)}, u32[]{:S(2)}) collective-permute-start(bf16[64,2048]{1,0:T(8,128)(2,1)S(1)} %get-tuple-element.37), channel_id=1, source_target_pairs={{0,8},{4,12},{8,0},{12,4},{16,24},{20,28},{24,16},{28,20},{1,9},{5... | collective-permute-start | bytes 786440 | tf_op jit(solution)/shard_map/ppermute | solution.py:270
  39.1 12.2 %collective-permute-start.9 = (bf16[64,2048]{1,0:T(8,128)(2,1)S(1)}, bf16[64,2048]{1,0:T(8,128)(2,1)S(1)}, u32[]{:S(2)}, u32[]{:S(2)}) collective-permute-start(bf16[64,2048]{1,0:T(8,128)(2,1)S(1)} %get-tuple-element.38), channel_id=1, source_target_pairs={{0,16},{4,20},{8,24},{12,28},{16,0},{20,4},{24,8},{28,12},{1,17},{... | collective-permute-start | bytes 786440 | tf_op jit(solution)/shard_map/ppermute | solution.py:270
  51.4 2.0 %collective-permute-start.11 = (bf16[128,2048]{1,0:T(8,128)(2,1)S(1)}, bf16[128,2048]{1,0:T(8,128)(2,1)S(1)}, u32[]{:S(2)}, u32[]{:S(2)}) collective-permute-start(bf16[128,2048]{1,0:T(8,128)(2,1)S(1)} %pack.1), channel_id=1, source_target_pairs={{0,4},{4,0},{8,12},{12,8},{16,20},{20,16},{24,28},{28,24},{1,5},{5... | collective-permute-start | bytes 1572872 | tf_op jit(solution)/shard_map/ppermute | solution.py:270

commit v9 on v8

--- a/solution.py
+++ b/solution.py
@@ -190,8 +190,9 @@
     return (lax.broadcasted_iota(jnp.int32, (seq_len, code.shape[1]), 0) == target).astype(F32)
 
 
-def base_kernel(groups, cap, size, scales, text_scale, gain, text, *rest):
-    *even, out, rows, done, sems = rest
+def base_kernel(groups, dp, cap, size, width, squares, text_scale, gain, text, *rest):
+    *even, out, scales, rows, done, sems = rest
+    scale_kernel(groups, dp, cap * size, width, squares, scales)
     seq_len = text.shape[0]
     g = gain[...]
     order = moves(seq_len, cap, size, range(0, groups, 2), scales)
@@ -358,15 +359,6 @@
         name="project",
     )(*known, last_b, weight, total, early, held)
     squares = lax.all_to_all(squares, ("grp", "dp"), 0, 0, tiled=True)
-    scales = pl.pallas_call(
-        functools.partial(scale_kernel, groups, dp, cap * size, columns * dp),
-        in_specs=[VMEM],
-        out_specs=VMEM,
-        out_shape=jax.ShapeDtypeStruct((128, 128), F32),
-        compiler_params=small,
-        cost_estimate=pl.CostEstimate(flops=0, bytes_accessed=4 * weight.size, transcendentals=0),
-        name="scale",
-    )(squares)
     even = [parts[0]] + [across(parts[j], 2 * j) for j in range(pairs - 1, 0, -1)][::-1]
     *even, squares = lax.optimization_barrier((*even, squares))
     arrived = jax.ShapeDtypeStruct((pairs * cap * size, columns), BF16)
@@ -375,16 +367,16 @@
     )(*even)
     odd = across(odd, 1)
     gain = out_gain[None, :]
-    base = pl.pallas_call(
-        functools.partial(base_kernel, groups, cap, size),
+    base, scales = pl.pallas_call(
+        functools.partial(base_kernel, groups, dp, cap, size, columns * dp),
         in_specs=[VMEM] * (4 + pairs),
-        out_specs=ANY,
-        out_shape=jax.ShapeDtypeStruct(text.shape, BF16),
+        out_specs=[ANY, VMEM],
+        out_shape=[jax.ShapeDtypeStruct(text.shape, BF16), jax.ShapeDtypeStruct((128, 128), F32)],
         scratch_shapes=[pltpu.VMEM(arrived.shape, BF16), pltpu.VMEM(text.shape, BF16), pltpu.SemaphoreType.DMA((4,))],
         compiler_params=small,
         cost_estimate=pl.CostEstimate(flops=0, bytes_accessed=2 * weight.size, transcendentals=0),
         name="base",
-    )(scales, text_scale, gain, text, *even)
+    )(squares, text_scale, gain, text, *even)
     return pl.pallas_call(
         functools.partial(place_kernel, groups, cap, size),
         in_specs=[VMEM] * 3 + [ANY],

time: 54.7 us -> 54.7 us (level)
    pallas_call x2 -> x1, Pallas kernels: 1.86 us -> 1.85 us  [fast(): pl.pallas_call(functools.partial(base_kernel, groups, dp, cap, size, colu...]
where the time goes in v9:
time: 54.7 us; the launch traced here: 54.3 us
  starting transfers between devices  17.9 us (33%)
  blocking collectives  11.7 us (21%)
  Pallas kernels  10.2 us (19%)
  local copies, waits for them, and re-layouts  8.28 us (15%)
  waiting for transfers between devices  5.39 us (10%)
  between operations  0.79 us (1%)
    all_to_all x1, blocking collectives, fast(): squares = lax.all_to_all(squares, ('grp', 'dp'), 0, 0, tiled=True)  11.7 us
    unnamed x20, local copies, waits for them, and re-layouts  8.28 us
    ppermute x2, starting transfers between devices, outer(): return lax.ppermute(x, 'dp', [(0, 1), (1, 0), (2, 3), (3, 2)])  4.92 us
    ppermute x4, starting transfers between devices, across(): lax.ppermute(x, 'grp', [(i, i ^ k) for i in range(lax.axis_size('grp'))])  3.62 us
    pallas_call x1, Pallas kernels, fast(): pl.pallas_call(early_kernel, in_specs=[VMEM] * 7, out_specs=VMEM, out_sha...  3.25 us
    ppermute x1, starting transfers between devices, ends(): return lax.ppermute(x, 'dp', [(0, 3), (3, 0), (1, 1), (2, 2)])  3.24 us
    ppermute x2, starting transfers between devices, far(): return lax.ppermute(x, 'dp', [(0, 2), (1, 0), (2, 3), (3, 1)])  3.08 us
    ppermute x1, waiting for transfers between devices, ends(): return lax.ppermute(x, 'dp', [(0, 3), (3, 0), (1, 1), (2, 2)])  2.97 us
  transfers between devices with their start and end apart: 12, of which 3 were waited for; matrix products, arithmetic and copies ran while one was open for 0% of the time, Pallas kernels for 15%

profile of v9, /device:TPU:0, one launch (start us, length us, event | category | flops | bytes accessed | tf_op | source)
XLA Modules:
  0.0 54.3 jit_solution(5030966873300129069)
XLA Ops:
  0.0 1.6 %collective-permute-start.3 = (bf16[64,3200]{1,0:T(8,128)(2,1)}, bf16[64,3200]{1,0:T(8,128)(2,1)S(1)}, u32[]{:S(2)}, u32[]{:S(2)}) collective-permute-start(bf16[64,3200]{1,0:T(8,128)(2,1)} %vis.1), channel_id=1, source_target_pairs={{1,2},{2,1},{0,0},{3,3},{5,6},{6,5},{4,4},{7,7},{9,10},{10,9},{8,8... | collective-permute-start | bytes 1228808 | tf_op jit(solution)/shard_map/ppermute | solution.py:251
  1.6 4.9 %collective-permute-start.4 = (bf16[64,3200]{1,0:T(8,128)(2,1)}, bf16[64,3200]{1,0:T(8,128)(2,1)S(1)}, u32[]{:S(2)}, u32[]{:S(2)}) collective-permute-start(bf16[64,3200]{1,0:T(8,128)(2,1)} %vis.1), channel_id=1, source_target_pairs={{0,1},{1,0},{2,3},{3,2},{4,5},{5,4},{6,7},{7,6},{8,9},{9,8},{10,11... | collective-permute-start | bytes 1228808 | tf_op jit(solution)/shard_map/ppermute | solution.py:247
  6.6 3.2 %collective-permute-start.7 = (bf16[64,3200]{1,0:T(8,128)(2,1)}, bf16[64,3200]{1,0:T(8,128)(2,1)S(1)}, u32[]{:S(2)}, u32[]{:S(2)}) collective-permute-start(bf16[64,3200]{1,0:T(8,128)(2,1)} %vis.1), channel_id=1, source_target_pairs={{0,3},{3,0},{1,1},{2,2},{4,7},{7,4},{5,5},{6,6},{8,11},{11,8},{9,9... | collective-permute-start | bytes 1228808 | tf_op jit(solution)/shard_map/ppermute | solution.py:255
  10.5 0.0 copy-start.2
  10.5 1.2 %copy-done.2 = bf16[256,2048]{1,0:T(8,128)(2,1)S(1)} copy-done((bf16[256,2048]{1,0:T(8,128)(2,1)S(1)}, bf16[256,2048]{1,0:T(8,128)(2,1)}, u32[]{:S(2)}) %copy-start.2) | copy-done | bytes 1048600
  11.7 0.0 copy-start.4
  11.7 1.0 %copy-done.4 = bf16[64,3200]{1,0:T(8,128)(2,1)S(1)} copy-done((bf16[64,3200]{1,0:T(8,128)(2,1)S(1)}, bf16[64,3200]{1,0:T(8,128)(2,1)}, u32[]{:S(2)}) %copy-start.4) | copy-done | bytes 409624
  12.7 0.0 copy-start.8
  12.7 0.7 %copy-done.8 = s32[4]{0:T(128)S(1)} copy-done((s32[4]{0:T(128)S(1)}, s32[4]{0:T(128)}, u32[]{:S(2)}) %copy-start.8) | copy-done | bytes 40
  13.4 0.0 copy-start.9
  13.4 0.7 %copy-done.9 = s32[4]{0:T(128)S(1)} copy-done((s32[4]{0:T(128)S(1)}, s32[4]{0:T(128)}, u32[]{:S(2)}) %copy-start.9) | copy-done | bytes 40
  14.0 0.0 copy-start.5
  14.0 0.0 copy-start.6
  14.0 0.9 %tables.1 = (f32[8,128]{1,0:T(8,128)S(1)}, bf16[64,3200]{1,0:T(8,128)(2,1)S(1)}, f32[8,128]{1,0:T(8,128)S(1)}) custom-call(bf16[256,2048]{1,0:T(8,128)(2,1)S(1)} %copy-done.2, bf16[64,3200]{1,0:T(8,128)(2,1)S(1)} %copy-done.4, s32[4]{0:T(128)S(1)} %copy-done.8, s32[4]{0:T(128)S(1)} %copy-done.9, s32[1]{0:T(128)S(6)} %copy.13.counts), custom_call_target="tpu_custom_call" | custom-call | tf_op jit(solution)/shard_map/tables/pallas_call | solution.py:288
  14.9 0.0 copy-start
  14.9 4.7 %copy-done = bf16[3200,2048]{1,0:T(8,128)(2,1)S(1)} copy-done((bf16[3200,2048]{1,0:T(8,128)(2,1)S(1)}, bf16[3200,2048]{1,0:T(8,128)(2,1)}, u32[]{:S(2)}) %copy-start) | copy-done | bytes 13107224
  19.6 0.0 copy-start.1
  19.6 0.0 collective-permute-done.3.inner
  19.6 0.0 copy-done.5
  19.6 0.2 pass.1
  19.9 0.0 collective-permute-done.4.outer
  19.9 0.1 collective-permute-start.6
  19.9 3.0 %collective-permute-start.5 = (bf16[64,768]{1,0:T(8,128)(2,1)S(1)}, bf16[64,768]{1,0:T(8,128)(2,1)S(1)}, u32[]{:S(2)}, u32[]{:S(2)}) collective-permute-start(bf16[64,768]{1,0:T(8,128)(2,1)S(1)} %get-tuple-element.34), channel_id=1, source_target_pairs={{0,2},{1,0},{2,3},{3,1},{4,6},{5,4},{6,7},{7,5},{8,10},{9,8},{10,1... | collective-permute-start | bytes 294920 | tf_op jit(solution)/shard_map/ppermute | solution.py:267
  23.0 0.1 collective-permute-start
  23.0 1.3 %collective-permute-start.1 = (f32[8,128]{1,0:T(8,128)S(1)}, f32[8,128]{1,0:T(8,128)S(1)}, u32[]{:S(2)}, u32[]{:S(2)}) collective-permute-start(f32[8,128]{1,0:T(8,128)S(1)} %get-tuple-element.28.i0), channel_id=1, source_target_pairs={{0,3},{1,2},{2,1},{3,0},{4,7},{5,6},{6,5},{7,4},{8,11},{9,10},{10,... | collective-permute-start | bytes 12296 | tf_op jit(solution)/shard_map/ppermute | solution.py:259
  24.4 3.0 %collective-permute-done.7.ends = bf16[64,3200]{1,0:T(8,128)(2,1)S(1)} collective-permute-done((bf16[64,3200]{1,0:T(8,128)(2,1)}, bf16[64,3200]{1,0:T(8,128)(2,1)S(1)}, u32[]{:S(2)}, u32[]{:S(2)}) %collective-permute-start.7) | collective-permute-done | bytes 409632 | tf_op jit(solution)/shard_map/ppermute | solution.py:255
  27.4 0.0 collective-permute-start.2
  27.4 0.0 copy-done.6
  27.4 0.0 copy-done.1
  27.4 3.3 %early.1 = bf16[192,2048]{1,0:T(8,128)(2,1)S(1)} custom-call(bf16[64,3200]{1,0:T(8,128)(2,1)S(1)} %get-tuple-element.29.own, bf16[64,3200]{1,0:T(8,128)(2,1)S(1)} %collective-permute-done.4.outer, bf16[64,3200]{1,0:T(8,128)(2,1)S(1)} %collective-permute-done.3.inner, bf16[64,3200]{1,0:T(8,128)(2,1)S(1)} %collective-permute-done.7.ends, f32[3200]{0:T(1024)S(1)} %copy-done.5, ...), custom_call_target="tpu_custom_call" | custom-call | tf_op jit(solution)/shard_map/early/pallas_call | solution.py:326
  30.6 0.0 copy-start.3
  30.6 0.0 copy-start.7
  30.7 1.9 %collective-permute-done.6.last = bf16[64,2432]{1,0:T(8,128)(2,1)S(1)} collective-permute-done((bf16[64,2432]{1,0:T(8,128)(2,1)S(1)}, bf16[64,2432]{1,0:T(8,128)(2,1)S(1)}, u32[]{:S(2)}, u32[]{:S(2)}) %collective-permute-start.6) | collective-permute-done | bytes 311328 | tf_op jit(solution)/shard_map/ppermute | solution.py:267
  32.6 1.8 %late.1.total = f32[64,2048]{1,0:T(8,128)S(1)} custom-call(bf16[64,2432]{1,0:T(8,128)(2,1)S(1)} %collective-permute-done.6.last, bf16[3200,2048]{1,0:T(8,128)(2,1)S(1)} %copy-done.1, f32[1,2048]{1,0:T(1,128)S(1)} %bitcast.8), custom_call_target="tpu_custom_call" | custom-call | tf_op jit(solution)/shard_map/late/pallas_call | solution.py:337
  34.4 0.5 collective-permute-done.i3
  34.9 0.0 collective-permute-done.1.i2
  34.9 0.0 collective-permute-done.2.i1
  34.9 0.0 collective-permute-done.5.last
  34.9 1.2 %project.1 = (bf16[64,2048]{1,0:T(8,128)(2,1)S(1)}, bf16[64,2048]{1,0:T(8,128)(2,1)S(1)}, bf16[64,2048]{1,0:T(8,128)(2,1)S(1)}, bf16[64,2048]{1,0:T(8,128)(2,1)S...) custom-call(f32[8,128]{1,0:T(8,128)S(1)} %collective-permute-done.i3, f32[8,128]{1,0:T(8,128)S(1)} %collective-permute-done.1.i2, ...), custom_call_target="tpu_custom_call" | custom-call | flops 2516582400 | bytes 13107200 | tf_op jit(solution)/shard_map/project/pallas_call | solution.py:346
  36.1 2.5 %collective-permute-start.10 = (bf16[64,2048]{1,0:T(8,128)(2,1)S(1)}, bf16[64,2048]{1,0:T(8,128)(2,1)S(1)}, u32[]{:S(2)}, u32[]{:S(2)}) collective-permute-start(bf16[64,2048]{1,0:T(8,128)(2,1)S(1)} %get-tuple-element.41), channel_id=1, source_target_pairs={{0,24},{4,28},{8,16},{12,20},{16,8},{20,12},{24,0},{28,4},{1,25},{... | collective-permute-start | bytes 786440 | tf_op jit(solution)/shard_map/ppermute | solution.py:271
  38.6 0.5 collective-permute-start.8
  39.1 0.5 collective-permute-start.9
  39.6 11.7 %all_to_all.12 = f32[32,1,128]{2,1,0:T(1,128)S(1)} all-to-all(f32[32,1,128]{2,1,0:T(1,128)S(1)} %bitcast.11), channel_id=1, replica_groups=mesh['grp'=8,'dp'=4] {'grp','dp'}, dimensions={0} | all-to-all | bytes 32768 | tf_op jit(solution)/shard_map/all_to_all | solution.py:361
  51.4 0.0 collective-permute-done.10.rest_3_.refs_3_
  51.4 0.0 collective-permute-done.8.rest_1_.refs_1_
  51.4 0.0 collective-permute-done.9.rest_2_.refs_2_
  51.4 0.1 collective-permute-start.11
  51.5 0.0 copy-done.3
  51.5 0.0 copy-done.7
  51.5 1.9 %base.1 = (bf16[256,2048]{1,0:T(8,128)(2,1)}, f32[128,128]{1,0:T(8,128)S(1)}) custom-call(f32[32,128]{1,0:T(8,128)S(1)} %bitcast.6, f32[8,128]{1,0:T(8,128)S(1)} %get-tuple-element.44.text_scale, f32[1,2048]{1,0:T(1,128)S(1)} %bitcast.9, bf16[256,2048]{1,0:T(8,128)(2,1)S(1)} %copy-done.3, bf16[64,2048]{1,0:T(8,128)(2,1)S(1)} %get-tuple-element.45.rest_0_.refs_0_, ...), custom_call_target="tpu_custom_call" | custom-call | bytes 13107200 | tf_op jit(solution)/shard_map/base/pallas_call | solution.py:370
  53.4 0.0 collective-permute-done.11.odd
  53.4 0.9 %place.1 = bf16[256,2048]{1,0:T(8,128)(2,1)} custom-call(f32[128,128]{1,0:T(8,128)S(1)} %get-tuple-element.49.scales, f32[1,2048]{1,0:T(1,128)S(1)} %bitcast.10, bf16[128,2048]{1,0:T(8,128)(2,1)S(1)} %collective-permute-done.11.odd, bf16[256,2048]{1,0:T(8,128)(2,1)} %get-tuple-element.50.base), custom_call_target="tpu_custom_call", output_to_operand_aliasing={{}: (3, {})} | custom-call | tf_op jit(solution)/shard_map/place/pallas_call | solution.py:380
  (2 shorter events, 0.0 us)
Async XLA Ops:
  0.0 19.6 %collective-permute-start.3 = (bf16[64,3200]{1,0:T(8,128)(2,1)}, bf16[64,3200]{1,0:T(8,128)(2,1)S(1)}, u32[]{:S(2)}, u32[]{:S(2)}) collective-permute-start(bf16[64,3200]{1,0:T(8,128)(2,1)} %vis.1), channel_id=1, source_target_pairs={{1,2},{2,1},{0,0},{3,3},{5,6},{6,5},{4,4},{7,7},{9,10},{10,9},{8,8... | collective-permute-start | bytes 1228808 | tf_op jit(solution)/shard_map/ppermute | solution.py:251
  1.6 18.2 %collective-permute-start.4 = (bf16[64,3200]{1,0:T(8,128)(2,1)}, bf16[64,3200]{1,0:T(8,128)(2,1)S(1)}, u32[]{:S(2)}, u32[]{:S(2)}) collective-permute-start(bf16[64,3200]{1,0:T(8,128)(2,1)} %vis.1), channel_id=1, source_target_pairs={{0,1},{1,0},{2,3},{3,2},{4,5},{5,4},{6,7},{7,6},{8,9},{9,8},{10,11... | collective-permute-start | bytes 1228808 | tf_op jit(solution)/shard_map/ppermute | solution.py:247
  6.6 20.8 %collective-permute-start.7 = (bf16[64,3200]{1,0:T(8,128)(2,1)}, bf16[64,3200]{1,0:T(8,128)(2,1)S(1)}, u32[]{:S(2)}, u32[]{:S(2)}) collective-permute-start(bf16[64,3200]{1,0:T(8,128)(2,1)} %vis.1), channel_id=1, source_target_pairs={{0,3},{3,0},{1,1},{2,2},{4,7},{7,4},{5,5},{6,6},{8,11},{11,8},{9,9... | collective-permute-start | bytes 1228808 | tf_op jit(solution)/shard_map/ppermute | solution.py:255
  10.5 1.2 %copy-start.2 = (bf16[256,2048]{1,0:T(8,128)(2,1)S(1)}, bf16[256,2048]{1,0:T(8,128)(2,1)}, u32[]{:S(2)}) copy-start(bf16[256,2048]{1,0:T(8,128)(2,1)} %text.3) | copy-start | bytes 3145732
  11.7 1.0 %copy-start.4 = (bf16[64,3200]{1,0:T(8,128)(2,1)S(1)}, bf16[64,3200]{1,0:T(8,128)(2,1)}, u32[]{:S(2)}) copy-start(bf16[64,3200]{1,0:T(8,128)(2,1)} %vis.1) | copy-start | bytes 1228804
  12.7 0.7 %copy-start.8 = (s32[4]{0:T(128)S(1)}, s32[4]{0:T(128)}, u32[]{:S(2)}) copy-start(s32[4]{0:T(128)} %owners.1) | copy-start | bytes 52
  13.4 0.7 %copy-start.9 = (s32[4]{0:T(128)S(1)}, s32[4]{0:T(128)}, u32[]{:S(2)}) copy-start(s32[4]{0:T(128)} %offsets.1) | copy-start | bytes 52
  14.0 5.6 %copy-start.5 = (f32[3200]{0:T(1024)S(1)}, f32[3200]{0:T(1024)}, u32[]{:S(2)}) copy-start(f32[3200]{0:T(1024)} %gain.3) | copy-start | bytes 38404
  14.0 13.4 %copy-start.6 = (f32[2048]{0:T(1024)S(1)}, f32[2048]{0:T(1024)}, u32[]{:S(2)}) copy-start(f32[2048]{0:T(1024)} %param.12) | copy-start | bytes 24580
  14.9 4.7 %copy-start = (bf16[3200,2048]{1,0:T(8,128)(2,1)S(1)}, bf16[3200,2048]{1,0:T(8,128)(2,1)}, u32[]{:S(2)}) copy-start(bf16[3200,2048]{1,0:T(8,128)(2,1)} %weight.7) | copy-start | bytes 39321604
  19.6 7.7 %copy-start.1 = (bf16[3200,2048]{1,0:T(8,128)(2,1)S(1)}, bf16[3200,2048]{1,0:T(8,128)(2,1)}, u32[]{:S(2)}) copy-start(bf16[3200,2048]{1,0:T(8,128)(2,1)} %weight.7) | copy-start | bytes 39321604
  19.9 12.7 %collective-permute-start.6 = (bf16[64,2432]{1,0:T(8,128)(2,1)S(1)}, bf16[64,2432]{1,0:T(8,128)(2,1)S(1)}, u32[]{:S(2)}, u32[]{:S(2)}) collective-permute-start(bf16[64,2432]{1,0:T(8,128)(2,1)S(1)} %get-tuple-element.35), channel_id=1, source_target_pairs={{0,2},{1,0},{2,3},{3,1},{4,6},{5,4},{6,7},{7,5},{8,10},{9,8},{10,1... | collective-permute-start | bytes 933896 | tf_op jit(solution)/shard_map/ppermute | solution.py:267
  19.9 15.0 %collective-permute-start.5 = (bf16[64,768]{1,0:T(8,128)(2,1)S(1)}, bf16[64,768]{1,0:T(8,128)(2,1)S(1)}, u32[]{:S(2)}, u32[]{:S(2)}) collective-permute-start(bf16[64,768]{1,0:T(8,128)(2,1)S(1)} %get-tuple-element.34), channel_id=1, source_target_pairs={{0,2},{1,0},{2,3},{3,1},{4,6},{5,4},{6,7},{7,5},{8,10},{9,8},{10,1... | collective-permute-start | bytes 294920 | tf_op jit(solution)/shard_map/ppermute | solution.py:267
  23.0 11.9 %collective-permute-start = (f32[8,128]{1,0:T(8,128)S(1)}, f32[8,128]{1,0:T(8,128)S(1)}, u32[]{:S(2)}, u32[]{:S(2)}) collective-permute-start(f32[8,128]{1,0:T(8,128)S(1)} %get-tuple-element.28.i0), channel_id=1, source_target_pairs={{0,2},{1,3},{2,0},{3,1},{4,6},{5,7},{6,4},{7,5},{8,10},{9,11},{10,... | collective-permute-start | bytes 12296 | tf_op jit(solution)/shard_map/ppermute | solution.py:263
  23.0 11.9 %collective-permute-start.1 = (f32[8,128]{1,0:T(8,128)S(1)}, f32[8,128]{1,0:T(8,128)S(1)}, u32[]{:S(2)}, u32[]{:S(2)}) collective-permute-start(f32[8,128]{1,0:T(8,128)S(1)} %get-tuple-element.28.i0), channel_id=1, source_target_pairs={{0,3},{1,2},{2,1},{3,0},{4,7},{5,6},{6,5},{7,4},{8,11},{9,10},{10,... | collective-permute-start | bytes 12296 | tf_op jit(solution)/shard_map/ppermute | solution.py:259
  27.4 7.5 %collective-permute-start.2 = (f32[8,128]{1,0:T(8,128)S(1)}, f32[8,128]{1,0:T(8,128)S(1)}, u32[]{:S(2)}, u32[]{:S(2)}) collective-permute-start(f32[8,128]{1,0:T(8,128)S(1)} %get-tuple-element.28.i0), channel_id=1, source_target_pairs={{0,1},{1,0},{2,3},{3,2},{4,5},{5,4},{6,7},{7,6},{8,9},{9,8},{10,11... | collective-permute-start | bytes 12296 | tf_op jit(solution)/shard_map/ppermute | solution.py:247
  30.6 20.9 %copy-start.3 = (bf16[256,2048]{1,0:T(8,128)(2,1)S(1)}, bf16[256,2048]{1,0:T(8,128)(2,1)}, u32[]{:S(2)}) copy-start(bf16[256,2048]{1,0:T(8,128)(2,1)} %text.3) | copy-start | bytes 3145732
  30.6 20.9 %copy-start.7 = (f32[2048]{0:T(1024)S(1)}, f32[2048]{0:T(1024)}, u32[]{:S(2)}) copy-start(f32[2048]{0:T(1024)} %param.14) | copy-start | bytes 24580
  36.1 15.3 %collective-permute-start.10 = (bf16[64,2048]{1,0:T(8,128)(2,1)S(1)}, bf16[64,2048]{1,0:T(8,128)(2,1)S(1)}, u32[]{:S(2)}, u32[]{:S(2)}) collective-permute-start(bf16[64,2048]{1,0:T(8,128)(2,1)S(1)} %get-tuple-element.41), channel_id=1, source_target_pairs={{0,24},{4,28},{8,16},{12,20},{16,8},{20,12},{24,0},{28,4},{1,25},{... | collective-permute-start | bytes 786440 | tf_op jit(solution)/shard_map/ppermute | solution.py:271
  38.6 12.8 %collective-permute-start.8 = (bf16[64,2048]{1,0:T(8,128)(2,1)S(1)}, bf16[64,2048]{1,0:T(8,128)(2,1)S(1)}, u32[]{:S(2)}, u32[]{:S(2)}) collective-permute-start(bf16[64,2048]{1,0:T(8,128)(2,1)S(1)} %get-tuple-element.39), channel_id=1, source_target_pairs={{0,8},{4,12},{8,0},{12,4},{16,24},{20,28},{24,16},{28,20},{1,9},{5... | collective-permute-start | bytes 786440 | tf_op jit(solution)/shard_map/ppermute | solution.py:271
  39.1 12.2 %collective-permute-start.9 = (bf16[64,2048]{1,0:T(8,128)(2,1)S(1)}, bf16[64,2048]{1,0:T(8,128)(2,1)S(1)}, u32[]{:S(2)}, u32[]{:S(2)}) collective-permute-start(bf16[64,2048]{1,0:T(8,128)(2,1)S(1)} %get-tuple-element.40), channel_id=1, source_target_pairs={{0,16},{4,20},{8,24},{12,28},{16,0},{20,4},{24,8},{28,12},{1,17},{... | collective-permute-start | bytes 786440 | tf_op jit(solution)/shard_map/ppermute | solution.py:271
  51.4 2.0 %collective-permute-start.11 = (bf16[128,2048]{1,0:T(8,128)(2,1)S(1)}, bf16[128,2048]{1,0:T(8,128)(2,1)S(1)}, u32[]{:S(2)}, u32[]{:S(2)}) collective-permute-start(bf16[128,2048]{1,0:T(8,128)(2,1)S(1)} %pack.1), channel_id=1, source_target_pairs={{0,4},{4,0},{8,12},{12,8},{16,20},{20,16},{24,28},{28,24},{1,5},{5... | collective-permute-start | bytes 1572872 | tf_op jit(solution)/shard_map/ppermute | solution.py:271
